TPU v7x, 32 devices: a whole 2x2x4 slice. The times are simulated.
32 devices in a mesh: batch: 4 (over y, x), seq: 8 (over z, core).
Axes of the slice: x: 2, y: 2, z: 4, core: 2. Of those that a mesh axis runs over, the one named last changes fastest.
Arguments:
- incoming_activations: bfloat16 [8, 2048, 1024], P('batch', 'seq'), may hold values from -6 to 6
- sequence_extents: int32 [8, 8], P('batch'), may hold values from 0 to 2048, as said below
- upstream_sensitivity: bfloat16 [8, 2048, 1024], P('batch', 'seq'), may hold values from -6 to 6
- initial_normalizer_scale: bfloat16 [1024], P(('batch', 'seq')), may hold values from 0.5 to 1.5
- initial_normalizer_offset: bfloat16 [1024], P(('batch', 'seq')), may hold values from -2.5 to 2.5
- temporal_lookup_fraction: bfloat16 [1024], P(('batch', 'seq')), may hold values from 0.099609375 to 0.8984375
- temporal_content_fraction: bfloat16 [1024], P(('batch', 'seq')), may hold values from 0.099609375 to 0.8984375
- temporal_receptance_fraction: bfloat16 [1024], P(('batch', 'seq')), may hold values from 0.099609375 to 0.8984375
- feature_forgetting_rate: bfloat16 [1024], P(('batch', 'seq')), may hold values from 9.536743e-06 to 0.049804688
- present_reward: bfloat16 [1024], P(('batch', 'seq')), may hold values from 0 to 3
- temporal_lookup_projection: bfloat16 [1024, 1024], P(('batch', 'seq')), may hold values from -0.1875 to 0.1875
- temporal_content_projection: bfloat16 [1024, 1024], P(('batch', 'seq')), may hold values from -0.1875 to 0.1875
- temporal_receptance_projection: bfloat16 [1024, 1024], P(('batch', 'seq')), may hold values from -0.1875 to 0.1875
- temporal_result_projection: bfloat16 [1024, 1024], P(('batch', 'seq')), may hold values from -0.75 to 0.75
- later_normalizer_scale: bfloat16 [1024], P(('batch', 'seq')), may hold values from 0.5 to 1.5
- later_normalizer_offset: bfloat16 [1024], P(('batch', 'seq')), may hold values from -2.5 to 2.5
- feature_lookup_fraction: bfloat16 [1024], P(('batch', 'seq')), may hold values from 0.099609375 to 0.8984375
- feature_receptance_fraction: bfloat16 [1024], P(('batch', 'seq')), may hold values from 0.099609375 to 0.8984375
- feature_lookup_projection: bfloat16 [1024, 4096], P(('batch', 'seq')), may hold values from -0.1875 to 0.1875
- feature_content_projection: bfloat16 [4096, 1024], P(('batch', 'seq')), may hold values from -0.09375 to 0.09375
- feature_receptance_projection: bfloat16 [1024, 1024], P(('batch', 'seq')), may hold values from -0.1875 to 0.1875
Outputs:
- output: bfloat16 [8, 2048, 1024], P('batch', 'seq')
- input_grad: float32 [8, 2048, 1024], P('batch', 'seq')
- grad_norm1_gain: float32 [1024], P(('batch', 'seq'))
- grad_norm1_bias: float32 [1024], P(('batch', 'seq'))
- grad_mix_key: float32 [1024], P(('batch', 'seq'))
- grad_mix_value: float32 [1024], P(('batch', 'seq'))
- grad_mix_gate: float32 [1024], P(('batch', 'seq'))
- grad_decay_rate: float32 [1024], P(('batch', 'seq'))
- grad_time_bonus: float32 [1024], P(('batch', 'seq'))
- grad_key_weight: float32 [1024, 1024], P(('batch', 'seq'))
- grad_value_weight: float32 [1024, 1024], P(('batch', 'seq'))
- grad_gate_weight: float32 [1024, 1024], P(('batch', 'seq'))
- grad_output_weight: float32 [1024, 1024], P(('batch', 'seq'))
- grad_norm2_gain: float32 [1024], P(('batch', 'seq'))
- grad_norm2_bias: float32 [1024], P(('batch', 'seq'))
- grad_ffn_mix_key: float32 [1024], P(('batch', 'seq'))
- grad_ffn_mix_gate: float32 [1024], P(('batch', 'seq'))
- grad_ffn_key_weight: float32 [1024, 4096], P(('batch', 'seq'))
- grad_ffn_value_weight: float32 [4096, 1024], P(('batch', 'seq'))
- grad_ffn_gate_weight: float32 [1024, 1024], P(('batch', 'seq'))
Inputs may be any that keep to these rules, and one draw needn't show every extreme that they name: `sequence_extents`: each row lists in order the lengths of the documents that fill its 2048 positions end to end, then zeros; the lengths sum to 2048. In each group of 2 rows of one index of batch one row holds a single document of 2048 positions; in the others every document has 256, 1024 or 2048 positions except the last, which may be shorter.
All inputs are finite; a program needn't handle non-finite values.
Results may differ from a plain program's by a relative error of at most 0.0085.
Values may be sent and summed in bfloat16 or wider, within the bound.
No kernel may reach another device: no remote copies, remote signals or barrier semaphores. Data moves between devices by JAX's collectives and lax.ppermute only.
A program may use at most 256 MiB of HBM per device.

v0:
```python
from functools import partial

import jax
import jax.numpy as jnp
from jax import lax
from jax.sharding import PartitionSpec as P

eps = 1e-05
highest = lax.Precision.HIGHEST


def shifted(shard, axis, by):
    length = lax.axis_size(axis)
    pairs = [(i, i + by) for i in range(length) if 0 <= i + by < length]
    return lax.ppermute(shard, axis, pairs)


def carried_in(part, axis, combine, identity, reverse):
    count = lax.axis_size(axis)
    place = lax.axis_index(axis)
    ahead = count - 1 - place if reverse else place
    gathered = jax.tree.map(lambda a: lax.all_gather(a, axis), part)
    state = jax.tree.map(lambda a, e: jnp.zeros_like(a) + jnp.asarray(e, a.dtype), part, identity)

    def one(lap, state):
        source = count - 1 - lap if reverse else lap
        return combine(
            state, jax.tree.map(lambda a: lax.dynamic_index_in_dim(a, source, 0, False), gathered)
        )

    return lax.fori_loop(0, ahead, one, state)


def norm_forward(values, gain_vec, bias_vec):
    centre = values - jnp.mean(values, axis=-1, keepdims=True)
    inv_std = lax.rsqrt(jnp.mean(centre * centre, axis=-1, keepdims=True) + eps)
    normed = centre * inv_std
    return (normed * gain_vec + bias_vec, normed, inv_std)


def norm_backward(grads, normed, inv_std, gain_vec):
    scaled = grads * gain_vec
    inner = (
        scaled
        - jnp.mean(scaled, axis=-1, keepdims=True)
        - normed * jnp.mean(scaled * normed, axis=-1, keepdims=True)
    )
    return (inv_std * inner, jnp.sum(grads * normed, axis=(0, 1)), jnp.sum(grads, axis=(0, 1)))


def project(rows_in, weight):
    return jnp.einsum("rtd,de->rte", rows_in, weight, preferred_element_type=jnp.float32)


def project_back(grads, weight):
    return jnp.einsum("rte,de->rtd", grads, weight, preferred_element_type=jnp.float32)


def weight_grad(rows_in, grads):
    return jnp.einsum("rtd,rte->de", rows_in, grads, preferred_element_type=jnp.float32)


def reduce_channel(gain_two, bias_two, ffn_mix_key, ffn_mix_gate, ffn_key_weight, ffn_value_weight):
    first_parts = (
        lax.psum_scatter(gain_two, ("batch", "seq"), scatter_dimension=0, tiled=True),
        lax.psum_scatter(bias_two, ("batch", "seq"), scatter_dimension=0, tiled=True),
        lax.psum_scatter(ffn_mix_key, ("batch", "seq"), scatter_dimension=0, tiled=True),
        lax.psum_scatter(ffn_mix_gate, ("batch", "seq"), scatter_dimension=0, tiled=True),
        lax.psum_scatter(ffn_key_weight, ("batch", "seq"), scatter_dimension=0, tiled=True),
    )
    second_part = lax.psum_scatter(
        ffn_value_weight, ("batch", "seq"), scatter_dimension=0, tiled=True
    )
    return tuple(first_parts) + (second_part,)


def weighted_value_local(
    key_row_block,
    value_row_block,
    feature_forgetting_rate,
    present_reward,
    state_numerator,
    state_denominator,
    document_segments,
):
    length = key_row_block.shape[1]
    width = key_row_block.shape[2]
    order_idx = jnp.arange(length)
    step_pos = order_idx.astype(jnp.float32)[:, None]
    powered_lookups = jnp.exp(key_row_block)
    grow_exp = jnp.exp(step_pos * feature_forgetting_rate)
    shrink = jnp.exp((1.0 - step_pos) * feature_forgetting_rate)
    pair_mask = (
        (order_idx[None, :] < order_idx[:, None])[None]
        & (document_segments[:, None, :] == document_segments[:, :, None])
    ).astype(jnp.float32)
    weighted = jnp.concatenate(
        [powered_lookups * value_row_block, powered_lookups], axis=2
    ) * jnp.concatenate([grow_exp, grow_exp], axis=1)
    past_sums = jnp.einsum(
        "rti,rie->rte", pair_mask, weighted, precision=highest
    ) * jnp.concatenate([shrink, shrink], axis=1)
    carry_fade = (document_segments == 0).astype(jnp.float32)[:, :, None] * jnp.exp(
        -step_pos * feature_forgetting_rate
    )
    present_token_contribution = jnp.exp(present_reward) * powered_lookups
    numer = (
        carry_fade * state_numerator[:, None, :]
        + past_sums[:, :, :width]
        + present_token_contribution * value_row_block
    )
    denom = (
        carry_fade * state_denominator[:, None, :]
        + past_sums[:, :, width:]
        + present_token_contribution
    )
    return numer / denom


def tail_terms(key_row_block, value_row_block, feature_forgetting_rate, document_segments):
    length = key_row_block.shape[1]
    step_pos = jnp.arange(length).astype(jnp.float32)[:, None]
    powered_lookups = jnp.exp(key_row_block)
    tail_fade = (document_segments == document_segments[:, -1:]).astype(jnp.float32)[
        :, :, None
    ] * jnp.exp((step_pos - (length - 1)) * feature_forgetting_rate)
    return (
        jnp.sum(tail_fade * powered_lookups * value_row_block, axis=1),
        jnp.sum(tail_fade * powered_lookups, axis=1),
        tail_fade,
        powered_lookups,
    )


def shards(
    incoming_activations,
    sequence_extents,
    upstream_sensitivity,
    initial_normalizer_scale,
    initial_normalizer_offset,
    temporal_lookup_fraction,
    temporal_content_fraction,
    temporal_receptance_fraction,
    feature_forgetting_rate,
    present_reward,
    temporal_lookup_projection,
    temporal_content_projection,
    temporal_receptance_projection,
    temporal_result_projection,
    later_normalizer_scale,
    later_normalizer_offset,
    feature_lookup_fraction,
    feature_receptance_fraction,
    feature_lookup_projection,
    feature_content_projection,
    feature_receptance_projection,
):
    gathered_sequences = (
        lax.all_gather(initial_normalizer_scale, ("batch", "seq"), axis=0, tiled=True),
        lax.all_gather(initial_normalizer_offset, ("batch", "seq"), axis=0, tiled=True),
        lax.all_gather(temporal_lookup_fraction, ("batch", "seq"), axis=0, tiled=True),
        lax.all_gather(temporal_content_fraction, ("batch", "seq"), axis=0, tiled=True),
        lax.all_gather(temporal_receptance_fraction, ("batch", "seq"), axis=0, tiled=True),
        lax.all_gather(feature_forgetting_rate, ("batch", "seq"), axis=0, tiled=True),
        lax.all_gather(present_reward, ("batch", "seq"), axis=0, tiled=True),
        lax.all_gather(temporal_lookup_projection, ("batch", "seq"), axis=0, tiled=True),
        lax.all_gather(temporal_content_projection, ("batch", "seq"), axis=0, tiled=True),
        lax.all_gather(temporal_receptance_projection, ("batch", "seq"), axis=0, tiled=True),
        lax.all_gather(temporal_result_projection, ("batch", "seq"), axis=0, tiled=True),
        lax.all_gather(later_normalizer_scale, ("batch", "seq"), axis=0, tiled=True),
        lax.all_gather(later_normalizer_offset, ("batch", "seq"), axis=0, tiled=True),
        lax.all_gather(feature_lookup_fraction, ("batch", "seq"), axis=0, tiled=True),
        lax.all_gather(feature_receptance_fraction, ("batch", "seq"), axis=0, tiled=True),
        lax.all_gather(feature_lookup_projection, ("batch", "seq"), axis=0, tiled=True),
        lax.all_gather(feature_content_projection, ("batch", "seq"), axis=0, tiled=True),
        lax.all_gather(feature_receptance_projection, ("batch", "seq"), axis=0, tiled=True),
    )
    opening_standardize_scale = gathered_sequences[0].astype(jnp.float32)
    opening_standardize_offset = gathered_sequences[1].astype(jnp.float32)
    temporal_lookup_mixture = gathered_sequences[2].astype(jnp.float32)
    temporal_content_mixture = gathered_sequences[3].astype(jnp.float32)
    temporal_receptance_mixture = gathered_sequences[4].astype(jnp.float32)
    decay_vec = gathered_sequences[5].astype(jnp.float32)
    reward_array = gathered_sequences[6].astype(jnp.float32)
    closing_standardize_scale = gathered_sequences[11].astype(jnp.float32)
    closing_standardize_offset = gathered_sequences[12].astype(jnp.float32)
    feature_lookup_mixture = gathered_sequences[13].astype(jnp.float32)
    feature_receptance_mixture = gathered_sequences[14].astype(jnp.float32)
    rows, length, width = incoming_activations.shape
    starts = jnp.cumsum(sequence_extents, axis=1) - sequence_extents
    places = lax.axis_index("seq") * length + jnp.arange(length, dtype=jnp.int32)
    resets = jnp.any(
        (starts[:, None, :] == places[None, :, None]) & (sequence_extents[:, None, :] > 0), axis=2
    )
    document_segments = jnp.cumsum(resets.astype(jnp.int32), axis=1)
    keep_mask = 1.0 - resets.astype(jnp.float32)[:, :, None]
    clear_flag = (document_segments[:, -1:] == 0).astype(jnp.float32)
    token_count = jnp.full((rows, 1), length, jnp.float32)
    zero_state = jnp.zeros((rows, width), jnp.float32)
    identity = (
        zero_state,
        zero_state,
        jnp.ones((rows, 1), jnp.float32),
        jnp.zeros((rows, 1), jnp.float32),
    )

    def combine(earlier, later):
        fade = later[2] * jnp.exp(-later[3] * decay_vec)
        return (
            fade * earlier[0] + later[0],
            fade * earlier[1] + later[1],
            earlier[2] * later[2],
            earlier[3] + later[3],
        )

    inputs = incoming_activations.astype(jnp.float32)
    left_rows = shifted(incoming_activations[:, length - 1 :, :], "seq", 1)
    normed_one, unit_one, inv_one = norm_forward(
        inputs, opening_standardize_scale, opening_standardize_offset
    )
    left_normed, _, _ = norm_forward(
        left_rows.astype(jnp.float32), opening_standardize_scale, opening_standardize_offset
    )
    before_one = jnp.concatenate([left_normed, normed_one[:, :-1, :]], axis=1) * keep_mask
    key_in = (
        normed_one * temporal_lookup_mixture + before_one * (1.0 - temporal_lookup_mixture)
    ).astype(jnp.bfloat16)
    value_in = (
        normed_one * temporal_content_mixture + before_one * (1.0 - temporal_content_mixture)
    ).astype(jnp.bfloat16)
    gate_in = (
        normed_one * temporal_receptance_mixture + before_one * (1.0 - temporal_receptance_mixture)
    ).astype(jnp.bfloat16)
    key_row_block = project(key_in, gathered_sequences[7])
    value_row_block = project(value_in, gathered_sequences[8])
    gates = jax.nn.sigmoid(project(gate_in, gathered_sequences[9]))
    tail_num, tail_den, tail_fade, powered_lookups = tail_terms(
        key_row_block, value_row_block, decay_vec, document_segments
    )
    state_numerator, state_denominator, _, _ = carried_in(
        (tail_num, tail_den, clear_flag, token_count), "seq", combine, identity, False
    )
    mixed, weighted_value_backward = jax.vjp(
        partial(weighted_value_local, document_segments=document_segments),
        key_row_block,
        value_row_block,
        decay_vec,
        reward_array,
        state_numerator,
        state_denominator,
    )
    gated = (gates * mixed).astype(jnp.bfloat16)
    middle = inputs + project(gated, gathered_sequences[10])
    normed_two, unit_two, inv_two = norm_forward(
        middle, closing_standardize_scale, closing_standardize_offset
    )
    before_rows = shifted(normed_two[:, length - 1 :, :], "seq", 1)
    before_two = jnp.concatenate([before_rows, normed_two[:, :-1, :]], axis=1) * keep_mask
    ffn_key_in = (
        normed_two * feature_lookup_mixture + before_two * (1.0 - feature_lookup_mixture)
    ).astype(jnp.bfloat16)
    ffn_gate_in = (
        normed_two * feature_receptance_mixture + before_two * (1.0 - feature_receptance_mixture)
    ).astype(jnp.bfloat16)
    hidden_pre = project(ffn_key_in, gathered_sequences[15])
    hidden = jnp.square(jax.nn.relu(hidden_pre)).astype(jnp.bfloat16)
    ffn_value = project(hidden, gathered_sequences[16])
    ffn_gates = jax.nn.sigmoid(project(ffn_gate_in, gathered_sequences[17]))
    output = (middle + ffn_gates * ffn_value).astype(jnp.bfloat16)
    matrices = (
        gathered_sequences[7],
        gathered_sequences[8],
        gathered_sequences[9],
        gathered_sequences[10],
        gathered_sequences[15],
        gathered_sequences[16],
        gathered_sequences[17],
    )
    grad_out = upstream_sensitivity.astype(jnp.float32)
    value_grad = (grad_out * ffn_gates).astype(jnp.bfloat16)
    ffn_gate_grad = (grad_out * ffn_value * ffn_gates * (1.0 - ffn_gates)).astype(jnp.bfloat16)
    hidden_grad = project_back(value_grad, matrices[5])
    grad_ffn_value = weight_grad(hidden, value_grad)
    pre_grad = (hidden_grad * 2.0 * jax.nn.relu(hidden_pre)).astype(jnp.bfloat16)
    grad_ffn_key = weight_grad(ffn_key_in, pre_grad)
    grad_ffn_gate = weight_grad(ffn_gate_in, ffn_gate_grad)
    key_two_grad = project_back(pre_grad, matrices[4])
    gate_two_grad = project_back(ffn_gate_grad, matrices[6])
    spread_two = normed_two - before_two
    grad_ffn_mix_key = jnp.sum(key_two_grad * spread_two, axis=(0, 1))
    grad_ffn_mix_gate = jnp.sum(gate_two_grad * spread_two, axis=(0, 1))
    normed_two_grad = (
        key_two_grad * feature_lookup_mixture + gate_two_grad * feature_receptance_mixture
    )
    before_two_grad = (
        key_two_grad * (1.0 - feature_lookup_mixture)
        + gate_two_grad * (1.0 - feature_receptance_mixture)
    ) * keep_mask
    from_right = shifted(before_two_grad[:, :1, :], "seq", -1)
    normed_two_grad = normed_two_grad + jnp.concatenate(
        [before_two_grad[:, 1:, :], from_right], axis=1
    )
    middle_norm_grad, grad_gain_two, grad_bias_two = norm_backward(
        normed_two_grad, unit_two, inv_two, closing_standardize_scale
    )
    middle_grad = grad_out + middle_norm_grad
    channel_parts = None
    branch_grad = middle_grad.astype(jnp.bfloat16)
    grad_output = weight_grad(gated, branch_grad)
    gated_grad = project_back(branch_grad, matrices[3])
    gate_pre_grad = (gated_grad * mixed * gates * (1.0 - gates)).astype(jnp.bfloat16)
    blended_gradient = gated_grad * gates
    (
        key_gradient,
        value_gradient,
        decay_gradient,
        reward_derivative,
        numerator_gradient,
        denominator_gradient,
    ) = weighted_value_backward(blended_gradient)
    num_next, den_next, _, _ = carried_in(
        (numerator_gradient, denominator_gradient, clear_flag, token_count),
        "seq",
        combine,
        identity,
        True,
    )
    num_tail = tail_fade * num_next[:, None, :]
    den_tail = tail_fade * den_next[:, None, :]
    tail_grad = powered_lookups * (value_row_block * num_tail + den_tail)
    key_gradient = key_gradient + tail_grad
    value_gradient = value_gradient + powered_lookups * num_tail
    offsets = (jnp.arange(length).astype(jnp.float32) - (length - 1))[:, None]
    block_fade = clear_flag * jnp.exp(-length * decay_vec)
    decay_gradient = decay_gradient + jnp.sum(offsets * tail_grad, axis=(0, 1))
    decay_gradient = decay_gradient - length * jnp.sum(
        block_fade * (state_numerator * num_next + state_denominator * den_next), axis=0
    )
    key_grad16 = key_gradient.astype(jnp.bfloat16)
    val_grad16 = value_gradient.astype(jnp.bfloat16)
    grad_key = weight_grad(key_in, key_grad16)
    grad_value = weight_grad(value_in, val_grad16)
    grad_gate = weight_grad(gate_in, gate_pre_grad)
    key_in_grad = project_back(key_grad16, matrices[0])
    value_in_grad = project_back(val_grad16, matrices[1])
    gate_in_grad = project_back(gate_pre_grad, matrices[2])
    spread_one = normed_one - before_one
    grad_mix_key = jnp.sum(key_in_grad * spread_one, axis=(0, 1))
    grad_mix_value = jnp.sum(value_in_grad * spread_one, axis=(0, 1))
    grad_mix_gate = jnp.sum(gate_in_grad * spread_one, axis=(0, 1))
    normed_one_grad = (
        key_in_grad * temporal_lookup_mixture
        + value_in_grad * temporal_content_mixture
        + gate_in_grad * temporal_receptance_mixture
    )
    before_one_grad = (
        key_in_grad * (1.0 - temporal_lookup_mixture)
        + value_in_grad * (1.0 - temporal_content_mixture)
        + gate_in_grad * (1.0 - temporal_receptance_mixture)
    ) * keep_mask
    from_next = shifted(before_one_grad[:, :1, :], "seq", -1)
    normed_one_grad = normed_one_grad + jnp.concatenate(
        [before_one_grad[:, 1:, :], from_next], axis=1
    )
    input_norm_grad, grad_gain_one, grad_bias_one = norm_backward(
        normed_one_grad, unit_one, inv_one, opening_standardize_scale
    )
    input_grad = middle_grad + input_norm_grad
    channel_parts = reduce_channel(
        grad_gain_two,
        grad_bias_two,
        grad_ffn_mix_key,
        grad_ffn_mix_gate,
        grad_ffn_key,
        grad_ffn_value,
    )
    time_parts = (
        lax.psum_scatter(grad_gain_one, ("batch", "seq"), scatter_dimension=0, tiled=True),
        lax.psum_scatter(grad_bias_one, ("batch", "seq"), scatter_dimension=0, tiled=True),
        lax.psum_scatter(grad_mix_key, ("batch", "seq"), scatter_dimension=0, tiled=True),
        lax.psum_scatter(grad_mix_value, ("batch", "seq"), scatter_dimension=0, tiled=True),
        lax.psum_scatter(grad_mix_gate, ("batch", "seq"), scatter_dimension=0, tiled=True),
        lax.psum_scatter(decay_gradient, ("batch", "seq"), scatter_dimension=0, tiled=True),
        lax.psum_scatter(reward_derivative, ("batch", "seq"), scatter_dimension=0, tiled=True),
        lax.psum_scatter(grad_key, ("batch", "seq"), scatter_dimension=0, tiled=True),
        lax.psum_scatter(grad_value, ("batch", "seq"), scatter_dimension=0, tiled=True),
        lax.psum_scatter(grad_gate, ("batch", "seq"), scatter_dimension=0, tiled=True),
    )
    square_parts = (
        lax.psum_scatter(grad_output, ("batch", "seq"), scatter_dimension=0, tiled=True),
        lax.psum_scatter(grad_ffn_gate, ("batch", "seq"), scatter_dimension=0, tiled=True),
    )
    return (
        output,
        input_grad,
        time_parts[0],
        time_parts[1],
        time_parts[2],
        time_parts[3],
        time_parts[4],
        time_parts[5],
        time_parts[6],
        time_parts[7],
        time_parts[8],
        time_parts[9],
        square_parts[0],
        channel_parts[0],
        channel_parts[1],
        channel_parts[2],
        channel_parts[3],
        channel_parts[4],
        channel_parts[5],
        square_parts[1],
    )


def solution(mesh):
    return jax.shard_map(
        shards,
        mesh=mesh,
        in_specs=(
            P("batch", "seq", None),
            P("batch", None),
            P("batch", "seq", None),
            P(("batch", "seq")),
            P(("batch", "seq")),
            P(("batch", "seq")),
            P(("batch", "seq")),
            P(("batch", "seq")),
            P(("batch", "seq")),
            P(("batch", "seq")),
            P(("batch", "seq"), None),
            P(("batch", "seq"), None),
            P(("batch", "seq"), None),
            P(("batch", "seq"), None),
            P(("batch", "seq")),
            P(("batch", "seq")),
            P(("batch", "seq")),
            P(("batch", "seq")),
            P(("batch", "seq"), None),
            P(("batch", "seq"), None),
            P(("batch", "seq"), None),
        ),
        out_specs=(
            P("batch", "seq", None),
            P("batch", "seq", None),
            P(("batch", "seq")),
            P(("batch", "seq")),
            P(("batch", "seq")),
            P(("batch", "seq")),
            P(("batch", "seq")),
            P(("batch", "seq")),
            P(("batch", "seq")),
            P(("batch", "seq"), None),
            P(("batch", "seq"), None),
            P(("batch", "seq"), None),
            P(("batch", "seq"), None),
            P(("batch", "seq")),
            P(("batch", "seq")),
            P(("batch", "seq")),
            P(("batch", "seq")),
            P(("batch", "seq"), None),
            P(("batch", "seq"), None),
            P(("batch", "seq"), None),
        ),
        check_vma=False,
    )
```

profile of v0, /device:TPU:0, one launch (start us, length us, event | category | flops | bytes accessed | tf_op | source)
XLA Modules:
  0.0 1563.0 jit_solution(8487931678435674340)
XLA Ops:
  25.1 42.1 %all-reduce.26 = (bf16[1024]{0:T(1024)(128)(2,1)S(1)}, bf16[1024]{0:T(1024)(128)(2,1)S(1)}, bf16[1024]{0:T(1024)(128)(2,1)S(1)}, bf16[1024]{0:T(1024)(128)(2,1)S...) all-reduce(bf16[1024]{0:T(1024)(128)(2,1)S(1)} %dynamic-update-slic, ...), channel_id=1, replica_groups=mesh['batch'=4,'seq'=8] {'batch','seq'}, use_global_device_ids=true, to_apply=%add.4 | all-reduce | flops 11264 | bytes 45056
  77.7 15.6 all-reduce.6
  101.2 27.7 %all-gather.19.cloned.1.call-done = bf16[1024,1024]{1,0:T(8,128)(2,1)} async-done(((bf16[32,1024]{1,0:T(8,128)(2,1)}), bf16[1024,1024]{1,0:T(8,128)(2,1)}) %all-gather.19.cloned.1.call-update) | async-done | bytes 2097168 | tf_op jit(solution)/shard_map/all_gather | solution.py:166
  128.9 5.8 fusion.75
  134.7 14.0 all-gather.5
  148.6 14.0 all-gather.6
  162.8 8.9 broadcast_multiply_fusion
  171.7 15.5 all-gather.17.cloned.1.call-done
  187.2 9.9 multiply_convert_fusion.3
  197.1 48.3 %all-gather.23.cloned.1.call-done = bf16[1024,1024]{1,0:T(8,128)(2,1)} async-done(((bf16[32,1024]{1,0:T(8,128)(2,1)}), bf16[1024,1024]{1,0:T(8,128)(2,1)}) %all-gather.23.cloned.1.call-update) | async-done | bytes 2097168 | tf_op jit(solution)/shard_map/all_gather | solution.py:169
  255.0 69.5 %all-gather.27.cloned.1.call-done = bf16[1024,4096]{1,0:T(8,128)(2,1)} async-done(((bf16[32,4096]{1,0:T(8,128)(2,1)}), bf16[1024,4096]{1,0:T(8,128)(2,1)}) %all-gather.27.cloned.1.call-update) | async-done | bytes 8388624 | tf_op jit(solution)/shard_map/all_gather | solution.py:174
  324.6 11.4 fusion.12
  336.0 67.4 %all-gather.29.cloned.1.call-done = bf16[4096,1024]{1,0:T(8,128)(2,1)} async-done(((bf16[128,1024]{1,0:T(8,128)(2,1)}), bf16[4096,1024]{1,0:T(8,128)(2,1)}) %all-gather.29.cloned.1.call-update) | async-done | bytes 8388624 | tf_op jit(solution)/shard_map/all_gather | solution.py:175
  403.4 11.6 fusion.8
  415.0 46.5 %all-gather.25.cloned.1.call-done = bf16[1024,1024]{1,0:T(8,128)(2,1)} async-done(((bf16[32,1024]{1,0:T(8,128)(2,1)}), bf16[1024,1024]{1,0:T(8,128)(2,1)}) %all-gather.25.cloned.1.call-update) | async-done | bytes 2097168 | tf_op jit(solution)/shard_map/all_gather | solution.py:176
  461.5 6.4 fusion.42
  472.4 13.4 multiply_convert_fusion
  485.8 8.4 fusion.10
  508.5 4.9 fusion.48
  513.5 14.3 all-gather.7
  527.8 14.4 all-gather.8
  542.2 7.1 multiply_reduce_fusion
  550.3 7.5 multiply_reduce_fusion.5
  577.8 12.8 convolution_bitcast_fusion.1
  590.9 14.6 convolution_bitcast_fusion
  622.4 41.1 %all-reduce.25 = (f32[1024]{0:T(1024)S(1)}, f32[1024]{0:T(1024)S(1)}, f32[1024]{0:T(1024)S(1)}, f32[1024]{0:T(1024)S(1)}, f32[1024]{0:T(1024)S(1)}, /*index=5*/f...) all-reduce(f32[1024]{0:T(1024)S(1)} %get-tuple-element.485, ...), channel_id=7, replica_groups=mesh['batch'=4,'seq'=8] {'batch','seq'}, use_global_device_ids=true, to_apply=%region_23.24.clone | all-reduce | flops 11264 | bytes 90112
  673.6 82.5 %reduce-scatter.8.cloned.1.call-done = f32[32,1024]{1,0:T(8,128)} async-done(((f32[1024,1024]{1,0:T(8,128)}), f32[32,1024]{1,0:T(8,128)}) %reduce-scatter.8.cloned.1.call-update) | async-done | bytes 131088 | tf_op jit(solution)/shard_map/reduce_scatter | solution.py:385
  756.1 142.0 %reduce-scatter.10.cloned.1.call-done = f32[32,1024]{1,0:T(8,128)} async-done(((f32[1024,1024]{1,0:T(8,128)}), f32[32,1024]{1,0:T(8,128)}) %reduce-scatter.10.cloned.1.call-update) | async-done | bytes 131088 | tf_op jit(solution)/shard_map/reduce_scatter | solution.py:386
  898.1 142.6 %reduce-scatter.12.cloned.1.call-done = f32[32,1024]{1,0:T(8,128)} async-done(((f32[1024,1024]{1,0:T(8,128)}), f32[32,1024]{1,0:T(8,128)}) %reduce-scatter.12.cloned.1.call-update) | async-done | bytes 131088 | tf_op jit(solution)/shard_map/reduce_scatter | solution.py:387
  1040.6 142.3 %reduce-scatter.14.cloned.1.call-done = f32[32,1024]{1,0:T(8,128)} async-done(((f32[1024,1024]{1,0:T(8,128)}), f32[32,1024]{1,0:T(8,128)}) %reduce-scatter.14.cloned.1.call-update) | async-done | bytes 131088 | tf_op jit(solution)/shard_map/reduce_scatter | solution.py:390
  1182.9 186.2 %reduce-scatter.16.cloned.1.call-done = f32[32,4096]{1,0:T(8,128)} async-done(((f32[1024,4096]{1,0:T(8,128)}), f32[32,4096]{1,0:T(8,128)}) %reduce-scatter.16.cloned.1.call-update) | async-done | bytes 524304 | tf_op jit(solution)/shard_map/reduce_scatter | solution.py:69
  1369.1 187.1 %reduce-scatter.18.cloned.1.call-done = f32[128,1024]{1,0:T(8,128)} async-done(((f32[4096,1024]{1,0:T(8,128)}), f32[128,1024]{1,0:T(8,128)}) %reduce-scatter.18.cloned.1.call-update) | async-done | bytes 524304 | tf_op jit(solution)/shard_map/reduce_scatter | solution.py:71
  (274 shorter events, 112.4 us)
Async XLA Ops:
  7.2 64.3 %copy-start.40 = (u32[32]{0:T(128)S(1)}, u32[32]{0:T(128)}, u32[]{:S(2)}) copy-start(u32[32]{0:T(128)} %constant.180) | copy-start | bytes 388
  7.2 63.8 %copy-start = (bf16[2,256,1024]{2,1,0:T(8,128)(2,1)S(1)}, bf16[2,256,1024]{2,1,0:T(8,128)(2,1)}, u32[]{:S(2)}) copy-start(bf16[2,256,1024]{2,1,0:T(8,128)(2,1)} %param.25) | copy-start | bytes 3145732
  7.2 89.4 %all-gather.21.cloned.1.call-start = ((), (), s32[]{:S(2)}) async-start(), calls=%async_computation.9 | async-start | bytes 2162688 | tf_op jit(solution)/shard_map/all_gather | solution.py:167
  7.9 120.9 %all-gather.19.cloned.1.call-start = ((), (), s32[]{:S(2)}) async-start(), calls=%async_computation.8 | async-start | bytes 2162688 | tf_op jit(solution)/shard_map/all_gather | solution.py:166
  8.7 178.5 %all-gather.17.cloned.1.call-start = ((), (), s32[]{:S(2)}) async-start(), calls=%async_computation.7 | async-start | bytes 2162688 | tf_op jit(solution)/shard_map/all_gather | solution.py:168
  9.4 236.0 %all-gather.23.cloned.1.call-start = ((), (), s32[]{:S(2)}) async-start(), calls=%async_computation.10 | async-start | bytes 2162688 | tf_op jit(solution)/shard_map/all_gather | solution.py:169
  10.0 314.6 %all-gather.27.cloned.1.call-start = ((), (), s32[]{:S(2)}) async-start(), calls=%async_computation.12 | async-start | bytes 8650752 | tf_op jit(solution)/shard_map/all_gather | solution.py:174
  10.6 392.8 %all-gather.29.cloned.1.call-start = ((), (), s32[]{:S(2)}) async-start(), calls=%async_computation.13 | async-start | bytes 8650752 | tf_op jit(solution)/shard_map/all_gather | solution.py:175
  11.2 450.3 %all-gather.25.cloned.1.call-start = ((), (), s32[]{:S(2)}) async-start(), calls=%async_computation.11 | async-start | bytes 2162688 | tf_op jit(solution)/shard_map/all_gather | solution.py:176
  12.0 81.4 %collective-permute-start = (bf16[2,1,1024]{2,1,0:T(2,128)(2,1)S(1)}, bf16[2,1,1024]{2,1,0:T(2,128)(2,1)S(1)}, u32[]{:S(2)}, u32[]{:S(2)}) collective-permute-start(bf16[2,1,1024]{2,1,0:T(2,128)(2,1)S(1)} %slice.42), channel_id=1, source_target_pairs={{0,1},{1,2},{2,3},{3,4},{4,5},{5,6},{6,7},{8,9},{9,10},{10,11},{11... | collective-permute-start | bytes 12296 | tf_op jit(solution)/shard_map/ppermute | solution.py:15
  14.4 659.2 %reduce-scatter.20.cloned.1.call-start = ((), (), s32[]{:S(2)}) async-start(), calls=%async_computation.20 | async-start | bytes 4325376 | tf_op jit(solution)/shard_map/reduce_scatter | solution.py:391
  77.7 19.0 %copy-start.5 = (f32[2,256,1024]{2,1,0:T(8,128)}, f32[2,256,1024]{2,1,0:T(8,128)S(1)}, u32[]{:S(2)}) copy-start(f32[2,256,1024]{2,1,0:T(8,128)S(1)} %fusion.28) | copy-start | bytes 6291460
  134.6 52.6 %copy-start.3 = (f32[2,256,1024]{2,1,0:T(8,128)}, f32[2,256,1024]{2,1,0:T(8,128)S(1)}, u32[]{:S(2)}) copy-start(f32[2,256,1024]{2,1,0:T(8,128)S(1)} %get-tuple-element.587) | copy-start | bytes 6291460
  249.5 3.0 collective-permute-start.1
  472.2 283.9 %reduce-scatter.8.cloned.1.call-start = ((), (), s32[]{:S(2)}) async-start(), calls=%async_computation.14 | async-start | bytes 4325376 | tf_op jit(solution)/shard_map/reduce_scatter | solution.py:385
  485.8 8.4 copy-start.2
  485.8 8.4 copy-start.26
  485.8 8.4 copy-start.35
  498.6 3.3 collective-permute-start.2
  508.5 33.7 %copy-start.4 = (f32[2,256,1024]{2,1,0:T(8,128)S(1)}, f32[2,256,1024]{2,1,0:T(8,128)}, u32[]{:S(2)}) copy-start(f32[2,256,1024]{2,1,0:T(8,128)} %copy-done.3) | copy-start | bytes 6291460
  508.5 33.7 %copy-start.7 = (f32[256,2048]{1,0:T(8,128)S(1)}, f32[256,2048]{1,0:T(8,128)}, u32[]{:S(2)}) copy-start(f32[256,2048]{1,0:T(8,128)} %get-tuple-element.601) | copy-start | bytes 6291460
  508.5 33.7 %copy-start.8 = (f32[256,2048]{1,0:T(8,128)S(1)}, f32[256,2048]{1,0:T(8,128)}, u32[]{:S(2)}) copy-start(f32[256,2048]{1,0:T(8,128)} %get-tuple-element.602) | copy-start | bytes 6291460
  508.5 33.7 %copy-start.13 = (f32[2,256,1024]{2,1,0:T(8,128)S(1)}, f32[2,256,1024]{2,1,0:T(8,128)}, u32[]{:S(2)}) copy-start(f32[2,256,1024]{2,1,0:T(8,128)} %get-tuple-element.577) | copy-start | bytes 6291460
  513.5 35.8 %copy-start.9 = (f32[2,256,1024]{2,1,0:T(8,128)}, f32[2,256,1024]{2,1,0:T(8,128)S(1)}, u32[]{:S(2)}) copy-start(f32[2,256,1024]{2,1,0:T(8,128)S(1)} %get-tuple-element.556) | copy-start | bytes 6291460
  513.5 35.8 %copy-start.11 = (f32[2,256,1024]{2,1,0:T(8,128)}, f32[2,256,1024]{2,1,0:T(8,128)S(1)}, u32[]{:S(2)}) copy-start(f32[2,256,1024]{2,1,0:T(8,128)S(1)} %get-tuple-element.557) | copy-start | bytes 6291460
  550.3 8.5 copy-start.24
  562.2 335.9 %reduce-scatter.10.cloned.1.call-start = ((), (), s32[]{:S(2)}) async-start(), calls=%async_computation.15 | async-start | bytes 4325376 | tf_op jit(solution)/shard_map/reduce_scatter | solution.py:386
  567.0 473.7 %reduce-scatter.12.cloned.1.call-start = ((), (), s32[]{:S(2)}) async-start(), calls=%async_computation.16 | async-start | bytes 4325376 | tf_op jit(solution)/shard_map/reduce_scatter | solution.py:387
  571.7 611.2 %reduce-scatter.14.cloned.1.call-start = ((), (), s32[]{:S(2)}) async-start(), calls=%async_computation.17 | async-start | bytes 4325376 | tf_op jit(solution)/shard_map/reduce_scatter | solution.py:390
  577.8 791.4 %reduce-scatter.16.cloned.1.call-start = ((), (), s32[]{:S(2)}) async-start(), calls=%async_computation.18 | async-start | bytes 17301504 | tf_op jit(solution)/shard_map/reduce_scatter | solution.py:69
  590.7 965.6 %reduce-scatter.18.cloned.1.call-start = ((), (), s32[]{:S(2)}) async-start(), calls=%async_computation.19 | async-start | bytes 17301504 | tf_op jit(solution)/shard_map/reduce_scatter | solution.py:71
  612.2 5.1 collective-permute-start.3
  (30 other events, 77.2 us)
Sparse Core Ops, SparseCore 0:
  11.0 59.3 all-gather.20
  73.4 55.4 all-gather.18
  131.9 55.3 all-gather.16
  190.1 55.3 all-gather.22
  248.3 76.2 all-gather.26
  327.4 75.9 all-gather.28
  406.4 55.0 all-gather.24
  472.3 141.3 reduce-scatter.19
  616.5 139.5 reduce-scatter.7
  758.8 139.2 reduce-scatter.9
  900.9 139.6 reduce-scatter.11
  1043.3 139.5 reduce-scatter.13
  1185.8 183.2 reduce-scatter.15
  1371.9 184.3 reduce-scatter.17
where the time goes:
time: 1570 us; the launch traced here: 1560 us
  waiting for transfers between devices  1160 us (74%)
  blocking collectives  156 us (10%)
  matrix products  149 us (9%)
  other arithmetic  36.9 us (2%)
  local copies, waits for them, and re-layouts  34.6 us (2%)
    reduce_scatter x1, waiting for transfers between devices, reduce_channel(): lax.psum_scatter(ffn_value_weight, ('batch', 'seq'), scatter_dimension=0,...  187 us
    reduce_scatter x1, waiting for transfers between devices, reduce_channel(): lax.psum_scatter(ffn_key_weight, ('batch', 'seq'), scatter_dimension=0, t...  186 us
    reduce_scatter x1, waiting for transfers between devices, shards(): lax.psum_scatter(grad_gate, ('batch', 'seq'), scatter_dimension=0, tiled=...  143 us
    reduce_scatter x1, waiting for transfers between devices, shards(): lax.psum_scatter(grad_output, ('batch', 'seq'), scatter_dimension=0, tile...  142 us
    reduce_scatter x1, waiting for transfers between devices, shards(): lax.psum_scatter(grad_value, ('batch', 'seq'), scatter_dimension=0, tiled...  142 us
    unnamed x3, blocking collectives  98.8 us
    reduce_scatter x1, waiting for transfers between devices, shards(): lax.psum_scatter(grad_key, ('batch', 'seq'), scatter_dimension=0, tiled=T...  82.5 us
    all_gather x1, waiting for transfers between devices, shards(): lax.all_gather(feature_lookup_projection, ('batch', 'seq'), axis=0, tiled...  69.5 us
  transfers between devices with their start and end apart: 18, of which 13 were waited for; matrix products, arithmetic and copies ran while one was open for 13% of the time, Pallas kernels for 0%

commit v1 on v0

v1 whole, which is shorter than its diff:
```python
from functools import partial

import jax
import jax.numpy as jnp
from jax import lax
from jax.experimental import pallas as pl
from jax.experimental.pallas import tpu as pltpu
from jax.sharding import PartitionSpec as P

eps = 1e-05
highest = lax.Precision.HIGHEST
BOTH = ("batch", "seq")


def moved(rule):
    return [(f, rule(f)) for f in range(32)]


FLIP_X = moved(lambda f: f ^ 8)
FLIP_Y = moved(lambda f: f ^ 16)
FLIP_C = moved(lambda f: f ^ 1)


def turn_z(by):
    return moved(lambda f: (f & 25) | ((((f >> 1) + by) & 3) << 1))


def sent(array, pairs):
    return lax.ppermute(array, BOTH, pairs)


def place_of(flat, dy, dx, dz, dc):
    turned = ((((flat >> 1) & 3) + dz) & 3) * 2
    return ((flat & 25) | turned) ^ (dy * 16 + dx * 8 + dc)


def tied(array, *after):
    zero = jnp.zeros((), jnp.float32)
    for other in after:
        first = other[(0,) * other.ndim].astype(jnp.float32)
        zero = zero + jnp.minimum(jnp.abs(first), 0.0)
    return array + zero.astype(array.dtype)


def assemble_kernel(owners, start, columns, slots_ref, *refs):
    pieces, out_ref, sems = refs[:-2], refs[-2], refs[-1]
    rows = out_ref.shape[1]
    copies = []
    number = 0
    for piece, count in zip(pieces, owners):
        for k in range(count):
            for q in range(columns):
                copies.append(
                    pltpu.make_async_copy(
                        piece.at[k, pl.ds(start + q * rows, rows), :],
                        out_ref.at[slots_ref[number], :, pl.ds(q * 1024, 1024)],
                        sems.at[number, q],
                    )
                )
            number += 1
    for copy in copies:
        copy.start()
    for copy in copies:
        copy.wait()


def assemble(pieces, slots, start, rows, columns):
    counts = [piece.shape[0] for piece in pieces]
    shape = (32, rows, columns * 1024)
    whole = pl.pallas_call(
        partial(assemble_kernel, counts, start, columns),
        out_shape=jax.ShapeDtypeStruct(shape, pieces[0].dtype),
        in_specs=[pl.BlockSpec(memory_space=pltpu.SMEM)]
        + [pl.BlockSpec(memory_space=pl.ANY)] * len(pieces),
        out_specs=pl.BlockSpec(memory_space=pltpu.VMEM),
        scratch_shapes=[pltpu.SemaphoreType.DMA((32, columns))],
        compiler_params=pltpu.CompilerParams(vmem_limit_bytes=24 * 1024 * 1024),
        cost_estimate=pl.CostEstimate(
            flops=0, transcendentals=0, bytes_accessed=2 * 2 * 32 * rows * columns * 1024
        ),
    )(slots, *pieces)
    return whole.reshape(32 * rows, columns * 1024)


def stacked(parts):
    rows = [part[:, q : q + 1024] for part in parts for q in range(0, part.shape[1], 1024)]
    return jnp.concatenate(rows, axis=0) if len(rows) > 1 else rows[0]


def around(part):
    return [sent(part, turn_z(d)) for d in (1, 2, 3)]


def long_slots(flat):
    every = (0, 1, 2, 3)
    steps = [(0, 0, every), (0, 1, every), (1, 0, every), (1, 1, (0, 1)), (1, 1, (2, 3))]
    return jnp.stack(
        [place_of(flat, dy, dx, -dz, dc) for dc in (0, 1) for dy, dx, dzs in steps for dz in dzs]
    ).astype(jnp.int32)


def send_far(from_x, from_y):
    half = from_x.shape[0] // 2
    return sent(from_x[:half], FLIP_Y), sent(from_y[half:], FLIP_X)


def both_cores(pieces):
    return pieces + [sent(piece, FLIP_C) for piece in pieces]


def vectors_of(blocks):
    rows = blocks[:, 0, : 11 * 32].reshape(32, 11, 32).astype(jnp.float32)
    return jnp.swapaxes(rows, 0, 1).reshape(11, 1024)


def choice(flat, width):
    index = jnp.arange(width)
    block, within = index // (width // 32), index % (width // 32)
    dc, rest = block >> 4, block & 15
    dy, dx, dz = rest >> 3, (rest >> 2) & 1, rest & 3
    wanted = place_of(flat, dy, dx, dz, dc) * (width // 32) + within
    return (jnp.arange(width)[:, None] == wanted[None, :]).astype(jnp.bfloat16)


def owner_order(flat):
    block = jnp.arange(32)
    dc, rest = block >> 4, block & 15
    dy, dx, dz = rest >> 3, (rest >> 2) & 1, rest & 3
    return place_of(flat, dy, dx, dz, dc).astype(jnp.int32)


def pick_kernel(order_ref, rows_ref, out_ref, sems):
    copies = [
        pltpu.make_async_copy(
            rows_ref.at[:, pl.ds(pl.multiple_of(order_ref[j] * 128, 128), 128)],
            out_ref.at[:, pl.ds(j * 128, 128)],
            sems.at[j],
        )
        for j in range(32)
    ]
    for copy in copies:
        copy.start()
    for copy in copies:
        copy.wait()


def pick(rows_in, order):
    return pl.pallas_call(
        pick_kernel,
        out_shape=jax.ShapeDtypeStruct(rows_in.shape, rows_in.dtype),
        in_specs=[pl.BlockSpec(memory_space=pltpu.SMEM), pl.BlockSpec(memory_space=pl.ANY)],
        out_specs=pl.BlockSpec(memory_space=pltpu.VMEM),
        scratch_shapes=[pltpu.SemaphoreType.DMA((32,))],
        compiler_params=pltpu.CompilerParams(vmem_limit_bytes=24 * 1024 * 1024),
    )(order, rows_in)


def chip_grad(own_in, other_in, grads, other_grads):
    total = jnp.einsum(
        "td,te->de", own_in, grads, preferred_element_type=jnp.float32
    ) + jnp.einsum("td,te->de", other_in, other_grads, preferred_element_type=jnp.float32)
    return total.astype(jnp.bfloat16).reshape(16, own_in.shape[1] // 16, grads.shape[1])


def ordered_halves(rows_in, flat):
    width = rows_in.shape[-1]
    rows_in = rows_in.reshape(-1, width)
    if width == 4096:
        ordered = pick(rows_in, owner_order(flat))
    else:
        ordered = jnp.dot(
            rows_in, choice(flat, width), preferred_element_type=jnp.bfloat16
        )
    return ordered[:, : width // 2], ordered[:, width // 2 :]


def sent_together(arrays):
    got = sent(jnp.concatenate(arrays, axis=1) if len(arrays) > 1 else arrays[0], FLIP_C)
    ends = [sum(a.shape[1] for a in arrays[: i + 1]) for i in range(len(arrays))]
    return [got[:, end - a.shape[1] : end] for a, end in zip(arrays, ends)]


def wide(array):
    return array.astype(jnp.float32)


def narrow(array):
    return array.astype(jnp.bfloat16)


def quarters(parts):
    return parts.reshape((2, 2, 4) + parts.shape[1:])


def add_corner(quad, add_a, add_b):
    to_y = jnp.concatenate([narrow(wide(quad[1, 0, :2]) + wide(add_a)), quad[1, 0, 2:]])
    to_x = jnp.concatenate([quad[0, 1, :2], narrow(wide(quad[0, 1, 2:]) + wide(add_b))])
    return to_y, to_x


def send_corner(quad):
    return sent(quad[1, 1, :2], FLIP_X), sent(quad[1, 1, 2:], FLIP_Y)


def send_sides(to_y, to_x):
    return sent(to_y, FLIP_Y), sent(to_x, FLIP_X)


def add_sides(quad, from_y, from_x):
    column = wide(quad[0, 0]) + wide(from_y) + wide(from_x)
    return column[0], [narrow(column[d]) for d in (1, 2, 3)]


def send_column(outgoing):
    return [sent(part, turn_z(d)) for d, part in zip((1, 2, 3), outgoing)]


def add_all(first, others):
    for other in others:
        first = first + wide(other)
    return first


def sum_vectors(rows_in, flat):
    total = rows_in
    for pairs in (FLIP_C, FLIP_X, FLIP_Y):
        total = total + sent(total, pairs)
    total = total + sum(sent(total, turn_z(d)) for d in (1, 2, 3))
    count = total.shape[1] // 32
    return lax.dynamic_slice_in_dim(total, flat * count, count, 1)


def shifted(shard, axis, by):
    length = lax.axis_size(axis)
    pairs = [(i, i + by) for i in range(length) if 0 <= i + by < length]
    return lax.ppermute(shard, axis, pairs)


def carried_in(part, starts_in, decay_vec, length, reverse):
    count = lax.axis_size("seq")
    place = lax.axis_index("seq")
    clear = 1.0 - starts_in.astype(jnp.float32)
    block_fade = jnp.exp(-length * decay_vec)

    def clear_of(block):
        return lax.dynamic_index_in_dim(clear, jnp.clip(block, 0, count - 1), 1, True)

    if count == 8:
        chip, core = place >> 1, place & 1
        other = sent(part, FLIP_C)
        is_far = (core == 1) == (not reverse)
        near = jnp.where(is_far, other, part)
        last = jnp.where(is_far, part, other)
        first_block, second_block = chip * 2 + (1 if reverse else 0), chip * 2 + (0 if reverse else 1)
        joined = clear_of(second_block) * block_fade * near + last
        step = -1 if reverse else 1
        entering = jnp.zeros_like(part)
        open_way = jnp.ones((part.shape[1], 1), jnp.float32)
        for d in (1, 2, 3):
            beside = chip - step * d
            live = ((beside >= 0) & (beside < 4)).astype(jnp.float32)
            fade = live * open_way * jnp.exp(-float(2 * (d - 1) * length) * decay_vec)
            entering = entering + fade * sent(joined, turn_z(step * d))
            open_way = open_way * clear_of(2 * beside) * clear_of(2 * beside + 1)
        return jnp.where(is_far, clear_of(first_block) * block_fade * entering + near, entering)
    gathered = lax.all_gather(part, "seq")

    def one(lap, state):
        source = count - 1 - lap if reverse else lap
        return clear_of(source) * block_fade * state + lax.dynamic_index_in_dim(gathered, source, 0, False)

    ahead = count - 1 - place if reverse else place
    return lax.fori_loop(0, ahead, one, jnp.zeros_like(part))


def norm_forward(values, gain_vec, bias_vec):
    centre = values - jnp.mean(values, axis=-1, keepdims=True)
    inv_std = lax.rsqrt(jnp.mean(centre * centre, axis=-1, keepdims=True) + eps)
    normed = centre * inv_std
    return (normed * gain_vec + bias_vec, normed, inv_std)


def norm_backward(grads, normed, inv_std, gain_vec):
    scaled = grads * gain_vec
    inner = (
        scaled
        - jnp.mean(scaled, axis=-1, keepdims=True)
        - normed * jnp.mean(scaled * normed, axis=-1, keepdims=True)
    )
    return (inv_std * inner, jnp.sum(grads * normed, axis=(0, 1)), jnp.sum(grads, axis=(0, 1)))


def project(rows_in, weight):
    return jnp.einsum("rtd,de->rte", rows_in, weight, preferred_element_type=jnp.float32)


def project_back(grads, weight):
    return jnp.einsum("rte,de->rtd", grads, weight, preferred_element_type=jnp.float32)


def weight_grad(rows_in, grads):
    total = jnp.einsum("rtd,rte->de", rows_in, grads, preferred_element_type=jnp.float32)
    return lax.psum_scatter(total, BOTH, scatter_dimension=0, tiled=True)


def weighted_value_local(
    key_row_block,
    value_row_block,
    feature_forgetting_rate,
    present_reward,
    state_numerator,
    state_denominator,
    document_segments,
):
    length = key_row_block.shape[1]
    width = key_row_block.shape[2]
    order_idx = jnp.arange(length)
    step_pos = order_idx.astype(jnp.float32)[:, None]
    powered_lookups = jnp.exp(key_row_block)
    grow_exp = jnp.exp(step_pos * feature_forgetting_rate)
    shrink = jnp.exp((1.0 - step_pos) * feature_forgetting_rate)
    pair_mask = (
        (order_idx[None, :] < order_idx[:, None])[None]
        & (document_segments[:, None, :] == document_segments[:, :, None])
    ).astype(jnp.float32)
    weighted = jnp.concatenate(
        [powered_lookups * value_row_block, powered_lookups], axis=2
    ) * jnp.concatenate([grow_exp, grow_exp], axis=1)
    past_sums = jnp.einsum(
        "rti,rie->rte", pair_mask, weighted, precision=highest
    ) * jnp.concatenate([shrink, shrink], axis=1)
    carry_fade = (document_segments == 0).astype(jnp.float32)[:, :, None] * jnp.exp(
        -step_pos * feature_forgetting_rate
    )
    present_token_contribution = jnp.exp(present_reward) * powered_lookups
    numer = (
        carry_fade * state_numerator[:, None, :]
        + past_sums[:, :, :width]
        + present_token_contribution * value_row_block
    )
    denom = (
        carry_fade * state_denominator[:, None, :]
        + past_sums[:, :, width:]
        + present_token_contribution
    )
    return numer / denom


def tail_terms(key_row_block, value_row_block, feature_forgetting_rate, document_segments):
    length = key_row_block.shape[1]
    step_pos = jnp.arange(length).astype(jnp.float32)[:, None]
    powered_lookups = jnp.exp(key_row_block)
    tail_fade = (document_segments == document_segments[:, -1:]).astype(jnp.float32)[
        :, :, None
    ] * jnp.exp((step_pos - (length - 1)) * feature_forgetting_rate)
    return (
        jnp.sum(tail_fade * powered_lookups * value_row_block, axis=1),
        jnp.sum(tail_fade * powered_lookups, axis=1),
        tail_fade,
        powered_lookups,
    )


def shards(
    tuned,
    incoming_activations,
    sequence_extents,
    upstream_sensitivity,
    initial_normalizer_scale,
    initial_normalizer_offset,
    temporal_lookup_fraction,
    temporal_content_fraction,
    temporal_receptance_fraction,
    feature_forgetting_rate,
    present_reward,
    temporal_lookup_projection,
    temporal_content_projection,
    temporal_receptance_projection,
    temporal_result_projection,
    later_normalizer_scale,
    later_normalizer_offset,
    feature_lookup_fraction,
    feature_receptance_fraction,
    feature_lookup_projection,
    feature_content_projection,
    feature_receptance_projection,
):
    flat = lax.axis_index("batch") * lax.axis_size("seq") + lax.axis_index("seq")
    vectors = jnp.stack(
        [
            initial_normalizer_scale,
            initial_normalizer_offset,
            temporal_lookup_fraction,
            temporal_content_fraction,
            temporal_receptance_fraction,
            feature_forgetting_rate,
            present_reward,
            later_normalizer_scale,
            later_normalizer_offset,
            feature_lookup_fraction,
            feature_receptance_fraction,
        ]
    )
    if tuned:
        order = long_slots(flat)
        late = lax.all_gather(
            stacked(
                [
                    feature_lookup_projection,
                    feature_content_projection,
                    feature_receptance_projection,
                    temporal_result_projection,
                ]
            ),
            BOTH,
        )
        packed = jnp.pad(vectors.reshape(1, -1), ((0, 15), (0, 1024 - vectors.size)))
        part = stacked(
            [
                temporal_lookup_projection,
                temporal_content_projection,
                temporal_receptance_projection,
                packed,
            ]
        )
        column = jnp.stack([part] + around(part))
        from_x, from_y = sent(column, FLIP_X), sent(column, FLIP_Y)
        early = both_cores([column, from_x, from_y, *send_far(from_x, from_y)])
        vectors = vectors_of(assemble(early, order, 96, 16, 1).reshape(32, 16, 1024))
        lookup_weight = assemble(early, order, 0, 32, 1)
        content_weight = assemble(early, order, 32, 32, 1)
        receptance_weight = assemble(early, order, 64, 32, 1)
        in_turn = jnp.arange(32, dtype=jnp.int32)
        ffn_key_weight = assemble([late], in_turn, 0, 32, 4)
        ffn_value_weight = assemble([late], in_turn, 128, 128, 1)
        ffn_gate_weight = assemble([late], in_turn, 256, 32, 1)
        result_weight = assemble([late], in_turn, 288, 32, 1)
    else:
        (
            lookup_weight,
            content_weight,
            receptance_weight,
            result_weight,
            ffn_key_weight,
            ffn_gate_weight,
            ffn_value_weight,
        ) = [
            lax.all_gather(part, BOTH, axis=0, tiled=True)
            for part in (
                temporal_lookup_projection,
                temporal_content_projection,
                temporal_receptance_projection,
                temporal_result_projection,
                feature_lookup_projection,
                feature_receptance_projection,
                feature_content_projection,
            )
        ]
        vectors = lax.all_gather(vectors, BOTH, axis=1, tiled=True).astype(jnp.float32)
    (
        opening_standardize_scale,
        opening_standardize_offset,
        temporal_lookup_mixture,
        temporal_content_mixture,
        temporal_receptance_mixture,
        decay_vec,
        reward_array,
        closing_standardize_scale,
        closing_standardize_offset,
        feature_lookup_mixture,
        feature_receptance_mixture,
    ) = tuple(vectors[i] for i in range(11))
    rows, length, width = incoming_activations.shape
    starts = jnp.cumsum(sequence_extents, axis=1) - sequence_extents
    places = lax.axis_index("seq") * length + jnp.arange(length, dtype=jnp.int32)
    resets = jnp.any(
        (starts[:, None, :] == places[None, :, None]) & (sequence_extents[:, None, :] > 0), axis=2
    )
    document_segments = jnp.cumsum(resets.astype(jnp.int32), axis=1)
    keep_mask = 1.0 - resets.astype(jnp.float32)[:, :, None]
    clear_flag = (document_segments[:, -1:] == 0).astype(jnp.float32)
    starts_in = jnp.any(
        (starts[:, None, :] // length == jnp.arange(lax.axis_size("seq"))[None, :, None])
        & (sequence_extents[:, None, :] > 0),
        axis=2,
    )

    inputs = incoming_activations.astype(jnp.float32)
    left_rows = shifted(incoming_activations[:, length - 1 :, :], "seq", 1)
    normed_one, unit_one, inv_one = norm_forward(
        inputs, opening_standardize_scale, opening_standardize_offset
    )
    left_normed, _, _ = norm_forward(
        left_rows.astype(jnp.float32), opening_standardize_scale, opening_standardize_offset
    )
    before_one = jnp.concatenate([left_normed, normed_one[:, :-1, :]], axis=1) * keep_mask
    key_in = (
        normed_one * temporal_lookup_mixture + before_one * (1.0 - temporal_lookup_mixture)
    ).astype(jnp.bfloat16)
    value_in = (
        normed_one * temporal_content_mixture + before_one * (1.0 - temporal_content_mixture)
    ).astype(jnp.bfloat16)
    gate_in = (
        normed_one * temporal_receptance_mixture + before_one * (1.0 - temporal_receptance_mixture)
    ).astype(jnp.bfloat16)
    key_row_block = project(key_in, lookup_weight)
    value_row_block = project(value_in, content_weight)
    gates = jax.nn.sigmoid(project(gate_in, receptance_weight))
    tail_num, tail_den, tail_fade, powered_lookups = tail_terms(
        key_row_block, value_row_block, decay_vec, document_segments
    )
    state_numerator, state_denominator = carried_in(
        jnp.stack([tail_num, tail_den]), starts_in, decay_vec, length, False
    )
    mixed, weighted_value_backward = jax.vjp(
        partial(weighted_value_local, document_segments=document_segments),
        key_row_block,
        value_row_block,
        decay_vec,
        reward_array,
        state_numerator,
        state_denominator,
    )
    gated = (gates * mixed).astype(jnp.bfloat16)
    if tuned:
        own_key, far_key = ordered_halves(key_in, flat)
        own_value, far_value = ordered_halves(value_in, flat)
        own_gate, far_gate = ordered_halves(gate_in, flat)
        own_gated, far_gated = ordered_halves(gated, flat)
        other_key, other_value, other_gate, other_gated = sent_together(
            [far_key, far_value, far_gate, far_gated]
        )
    middle = inputs + project(gated, result_weight)
    normed_two, unit_two, inv_two = norm_forward(
        middle, closing_standardize_scale, closing_standardize_offset
    )
    before_rows = shifted(normed_two[:, length - 1 :, :], "seq", 1)
    before_two = jnp.concatenate([before_rows, normed_two[:, :-1, :]], axis=1) * keep_mask
    ffn_key_in = (
        normed_two * feature_lookup_mixture + before_two * (1.0 - feature_lookup_mixture)
    ).astype(jnp.bfloat16)
    ffn_gate_in = (
        normed_two * feature_receptance_mixture + before_two * (1.0 - feature_receptance_mixture)
    ).astype(jnp.bfloat16)
    hidden_pre = project(ffn_key_in, ffn_key_weight)
    hidden = jnp.square(jax.nn.relu(hidden_pre)).astype(jnp.bfloat16)
    if tuned:
        own_ffn_key, far_ffn_key = ordered_halves(ffn_key_in, flat)
        own_ffn_gate, far_ffn_gate = ordered_halves(ffn_gate_in, flat)
        own_hidden, far_hidden = ordered_halves(hidden, flat)
        other_ffn_key, other_ffn_gate = sent_together([far_ffn_key, far_ffn_gate])
        (other_hidden,) = sent_together([far_hidden])
    ffn_value = project(hidden, ffn_value_weight)
    ffn_gates = jax.nn.sigmoid(project(ffn_gate_in, ffn_gate_weight))
    output = (middle + ffn_gates * ffn_value).astype(jnp.bfloat16)
    matrices = (
        lookup_weight,
        content_weight,
        receptance_weight,
        result_weight,
        ffn_key_weight,
        ffn_value_weight,
        ffn_gate_weight,
    )
    grad_out = upstream_sensitivity.astype(jnp.float32)
    value_grad = (grad_out * ffn_gates).astype(jnp.bfloat16)
    ffn_gate_grad = (grad_out * ffn_value * ffn_gates * (1.0 - ffn_gates)).astype(jnp.bfloat16)
    hidden_grad = project_back(value_grad, matrices[5])
    pre_grad = (hidden_grad * 2.0 * jax.nn.relu(hidden_pre)).astype(jnp.bfloat16)
    if tuned:
        flat_value_grad = value_grad.reshape(-1, width)
        flat_gate_grad = ffn_gate_grad.reshape(-1, width)
        flat_pre_grad = pre_grad.reshape(-1, pre_grad.shape[2])
        other_value_grad, other_gate_grad = sent_together([flat_value_grad, flat_gate_grad])
        (other_pre_grad,) = sent_together([flat_pre_grad])
        ffn_value_part = chip_grad(own_hidden, other_hidden, flat_value_grad, other_value_grad)
        ffn_key_part = chip_grad(own_ffn_key, other_ffn_key, flat_pre_grad, other_pre_grad)
        ffn_gate_part = chip_grad(own_ffn_gate, other_ffn_gate, flat_gate_grad, other_gate_grad)
        value_quad = quarters(ffn_value_part)
        value_corner = send_corner(value_quad)
        key_quad = quarters(
            jnp.concatenate(
                [ffn_key_part[:, :, q : q + 1024] for q in range(0, 4096, 1024)] + [ffn_gate_part],
                axis=1,
            )
        )
        value_from = send_sides(*add_corner(value_quad, *value_corner))
        value_first, value_outgoing = add_sides(value_quad, *value_from)
    else:
        grad_ffn_value = weight_grad(hidden, value_grad)
        grad_ffn_key = weight_grad(ffn_key_in, pre_grad)
        grad_ffn_gate = weight_grad(ffn_gate_in, ffn_gate_grad)
    key_two_grad = project_back(tied(pre_grad, ffn_value_part, key_quad) if tuned else pre_grad, matrices[4])
    gate_two_grad = project_back(ffn_gate_grad, matrices[6])
    spread_two = normed_two - before_two
    grad_ffn_mix_key = jnp.sum(key_two_grad * spread_two, axis=(0, 1))
    grad_ffn_mix_gate = jnp.sum(gate_two_grad * spread_two, axis=(0, 1))
    normed_two_grad = (
        key_two_grad * feature_lookup_mixture + gate_two_grad * feature_receptance_mixture
    )
    before_two_grad = (
        key_two_grad * (1.0 - feature_lookup_mixture)
        + gate_two_grad * (1.0 - feature_receptance_mixture)
    ) * keep_mask
    from_right = shifted(before_two_grad[:, :1, :], "seq", -1)
    normed_two_grad = normed_two_grad + jnp.concatenate(
        [before_two_grad[:, 1:, :], from_right], axis=1
    )
    middle_norm_grad, grad_gain_two, grad_bias_two = norm_backward(
        normed_two_grad, unit_two, inv_two, closing_standardize_scale
    )
    middle_grad = grad_out + middle_norm_grad
    branch_grad = middle_grad.astype(jnp.bfloat16)
    if tuned:
        flat_branch_grad = branch_grad.reshape(-1, width)
        (other_branch_grad,) = sent_together([flat_branch_grad])
        output_part = chip_grad(own_gated, other_gated, flat_branch_grad, other_branch_grad)
        value_got = send_column(value_outgoing)
        key_sides = add_corner(key_quad, *send_corner(key_quad))
    else:
        grad_output = weight_grad(gated, branch_grad)
    gated_grad = project_back(
        tied(branch_grad, *value_outgoing) if tuned else branch_grad, matrices[3]
    )
    gate_pre_grad = (gated_grad * mixed * gates * (1.0 - gates)).astype(jnp.bfloat16)
    blended_gradient = gated_grad * gates
    if tuned:
        blended_gradient = tied(blended_gradient, *key_sides)
    (
        key_gradient,
        value_gradient,
        decay_gradient,
        reward_derivative,
        numerator_gradient,
        denominator_gradient,
    ) = weighted_value_backward(blended_gradient)
    if tuned:
        key_from = send_sides(*key_sides)
        key_first, key_outgoing = add_sides(key_quad, *key_from)
    num_next, den_next = carried_in(
        jnp.stack([numerator_gradient, denominator_gradient]), starts_in, decay_vec, length, True
    )
    num_tail = tail_fade * num_next[:, None, :]
    den_tail = tail_fade * den_next[:, None, :]
    tail_grad = powered_lookups * (value_row_block * num_tail + den_tail)
    key_gradient = key_gradient + tail_grad
    value_gradient = value_gradient + powered_lookups * num_tail
    offsets = (jnp.arange(length).astype(jnp.float32) - (length - 1))[:, None]
    block_fade = clear_flag * jnp.exp(-length * decay_vec)
    decay_gradient = decay_gradient + jnp.sum(offsets * tail_grad, axis=(0, 1))
    decay_gradient = decay_gradient - length * jnp.sum(
        block_fade * (state_numerator * num_next + state_denominator * den_next), axis=0
    )
    key_grad16 = key_gradient.astype(jnp.bfloat16)
    val_grad16 = value_gradient.astype(jnp.bfloat16)
    if tuned:
        flat_grads = [g.reshape(-1, width) for g in (key_grad16, val_grad16, gate_pre_grad)]
        other_grads = sent_together(flat_grads)
        key_part = chip_grad(own_key, other_key, flat_grads[0], other_grads[0])
        value_part = chip_grad(own_value, other_value, flat_grads[1], other_grads[1])
        gate_part = chip_grad(own_gate, other_gate, flat_grads[2], other_grads[2])
        time_quad = quarters(
            jnp.concatenate([key_part, value_part, gate_part, output_part], axis=1)
        )
        key_got = send_column(key_outgoing)
        time_sides = add_corner(time_quad, *send_corner(time_quad))
        time_from = send_sides(*time_sides)
        time_first, time_outgoing = add_sides(time_quad, *time_from)
        time_total = add_all(time_first, send_column(time_outgoing))
        grad_key, grad_value, grad_gate, grad_output = (
            time_total[i : i + 32] for i in (0, 32, 64, 96)
        )
        grad_ffn_value = add_all(value_first, value_got)
        key_total = add_all(key_first, key_got)
        grad_ffn_key = jnp.concatenate([key_total[i : i + 32] for i in (0, 32, 64, 96)], axis=1)
        grad_ffn_gate = key_total[128:]
    else:
        grad_key = weight_grad(key_in, key_grad16)
        grad_value = weight_grad(value_in, val_grad16)
        grad_gate = weight_grad(gate_in, gate_pre_grad)
    key_in_grad = project_back(
        tied(key_grad16, time_quad, *key_outgoing) if tuned else key_grad16, matrices[0]
    )
    value_in_grad = project_back(val_grad16, matrices[1])
    gate_in_grad = project_back(gate_pre_grad, matrices[2])
    spread_one = normed_one - before_one
    grad_mix_key = jnp.sum(key_in_grad * spread_one, axis=(0, 1))
    grad_mix_value = jnp.sum(value_in_grad * spread_one, axis=(0, 1))
    grad_mix_gate = jnp.sum(gate_in_grad * spread_one, axis=(0, 1))
    normed_one_grad = (
        key_in_grad * temporal_lookup_mixture
        + value_in_grad * temporal_content_mixture
        + gate_in_grad * temporal_receptance_mixture
    )
    before_one_grad = (
        key_in_grad * (1.0 - temporal_lookup_mixture)
        + value_in_grad * (1.0 - temporal_content_mixture)
        + gate_in_grad * (1.0 - temporal_receptance_mixture)
    ) * keep_mask
    from_next = shifted(before_one_grad[:, :1, :], "seq", -1)
    normed_one_grad = normed_one_grad + jnp.concatenate(
        [before_one_grad[:, 1:, :], from_next], axis=1
    )
    input_norm_grad, grad_gain_one, grad_bias_one = norm_backward(
        normed_one_grad, unit_one, inv_one, opening_standardize_scale
    )
    input_grad = middle_grad + input_norm_grad
    vector_grads = jnp.stack(
        [
            grad_gain_one,
            grad_bias_one,
            grad_mix_key,
            grad_mix_value,
            grad_mix_gate,
            decay_gradient,
            reward_derivative,
            grad_gain_two,
            grad_bias_two,
            grad_ffn_mix_key,
            grad_ffn_mix_gate,
        ]
    )
    if tuned:
        vector_grads = sum_vectors(vector_grads, flat)
    else:
        vector_grads = lax.psum_scatter(vector_grads, BOTH, scatter_dimension=1, tiled=True)
    return (
        output,
        input_grad,
        vector_grads[0],
        vector_grads[1],
        vector_grads[2],
        vector_grads[3],
        vector_grads[4],
        vector_grads[5],
        vector_grads[6],
        grad_key,
        grad_value,
        grad_gate,
        grad_output,
        vector_grads[7],
        vector_grads[8],
        vector_grads[9],
        vector_grads[10],
        grad_ffn_key,
        grad_ffn_value,
        grad_ffn_gate,
    )


def solution(mesh):
    tuned = tuple(mesh.shape.items()) == (("batch", 4), ("seq", 8))
    return jax.shard_map(
        partial(shards, tuned),
        mesh=mesh,
        in_specs=(
            P("batch", "seq", None),
            P("batch", None),
            P("batch", "seq", None),
            P(("batch", "seq")),
            P(("batch", "seq")),
            P(("batch", "seq")),
            P(("batch", "seq")),
            P(("batch", "seq")),
            P(("batch", "seq")),
            P(("batch", "seq")),
            P(("batch", "seq"), None),
            P(("batch", "seq"), None),
            P(("batch", "seq"), None),
            P(("batch", "seq"), None),
            P(("batch", "seq")),
            P(("batch", "seq")),
            P(("batch", "seq")),
            P(("batch", "seq")),
            P(("batch", "seq"), None),
            P(("batch", "seq"), None),
            P(("batch", "seq"), None),
        ),
        out_specs=(
            P("batch", "seq", None),
            P("batch", "seq", None),
            P(("batch", "seq")),
            P(("batch", "seq")),
            P(("batch", "seq")),
            P(("batch", "seq")),
            P(("batch", "seq")),
            P(("batch", "seq")),
            P(("batch", "seq")),
            P(("batch", "seq"), None),
            P(("batch", "seq"), None),
            P(("batch", "seq"), None),
            P(("batch", "seq"), None),
            P(("batch", "seq")),
            P(("batch", "seq")),
            P(("batch", "seq")),
            P(("batch", "seq")),
            P(("batch", "seq"), None),
            P(("batch", "seq"), None),
            P(("batch", "seq"), None),
        ),
        check_vma=False,
    )
```

time: 1570 us -> 565 us (0.36)
  waiting for transfers between devices: 1160 us -> 186 us
  blocking collectives: 156 us -> 0 us
  starting transfers between devices: 8.67 us -> 82.7 us
  matrix products: 149 us -> 111 us
  local copies, waits for them, and re-layouts: 34.6 us -> 63.7 us
  Pallas kernels: 0 us -> 28.7 us
  other arithmetic: 36.9 us -> 61.2 us
    reduce_scatter x7 -> x0, waiting for transfers between devices: 883 us -> none  [the longest x1 187 us: reduce_channel(): lax.psum_scatter(ffn_value_weight, ('batch', 'seq'), scatter_dimension=0,...]
    all_gather x7 -> x1, waiting for transfers between devices: 275 us -> 13 us  [shards(): lax.all_gather(stacked([feature_lookup_projection, feature_content_projec...]
    ppermute x0 -> x54, waiting for transfers between devices: none -> 173 us  [sent(): return lax.ppermute(array, BOTH, pairs)]
    unnamed x3 -> x0, blocking collectives: 98.8 us -> none
    ppermute x0 -> x54, starting transfers between devices: none -> 75.7 us  [sent(): return lax.ppermute(array, BOTH, pairs)]
    all_gather x4 -> x0, blocking collectives: 56.7 us -> none  [carried_in(): gathered = jax.tree.map(lambda a: lax.all_gather(a, axis), part)]
    pallas_call x0 -> x9, Pallas kernels: none -> 28.7 us  [the longest x8 26.5 us: assemble(): pl.pallas_call(partial(assemble_kernel, counts, start, columns), out_shap...]
    dot_general x7, matrix products: 52.8 us -> 25.5 us  [project(): jnp.einsum('rtd,de->rte', rows_in, weight, preferred_element_type=jnp.flo...]
  transfers between devices with their start and end apart: 18 -> 59, of which waited for: 13 -> 26; matrix products, arithmetic and copies ran while one was open for 13% -> 29% of each run, Pallas kernels for 0% -> 4%
where the time goes in v1:
time: 565 us; the launch traced here: 558 us
  waiting for transfers between devices  186 us (33%)
  matrix products  111 us (20%)
  starting transfers between devices  82.7 us (15%)
  local copies, waits for them, and re-layouts  63.7 us (11%)
  other arithmetic  61.2 us (11%)
  Pallas kernels  28.7 us (5%)
  between operations  24.2 us (4%)
    ppermute x54, waiting for transfers between devices, sent(): return lax.ppermute(array, BOTH, pairs)  173 us
    ppermute x54, starting transfers between devices, sent(): return lax.ppermute(array, BOTH, pairs)  75.7 us
    unnamed x362, local copies, waits for them, and re-layouts  38 us
    dot_general x7, matrix products, project_back(): jnp.einsum('rte,de->rtd', grads, weight, preferred_element_type=jnp.float32)  31 us
    pallas_call x8, Pallas kernels, assemble(): pl.pallas_call(partial(assemble_kernel, counts, start, columns), out_shap...  26.5 us
    dot_general x7, matrix products, project(): jnp.einsum('rtd,de->rte', rows_in, weight, preferred_element_type=jnp.flo...  25.5 us
    dot_general x7, matrix products, chip_grad(): jnp.einsum('td,te->de', other_in, other_grads, preferred_element_type=jnp...  18.5 us
    dot_general x7, matrix products, chip_grad(): jnp.einsum('td,te->de', own_in, grads, preferred_element_type=jnp.float32)  13.5 us
  transfers between devices with their start and end apart: 59, of which 26 were waited for; matrix products, arithmetic and copies ran while one was open for 29% of the time, Pallas kernels for 4%

profile of v1, /device:TPU:0, one launch (start us, length us, event | category | flops | bytes accessed | tf_op | source)
XLA Modules:
  0.0 557.8 jit_solution(2665745187109962406)
XLA Ops:
  16.8 4.1 collective-permute-start.1
  29.7 16.9 %collective-permute-done.1 = bf16[112,1024]{1,0:T(8,128)(2,1)S(1)} collective-permute-done((bf16[112,1024]{1,0:T(8,128)(2,1)S(1)}, bf16[112,1024]{1,0:T(8,128)(2,1)S(1)}, u32[]{:S(2)}, u32[]{:S(2)}) %collective-permute-start.1) | collective-permute-done | bytes 229408 | tf_op jit(solution)/shard_map/ppermute | solution.py:29
  54.6 15.2 %collective-permute-done.4.refs_2_ = bf16[4,112,1024]{2,1,0:T(8,128)(2,1)S(1)} collective-permute-done((bf16[4,112,1024]{2,1,0:T(8,128)(2,1)S(1)}, bf16[4,112,1024]{2,1,0:T(8,128)(2,1)S(1)}, u32[]{:S(2)}, u32[]{:S(2)}) %collective-permute-start.4) | collective-permute-done | bytes 917536 | tf_op jit(solution)/shard_map/ppermute | solution.py:29
  72.1 5.5 collective-permute-done.3.refs_1_
  81.2 11.3 %collective-permute-done.6.refs_4_ = bf16[2,112,1024]{2,1,0:T(8,128)(2,1)S(1)} collective-permute-done((bf16[2,112,1024]{2,1,0:T(8,128)(2,1)}, bf16[2,112,1024]{2,1,0:T(8,128)(2,1)S(1)}, u32[]{:S(2)}, u32[]{:S(2)}) %collective-permute-start.6) | collective-permute-done | bytes 458784 | tf_op jit(solution)/shard_map/ppermute | solution.py:29
  129.0 6.3 %broadcast_multiply_fusion = (f32[2,256,2048]{2,1,0:T(8,128)}, f32[2,256,2048]{2,1,0:T(8,128)}) fusion(f32[256,2048]{1,0:T(8,128)S(1)} %get-tuple-element.185, f32[2,256,1024]{2,1,0:T(8,128)S(1)} %convolution_exponential_fusion, f32[2,256,1024]{2,1,0:T(8,128)S(1)} %get-tuple-element.111, f32[256,2048]{1,0:T(8,128)S(1)} %get-tuple-element.184, ...), kind=kOutput, calls=%fused_computation.122 | convolution fusion | flops 3224633344 | bytes 16844800 | tf_op jit(solution)/shard_map/jvp(rti,rie->rte)/dot_general | solution.py:329
  139.2 14.3 %collective-permute-start.15 = (f32[2,2,1024]{2,1,0:T(2,128)S(1)}, f32[2,2,1024]{2,1,0:T(2,128)S(1)}, u32[]{:S(2)}, u32[]{:S(2)}) collective-permute-start(f32[2,2,1024]{2,1,0:T(2,128)S(1)} %select_add_fusion.1), channel_id=1, source_target_pairs={{0,4},{1,5},{2,6},{3,7},{4,0},{5,1},{6,2},{7,3},{8,12},{9,13},{10,... | collective-permute-start | bytes 49160 | tf_op jit(solution)/shard_map/ppermute | solution.py:29
  158.6 4.1 shard_map.357
  164.0 5.8 %multiply_convert_fusion.3 = (bf16[2,256,1024]{2,1,0:T(8,128)(2,1)S(1)}, f32[2,256,1024]{2,1,0:T(8,128)}, f32[2,256,1024]{2,1,0:T(8,128)}, f32[2,256,1024]{2,1,0:T(8,128)}, f32[2,256,1024]{2,1,0:T(8,128)}) fusion(f32[2,256,1024]{2,1,0:T(8,128)S(1)} %copy-done.33, f32[1024]{0:T(1024)S(1)} %exp.94, f32[2,256,2048]{2,1,0:T(8,128)S(1)} %copy-done.60, ...), kind=kOutput, calls=%fused_computation.120 | convolution fusion | flops 1081606144 | bytes 22042624 | tf_op jit(solution)/shard_map/rtd,de->rte/dot_general | solution.py:294
  169.8 13.0 %all-gather.3.cloned.1.call-done = bf16[10240,1024]{1,0:T(8,128)(2,1)} async-done(((bf16[320,1024]{1,0:T(8,128)(2,1)}), bf16[10240,1024]{1,0:T(8,128)(2,1)}) %all-gather.3.cloned.1.call-update) | async-done | bytes 20971536 | tf_op jit(solution)/shard_map/all_gather | solution.py:406
  182.8 7.0 %copy-done = bf16[10240,1024]{1,0:T(8,128)(2,1)S(1)} copy-done((bf16[10240,1024]{1,0:T(8,128)(2,1)S(1)}, bf16[10240,1024]{1,0:T(8,128)(2,1)}, u32[]{:S(2)}) %copy-start) | copy-done | bytes 20971544
  198.2 7.0 %copy-done.1 = bf16[10240,1024]{1,0:T(8,128)(2,1)S(1)} copy-done((bf16[10240,1024]{1,0:T(8,128)(2,1)S(1)}, bf16[10240,1024]{1,0:T(8,128)(2,1)}, u32[]{:S(2)}) %copy-start.1) | copy-done | bytes 20971544
  210.5 4.7 shard_map.362
  215.2 6.4 %add_convert_fusion.8 = (bf16[2,256,1024]{2,1,0:T(8,128)(2,1)S(1)}, bf16[2,256,1024]{2,1,0:T(8,128)(2,1)S(1)}) fusion(f32[2,255,1024]{2,1,0:T(8,128)} %bitcast.348, f32[2,1,1024]{2,1,0:T(1,128)S(1)} %collective-permute-done.17, f32[1024]{0:T(1024)S(1)} %get-tuple-element.188, f32[1024]{0:T(1024)S(1)} %mul.1216, f32[2,256]{1,0:T(2,128)S(1)} %get-tuple-element.182, ...), kind=kLoop, calls=%fused_computation.115 | loop fusion | flops 7340032 | bytes 6322176 | tf_op jit(solution)/shard_map/convert_element_type | solution.py:541
  221.6 6.8 %multiply_convert_fusion.1 = (bf16[2,256,4096]{2,1,0:T(8,128)(2,1)S(1)}, f32[2,256,4096]{2,1,0:T(8,128)}) fusion(bf16[2,256,1024]{2,1,0:T(8,128)(2,1)S(1)} %get-tuple-element.87, bf16[1024,4096,1]{1,0,2:T(8,128)(2,1)S(1)} %bitcast.339), kind=kOutput, calls=%fused_computation.3 | convolution fusion | flops 4301258752 | bytes 22020096 | tf_op jit(solution)/shard_map/rtd,de->rte/dot_general | solution.py:294
  228.4 4.6 fusion.187
  247.9 11.4 %multiply_convert_fusion = bf16[2,256,4096]{2,1,0:T(8,128)(2,1)} fusion(f32[2,256,4096]{2,1,0:T(8,128)} %get-tuple-element.176, bf16[2,256,1024]{2,1,0:T(8,128)(2,1)S(1)} %copy-done.94, bf16[4096,1024,1]{1,0,2:T(8,128)(2,1)} %bitcast.342), kind=kOutput, calls=%fused_computation.2 | convolution fusion | flops 4303355904 | bytes 22020096 | tf_op jit(solution)/shard_map/rte,de->rtd/dot_general | solution.py:298
  261.9 4.5 add_convert_fusion.1
  271.8 9.3 %collective-permute-done.23 = bf16[2,128,1024]{2,1,0:T(8,128)(2,1)S(1)} collective-permute-done((bf16[2,128,1024]{2,1,0:T(8,128)(2,1)S(1)}, bf16[2,128,1024]{2,1,0:T(8,128)(2,1)S(1)}, u32[]{:S(2)}, u32[]{:S(2)}) %collective-permute-start.23) | collective-permute-done | bytes 524320 | tf_op jit(solution)/shard_map/ppermute | solution.py:29
  291.6 15.7 %collective-permute-done.26 = bf16[4,128,1024]{2,1,0:T(8,128)(2,1)S(1)} collective-permute-done((bf16[4,128,1024]{2,1,0:T(8,128)(2,1)S(1)}, bf16[4,128,1024]{2,1,0:T(8,128)(2,1)S(1)}, u32[]{:S(2)}, u32[]{:S(2)}) %collective-permute-start.26) | collective-permute-done | bytes 1048608 | tf_op jit(solution)/shard_map/ppermute | solution.py:29
  318.5 13.4 %collective-permute-done.56 = bf16[128,1024]{1,0:T(8,128)(2,1)S(1)} collective-permute-done((bf16[128,1024]{1,0:T(8,128)(2,1)S(1)}, bf16[128,1024]{1,0:T(8,128)(2,1)S(1)}, u32[]{:S(2)}, u32[]{:S(2)}) %collective-permute-start.56) | collective-permute-done | bytes 262176 | tf_op jit(solution)/shard_map/ppermute | solution.py:29
  339.5 8.4 %fusion.2 = f32[2,256,1024]{2,1,0:T(8,128)S(1)} fusion(bf16[1024,4096,1]{1,0,2:T(8,128)(2,1)} %bitcast.340, bf16[2,256,4096]{2,1,0:T(8,128)(2,1)} %multiply_convert_fusion, bf16[]{:T(256)S(6)} %add.563), kind=kOutput, calls=%fused_computation.15 | convolution fusion | flops 4297064448 | bytes 14680066 | tf_op jit(solution)/shard_map/rte,de->rtd/dot_general | solution.py:298
  366.6 8.1 %collective-permute-done.35 = bf16[2,160,1024]{2,1,0:T(8,128)(2,1)S(1)} collective-permute-done((bf16[2,160,1024]{2,1,0:T(8,128)(2,1)S(1)}, bf16[2,160,1024]{2,1,0:T(8,128)(2,1)S(1)}, u32[]{:S(2)}, u32[]{:S(2)}) %collective-permute-start.35) | collective-permute-done | bytes 655392 | tf_op jit(solution)/shard_map/ppermute | solution.py:29
  382.3 5.1 multiply_reduce_fusion
  412.6 14.8 %collective-permute-done.34 = bf16[4,160,1024]{2,1,0:T(8,128)(2,1)S(1)} collective-permute-done((bf16[4,160,1024]{2,1,0:T(8,128)(2,1)S(1)}, bf16[4,160,1024]{2,1,0:T(8,128)(2,1)S(1)}, u32[]{:S(2)}, u32[]{:S(2)}) %collective-permute-start.34) | collective-permute-done | bytes 1310752 | tf_op jit(solution)/shard_map/ppermute | solution.py:29
  440.4 19.0 %collective-permute-done.53 = bf16[160,1024]{1,0:T(8,128)(2,1)S(1)} collective-permute-done((bf16[160,1024]{1,0:T(8,128)(2,1)S(1)}, bf16[160,1024]{1,0:T(8,128)(2,1)S(1)}, u32[]{:S(2)}, u32[]{:S(2)}) %collective-permute-start.53) | collective-permute-done | bytes 327712 | tf_op jit(solution)/shard_map/ppermute | solution.py:29
  488.9 3.8 fusion.26
  495.6 14.0 %collective-permute-done.39 = f32[11,1024]{1,0:T(8,128)S(1)} collective-permute-done((f32[11,1024]{1,0:T(8,128)S(1)}, f32[11,1024]{1,0:T(8,128)S(1)}, u32[]{:S(2)}, u32[]{:S(2)}) %collective-permute-start.39) | collective-permute-done | bytes 45088 | tf_op jit(solution)/shard_map/ppermute | solution.py:29
  510.3 4.2 fusion.25
  515.2 6.3 %collective-permute-start.42 = (f32[11,1024]{1,0:T(8,128)S(1)}, f32[11,1024]{1,0:T(8,128)S(1)}, u32[]{:S(2)}, u32[]{:S(2)}) collective-permute-start(f32[11,1024]{1,0:T(8,128)S(1)} %add.613), channel_id=1, source_target_pairs={{0,4},{1,5},{2,6},{3,7},{4,0},{5,1},{6,2},{7,3},{8,12},{9,13},{10,... | collective-permute-start | bytes 135176 | tf_op jit(solution)/shard_map/ppermute | solution.py:29
  530.6 6.7 %collective-permute-done.49 = bf16[128,1024]{1,0:T(8,128)(2,1)S(1)} collective-permute-done((bf16[128,1024]{1,0:T(8,128)(2,1)S(1)}, bf16[128,1024]{1,0:T(8,128)(2,1)S(1)}, u32[]{:S(2)}, u32[]{:S(2)}) %collective-permute-start.49) | collective-permute-done | bytes 262176 | tf_op jit(solution)/shard_map/ppermute | solution.py:29
  538.4 11.3 %collective-permute-done.50 = bf16[128,1024]{1,0:T(8,128)(2,1)S(1)} collective-permute-done((bf16[128,1024]{1,0:T(8,128)(2,1)S(1)}, bf16[128,1024]{1,0:T(8,128)(2,1)S(1)}, u32[]{:S(2)}, u32[]{:S(2)}) %collective-permute-start.50) | collective-permute-done | bytes 262176 | tf_op jit(solution)/shard_map/ppermute | solution.py:29
  (657 shorter events, 244.6 us)
Async XLA Ops:
  7.2 175.6 %all-gather.3.cloned.1.call-start = ((), (), s32[]{:S(2)}) async-start(), calls=%async_computation | async-start | bytes 21626880 | tf_op jit(solution)/shard_map/all_gather | solution.py:406
  16.8 29.7 %collective-permute-start.1 = (bf16[112,1024]{1,0:T(8,128)(2,1)S(1)}, bf16[112,1024]{1,0:T(8,128)(2,1)S(1)}, u32[]{:S(2)}, u32[]{:S(2)}) collective-permute-start(bf16[112,1024]{1,0:T(8,128)(2,1)S(1)} %get-tuple-element.136), channel_id=1, source_target_pairs={{0,4},{1,5},{2,6},{3,7},{4,0},{5,1},{6,2},{7,3},{8,12},{9,13},{10,... | collective-permute-start | bytes 688136 | tf_op jit(solution)/shard_map/ppermute | solution.py:29
  20.9 25.6 %collective-permute-start = (bf16[112,1024]{1,0:T(8,128)(2,1)S(1)}, bf16[112,1024]{1,0:T(8,128)(2,1)S(1)}, u32[]{:S(2)}, u32[]{:S(2)}) collective-permute-start(bf16[112,1024]{1,0:T(8,128)(2,1)S(1)} %get-tuple-element.136), channel_id=1, source_target_pairs={{0,2},{1,3},{2,4},{3,5},{4,6},{5,7},{6,0},{7,1},{8,10},{9,11},{10,... | collective-permute-start | bytes 688136 | tf_op jit(solution)/shard_map/ppermute | solution.py:29
  22.5 24.1 %collective-permute-start.2 = (bf16[112,1024]{1,0:T(8,128)(2,1)S(1)}, bf16[112,1024]{1,0:T(8,128)(2,1)S(1)}, u32[]{:S(2)}, u32[]{:S(2)}) collective-permute-start(bf16[112,1024]{1,0:T(8,128)(2,1)S(1)} %get-tuple-element.136), channel_id=1, source_target_pairs={{0,6},{1,7},{2,0},{3,1},{4,2},{5,3},{6,4},{7,5},{8,14},{9,15},{10,... | collective-permute-start | bytes 688136 | tf_op jit(solution)/shard_map/ppermute | solution.py:29
  24.7 54.7 %collective-permute-start.12 = (bf16[2,1,1024]{2,1,0:T(2,128)(2,1)S(1)}, bf16[2,1,1024]{2,1,0:T(2,128)(2,1)S(1)}, u32[]{:S(2)}, u32[]{:S(2)}) collective-permute-start(bf16[2,1,1024]{2,1,0:T(2,128)(2,1)S(1)} %slice.403), channel_id=1, source_target_pairs={{0,1},{1,2},{2,3},{3,4},{4,5},{5,6},{6,7},{8,9},{9,10},{10,11},{11... | collective-permute-start | bytes 12296 | tf_op jit(solution)/shard_map/ppermute | solution.py:236
  46.7 23.1 %collective-permute-start.4 = (bf16[4,112,1024]{2,1,0:T(8,128)(2,1)S(1)}, bf16[4,112,1024]{2,1,0:T(8,128)(2,1)S(1)}, u32[]{:S(2)}, u32[]{:S(2)}) collective-permute-start(bf16[4,112,1024]{2,1,0:T(8,128)(2,1)S(1)} %pad_maximum_fusion.15.refs_0_), channel_id=1, source_target_pairs={{0,16},{1,17},{2,18},{3,19},{4,20},{5,21},{6,22},{7,23},{8,24},{9,... | collective-permute-start | bytes 2752520 | tf_op jit(solution)/shard_map/ppermute | solution.py:29
  49.5 28.1 %collective-permute-start.3 = (bf16[4,112,1024]{2,1,0:T(8,128)(2,1)S(1)}, bf16[4,112,1024]{2,1,0:T(8,128)(2,1)S(1)}, u32[]{:S(2)}, u32[]{:S(2)}) collective-permute-start(bf16[4,112,1024]{2,1,0:T(8,128)(2,1)S(1)} %pad_maximum_fusion.15.refs_0_), channel_id=1, source_target_pairs={{0,8},{1,9},{2,10},{3,11},{4,12},{5,13},{6,14},{7,15},{8,0},{9,1},... | collective-permute-start | bytes 2752520 | tf_op jit(solution)/shard_map/ppermute | solution.py:29
  70.6 21.8 %collective-permute-start.6 = (bf16[2,112,1024]{2,1,0:T(8,128)(2,1)}, bf16[2,112,1024]{2,1,0:T(8,128)(2,1)S(1)}, u32[]{:S(2)}, u32[]{:S(2)}) collective-permute-start(bf16[2,112,1024]{2,1,0:T(8,128)(2,1)} %slice.523), channel_id=1, source_target_pairs={{0,8},{1,9},{2,10},{3,11},{4,12},{5,13},{6,14},{7,15},{8,0},{9,1},... | collective-permute-start | bytes 1376264 | tf_op jit(solution)/shard_map/ppermute | solution.py:29
  79.0 15.9 %collective-permute-start.9 = (bf16[4,112,1024]{2,1,0:T(8,128)(2,1)S(1)}, bf16[4,112,1024]{2,1,0:T(8,128)(2,1)}, u32[]{:S(2)}, u32[]{:S(2)}) collective-permute-start(bf16[4,112,1024]{2,1,0:T(8,128)(2,1)S(1)} %collective-permute-done.4.refs_2_), channel_id=1, source_target_pairs={{0,1},{1,0},{2,3},{3,2},{4,5},{5,4},{6,7},{7,6},{8,9},{9,8},{10,11... | collective-permute-start | bytes 2752520 | tf_op jit(solution)/shard_map/ppermute | solution.py:29
  135.4 27.3 %collective-permute-start.16 = (f32[2,2,1024]{2,1,0:T(2,128)S(1)}, f32[2,2,1024]{2,1,0:T(2,128)S(1)}, u32[]{:S(2)}, u32[]{:S(2)}) collective-permute-start(f32[2,2,1024]{2,1,0:T(2,128)S(1)} %select_add_fusion.1), channel_id=1, source_target_pairs={{0,6},{1,7},{2,0},{3,1},{4,2},{5,3},{6,4},{7,5},{8,14},{9,15},{10,... | collective-permute-start | bytes 49160 | tf_op jit(solution)/shard_map/ppermute | solution.py:29
  139.2 23.5 %collective-permute-start.15 = (f32[2,2,1024]{2,1,0:T(2,128)S(1)}, f32[2,2,1024]{2,1,0:T(2,128)S(1)}, u32[]{:S(2)}, u32[]{:S(2)}) collective-permute-start(f32[2,2,1024]{2,1,0:T(2,128)S(1)} %select_add_fusion.1), channel_id=1, source_target_pairs={{0,4},{1,5},{2,6},{3,7},{4,0},{5,1},{6,2},{7,3},{8,12},{9,13},{10,... | collective-permute-start | bytes 49160 | tf_op jit(solution)/shard_map/ppermute | solution.py:29
  195.6 19.5 %collective-permute-start.17 = (f32[2,1,1024]{2,1,0:T(1,128)S(1)}, f32[2,1,1024]{2,1,0:T(1,128)S(1)}, u32[]{:S(2)}, u32[]{:S(2)}) collective-permute-start(f32[2,1,1024]{2,1,0:T(1,128)S(1)} %slice.540), channel_id=1, source_target_pairs={{0,1},{1,2},{2,3},{3,4},{4,5},{5,6},{6,7},{8,9},{9,10},{10,11},{11... | collective-permute-start | bytes 24584 | tf_op jit(solution)/shard_map/ppermute | solution.py:236
  237.7 24.2 %collective-permute-start.19 = (bf16[512,2048]{1,0:T(8,128)(2,1)}, bf16[512,2048]{1,0:T(8,128)(2,1)}, u32[]{:S(2)}, u32[]{:S(2)}) collective-permute-start(bf16[512,2048]{1,0:T(8,128)(2,1)} %pad_maximum_fusion.6), channel_id=1, source_target_pairs={{0,1},{1,0},{2,3},{3,2},{4,5},{5,4},{6,7},{7,6},{8,9},{9,8},{10,11... | collective-permute-start | bytes 6291464 | tf_op jit(solution)/shard_map/ppermute | solution.py:29
  242.5 19.5 %collective-permute-start.18 = (bf16[512,2048]{1,0:T(8,128)(2,1)}, bf16[512,2048]{1,0:T(8,128)(2,1)}, u32[]{:S(2)}, u32[]{:S(2)}) collective-permute-start(bf16[512,2048]{1,0:T(8,128)(2,1)} %slice.544), channel_id=1, source_target_pairs={{0,1},{1,0},{2,3},{3,2},{4,5},{5,4},{6,7},{7,6},{8,9},{9,8},{10,11... | collective-permute-start | bytes 6291464 | tf_op jit(solution)/shard_map/ppermute | solution.py:29
  259.4 73.4 %collective-permute-start.21 = (bf16[512,4096]{1,0:T(8,128)(2,1)}, bf16[512,4096]{1,0:T(8,128)(2,1)S(1)}, u32[]{:S(2)}, u32[]{:S(2)}) collective-permute-start(bf16[512,4096]{1,0:T(8,128)(2,1)} %bitcast.374), channel_id=1, source_target_pairs={{0,1},{1,0},{2,3},{3,2},{4,5},{5,4},{6,7},{7,6},{8,9},{9,8},{10,11... | collective-permute-start | bytes 12582920 | tf_op jit(solution)/shard_map/ppermute | solution.py:29
  270.5 140.0 %collective-permute-start.32 = (bf16[512,2048]{1,0:T(8,128)(2,1)}, bf16[512,2048]{1,0:T(8,128)(2,1)}, u32[]{:S(2)}, u32[]{:S(2)}) collective-permute-start(bf16[512,2048]{1,0:T(8,128)(2,1)} %pad_maximum_fusion.7), channel_id=1, source_target_pairs={{0,1},{1,0},{2,3},{3,2},{4,5},{5,4},{6,7},{7,6},{8,9},{9,8},{10,11... | collective-permute-start | bytes 6291464 | tf_op jit(solution)/shard_map/ppermute | solution.py:29
  282.8 24.5 %collective-permute-start.26 = (bf16[4,128,1024]{2,1,0:T(8,128)(2,1)S(1)}, bf16[4,128,1024]{2,1,0:T(8,128)(2,1)S(1)}, u32[]{:S(2)}, u32[]{:S(2)}) collective-permute-start(bf16[4,128,1024]{2,1,0:T(8,128)(2,1)S(1)} %pad_maximum_fusion.12), channel_id=1, source_target_pairs={{0,8},{1,9},{2,10},{3,11},{4,12},{5,13},{6,14},{7,15},{8,0},{9,1},... | collective-permute-start | bytes 3145736 | tf_op jit(solution)/shard_map/ppermute | solution.py:29
  283.5 24.2 %collective-permute-start.24 = (bf16[4,128,1024]{2,1,0:T(8,128)(2,1)S(1)}, bf16[4,128,1024]{2,1,0:T(8,128)(2,1)S(1)}, u32[]{:S(2)}, u32[]{:S(2)}) collective-permute-start(bf16[4,128,1024]{2,1,0:T(8,128)(2,1)S(1)} %pad_maximum_fusion.11), channel_id=1, source_target_pairs={{0,16},{1,17},{2,18},{3,19},{4,20},{5,21},{6,22},{7,23},{8,24},{9,... | collective-permute-start | bytes 3145736 | tf_op jit(solution)/shard_map/ppermute | solution.py:29
  286.6 24.6 %collective-permute-start.20 = (bf16[512,1024]{1,0:T(8,128)(2,1)S(1)}, bf16[512,1024]{1,0:T(8,128)(2,1)S(1)}, u32[]{:S(2)}, u32[]{:S(2)}) collective-permute-start(bf16[512,1024]{1,0:T(8,128)(2,1)S(1)} %pad_maximum_fusion.10), channel_id=1, source_target_pairs={{0,1},{1,0},{2,3},{3,2},{4,5},{5,4},{6,7},{7,6},{8,9},{9,8},{10,11... | collective-permute-start | bytes 3145736 | tf_op jit(solution)/shard_map/ppermute | solution.py:29
  310.2 21.7 %collective-permute-start.56 = (bf16[128,1024]{1,0:T(8,128)(2,1)S(1)}, bf16[128,1024]{1,0:T(8,128)(2,1)S(1)}, u32[]{:S(2)}, u32[]{:S(2)}) collective-permute-start(bf16[128,1024]{1,0:T(8,128)(2,1)S(1)} %get-tuple-element.123), channel_id=1, source_target_pairs={{0,4},{1,5},{2,6},{3,7},{4,0},{5,1},{6,2},{7,3},{8,12},{9,13},{10,... | collective-permute-start | bytes 786440 | tf_op jit(solution)/shard_map/ppermute | solution.py:29
  311.2 20.7 %collective-permute-start.55 = (bf16[128,1024]{1,0:T(8,128)(2,1)S(1)}, bf16[128,1024]{1,0:T(8,128)(2,1)S(1)}, u32[]{:S(2)}, u32[]{:S(2)}) collective-permute-start(bf16[128,1024]{1,0:T(8,128)(2,1)S(1)} %get-tuple-element.124), channel_id=1, source_target_pairs={{0,2},{1,3},{2,4},{3,5},{4,6},{5,7},{6,0},{7,1},{8,10},{9,11},{10,... | collective-permute-start | bytes 786440 | tf_op jit(solution)/shard_map/ppermute | solution.py:29
  357.2 17.5 %collective-permute-start.35 = (bf16[2,160,1024]{2,1,0:T(8,128)(2,1)S(1)}, bf16[2,160,1024]{2,1,0:T(8,128)(2,1)S(1)}, u32[]{:S(2)}, u32[]{:S(2)}) collective-permute-start(bf16[2,160,1024]{2,1,0:T(8,128)(2,1)S(1)} %get-tuple-element.82), channel_id=1, source_target_pairs={{0,16},{1,17},{2,18},{3,19},{4,20},{5,21},{6,22},{7,23},{8,24},{9,... | collective-permute-start | bytes 1966088 | tf_op jit(solution)/shard_map/ppermute | solution.py:29
  358.7 17.5 %collective-permute-start.27 = (bf16[2,160,1024]{2,1,0:T(8,128)(2,1)S(1)}, bf16[2,160,1024]{2,1,0:T(8,128)(2,1)S(1)}, u32[]{:S(2)}, u32[]{:S(2)}) collective-permute-start(bf16[2,160,1024]{2,1,0:T(8,128)(2,1)S(1)} %get-tuple-element.84), channel_id=1, source_target_pairs={{0,8},{1,9},{2,10},{3,11},{4,12},{5,13},{6,14},{7,15},{8,0},{9,1},... | collective-permute-start | bytes 1966088 | tf_op jit(solution)/shard_map/ppermute | solution.py:29
  362.9 47.5 %collective-permute-start.44 = (bf16[512,1024]{1,0:T(8,128)(2,1)}, bf16[512,1024]{1,0:T(8,128)(2,1)}, u32[]{:S(2)}, u32[]{:S(2)}) collective-permute-start(bf16[512,1024]{1,0:T(8,128)(2,1)} %bitcast.150), channel_id=1, source_target_pairs={{0,1},{1,0},{2,3},{3,2},{4,5},{5,4},{6,7},{7,6},{8,9},{9,8},{10,11... | collective-permute-start | bytes 3145736 | tf_op jit(solution)/shard_map/ppermute | solution.py:29
  397.2 30.2 %collective-permute-start.34 = (bf16[4,160,1024]{2,1,0:T(8,128)(2,1)S(1)}, bf16[4,160,1024]{2,1,0:T(8,128)(2,1)S(1)}, u32[]{:S(2)}, u32[]{:S(2)}) collective-permute-start(bf16[4,160,1024]{2,1,0:T(8,128)(2,1)S(1)} %pad_maximum_fusion.8), channel_id=1, source_target_pairs={{0,16},{1,17},{2,18},{3,19},{4,20},{5,21},{6,22},{7,23},{8,24},{9,... | collective-permute-start | bytes 3932168 | tf_op jit(solution)/shard_map/ppermute | solution.py:29
  397.8 30.0 %collective-permute-start.36 = (bf16[4,160,1024]{2,1,0:T(8,128)(2,1)S(1)}, bf16[4,160,1024]{2,1,0:T(8,128)(2,1)S(1)}, u32[]{:S(2)}, u32[]{:S(2)}) collective-permute-start(bf16[4,160,1024]{2,1,0:T(8,128)(2,1)S(1)} %pad_maximum_fusion.9), channel_id=1, source_target_pairs={{0,8},{1,9},{2,10},{3,11},{4,12},{5,13},{6,14},{7,15},{8,0},{9,1},... | collective-permute-start | bytes 3932168 | tf_op jit(solution)/shard_map/ppermute | solution.py:29
  402.4 58.7 %collective-permute-start.33 = (bf16[512,3072]{1,0:T(8,128)(2,1)S(1)}, bf16[512,3072]{1,0:T(8,128)(2,1)S(1)}, u32[]{:S(2)}, u32[]{:S(2)}) collective-permute-start(bf16[512,3072]{1,0:T(8,128)(2,1)S(1)} %pad_maximum_fusion.3), channel_id=1, source_target_pairs={{0,1},{1,0},{2,3},{3,2},{4,5},{5,4},{6,7},{7,6},{8,9},{9,8},{10,11... | collective-permute-start | bytes 9437192 | tf_op jit(solution)/shard_map/ppermute | solution.py:29
  432.1 27.2 %collective-permute-start.53 = (bf16[160,1024]{1,0:T(8,128)(2,1)S(1)}, bf16[160,1024]{1,0:T(8,128)(2,1)S(1)}, u32[]{:S(2)}, u32[]{:S(2)}) collective-permute-start(bf16[160,1024]{1,0:T(8,128)(2,1)S(1)} %get-tuple-element.117), channel_id=1, source_target_pairs={{0,4},{1,5},{2,6},{3,7},{4,0},{5,1},{6,2},{7,3},{8,12},{9,13},{10,... | collective-permute-start | bytes 983048 | tf_op jit(solution)/shard_map/ppermute | solution.py:29
  432.6 26.8 %collective-permute-start.52 = (bf16[160,1024]{1,0:T(8,128)(2,1)S(1)}, bf16[160,1024]{1,0:T(8,128)(2,1)S(1)}, u32[]{:S(2)}, u32[]{:S(2)}) collective-permute-start(bf16[160,1024]{1,0:T(8,128)(2,1)S(1)} %get-tuple-element.118), channel_id=1, source_target_pairs={{0,2},{1,3},{2,4},{3,5},{4,6},{5,7},{6,0},{7,1},{8,10},{9,11},{10,... | collective-permute-start | bytes 983048 | tf_op jit(solution)/shard_map/ppermute | solution.py:29
  485.7 37.7 %collective-permute-start.48 = (bf16[4,128,1024]{2,1,0:T(8,128)(2,1)}, bf16[4,128,1024]{2,1,0:T(8,128)(2,1)}, u32[]{:S(2)}, u32[]{:S(2)}) collective-permute-start(bf16[4,128,1024]{2,1,0:T(8,128)(2,1)} %pad_maximum_fusion.14), channel_id=1, source_target_pairs={{0,8},{1,9},{2,10},{3,11},{4,12},{5,13},{6,14},{7,15},{8,0},{9,1},... | collective-permute-start | bytes 3145736 | tf_op jit(solution)/shard_map/ppermute | solution.py:29
  488.2 35.2 %collective-permute-start.46 = (bf16[4,128,1024]{2,1,0:T(8,128)(2,1)}, bf16[4,128,1024]{2,1,0:T(8,128)(2,1)}, u32[]{:S(2)}, u32[]{:S(2)}) collective-permute-start(bf16[4,128,1024]{2,1,0:T(8,128)(2,1)} %pad_maximum_fusion.13), channel_id=1, source_target_pairs={{0,16},{1,17},{2,18},{3,19},{4,20},{5,21},{6,22},{7,23},{8,24},{9,... | collective-permute-start | bytes 3145736 | tf_op jit(solution)/shard_map/ppermute | solution.py:29
  529.9 19.8 %collective-permute-start.50 = (bf16[128,1024]{1,0:T(8,128)(2,1)S(1)}, bf16[128,1024]{1,0:T(8,128)(2,1)S(1)}, u32[]{:S(2)}, u32[]{:S(2)}) collective-permute-start(bf16[128,1024]{1,0:T(8,128)(2,1)S(1)} %get-tuple-element.121), channel_id=1, source_target_pairs={{0,4},{1,5},{2,6},{3,7},{4,0},{5,1},{6,2},{7,3},{8,12},{9,13},{10,... | collective-permute-start | bytes 786440 | tf_op jit(solution)/shard_map/ppermute | solution.py:29
  (206 other events, 1656.4 us)
Sparse Core Ops, SparseCore 0:
  14.4 168.3 all-gather.2

commit v2 on v1

--- a/solution.py
+++ b/solution.py
@@ -40,6 +40,10 @@
         first = other[(0,) * other.ndim].astype(jnp.float32)
         zero = zero + jnp.minimum(jnp.abs(first), 0.0)
     return array + zero.astype(array.dtype)
+
+
+def all_tied(arrays, after):
+    return [tied(array, after) for array in arrays]
 
 
 def assemble_kernel(owners, start, columns, slots_ref, *refs):
@@ -71,7 +75,7 @@
         partial(assemble_kernel, counts, start, columns),
         out_shape=jax.ShapeDtypeStruct(shape, pieces[0].dtype),
         in_specs=[pl.BlockSpec(memory_space=pltpu.SMEM)]
-        + [pl.BlockSpec(memory_space=pl.ANY)] * len(pieces),
+        + [pl.BlockSpec(memory_space=pltpu.HBM)] * len(pieces),
         out_specs=pl.BlockSpec(memory_space=pltpu.VMEM),
         scratch_shapes=[pltpu.SemaphoreType.DMA((32, columns))],
         compiler_params=pltpu.CompilerParams(vmem_limit_bytes=24 * 1024 * 1024),
@@ -108,11 +112,6 @@
     return pieces + [sent(piece, FLIP_C) for piece in pieces]
 
 
-def vectors_of(blocks):
-    rows = blocks[:, 0, : 11 * 32].reshape(32, 11, 32).astype(jnp.float32)
-    return jnp.swapaxes(rows, 0, 1).reshape(11, 1024)
-
-
 def choice(flat, width):
     index = jnp.arange(width)
     block, within = index // (width // 32), index % (width // 32)
@@ -122,55 +121,341 @@
     return (jnp.arange(width)[:, None] == wanted[None, :]).astype(jnp.bfloat16)
 
 
-def owner_order(flat):
-    block = jnp.arange(32)
-    dc, rest = block >> 4, block & 15
-    dy, dx, dz = rest >> 3, (rest >> 2) & 1, rest & 3
-    return place_of(flat, dy, dx, dz, dc).astype(jnp.int32)
-
-
-def pick_kernel(order_ref, rows_ref, out_ref, sems):
-    copies = [
-        pltpu.make_async_copy(
-            rows_ref.at[:, pl.ds(pl.multiple_of(order_ref[j] * 128, 128), 128)],
-            out_ref.at[:, pl.ds(j * 128, 128)],
-            sems.at[j],
-        )
-        for j in range(32)
-    ]
-    for copy in copies:
-        copy.start()
-    for copy in copies:
-        copy.wait()
-
-
-def pick(rows_in, order):
+def dot_nt(left, right):
+    return lax.dot_general(
+        left, right, (((1,), (1,)), ((), ())), preferred_element_type=jnp.float32
+    )
+
+
+def channel_kernel(slots_ref, *refs):
+    key_in_ref, gate_in_ref, middle_ref, grad_ref, late_ref = refs[:5]
+    refs = refs[5:]
+    out_ref, value_grad_ref, gate_grad_ref, key_back_ref, gate_back_ref = refs[:5]
+    hidden_ref, far_hidden_ref, pre_grad_ref, key_w, value_w, gate_w = refs[5:11]
+    relu_s, hidden_s, pre_s, total_s, in_sems, hidden_sems, pre_sems = refs[11:]
+
+    def key_copy(q):
+        return pltpu.make_async_copy(
+            late_ref.at[:, pl.ds(q * 32, 32), :], key_w.at[q], in_sems.at[q]
+        )
+
+    def value_copy(q):
+        return pltpu.make_async_copy(
+            late_ref.at[pl.ds(q * 8, 8), pl.ds(128, 128), :],
+            value_w.at[pl.ds(q * 8, 8)],
+            in_sems.at[4 + q],
+        )
+
+    gate_copy = pltpu.make_async_copy(
+        late_ref.at[:, pl.ds(256, 32), :], gate_w, in_sems.at[8]
+    )
+    for q in range(4):
+        key_copy(q).start()
+        value_copy(q).start()
+    gate_copy.start()
+
+    def hidden_copy(q, k, target):
+        return pltpu.make_async_copy(
+            hidden_s.at[q, :, pl.ds(k * 128, 128)], target, hidden_sems.at[q, k]
+        )
+
+    def hidden_start(q, k):
+        slot = slots_ref[q * 8 + k]
+        columns = pl.ds(pl.multiple_of((slot & 3) * 128, 128), 128)
+
+        @pl.when(slot < 16)
+        def _():
+            hidden_copy(q, k, hidden_ref.at[slot >> 2, :, columns]).start()
+
+        @pl.when(slot >= 16)
+        def _():
+            hidden_copy(q, k, far_hidden_ref.at[(slot >> 2) - 4, :, columns]).start()
+
+    def pre_copy(q):
+        return pltpu.make_async_copy(
+            pre_s.at[q], pre_grad_ref.at[:, pl.ds(pl.multiple_of(q * 1024, 1024), 1024)], pre_sems.at[q]
+        )
+
+    def forward(q, _):
+        key_copy(q).wait()
+        for half in range(2):
+            rows = pl.ds(half * 256, 256)
+            relu_s[q, rows, :] = jnp.maximum(
+                jnp.dot(
+                    key_in_ref[rows, :],
+                    key_w[q].reshape(1024, 1024),
+                    preferred_element_type=jnp.float32,
+                ),
+                0.0,
+            )
+            hidden_s[q, rows, :] = (relu_s[q, rows, :] * relu_s[q, rows, :]).astype(jnp.bfloat16)
+        for k in range(8):
+            hidden_start(q, k)
+        value_copy(q).wait()
+        for half in range(2):
+            rows = pl.ds(half * 256, 256)
+            more = jnp.dot(
+                hidden_s[q, rows, :],
+                value_w[pl.ds(q * 8, 8)].reshape(1024, 1024),
+                preferred_element_type=jnp.float32,
+            )
+
+            @pl.when(q == 0)
+            def _():
+                total_s[rows, :] = more
+
+            @pl.when(q > 0)
+            def _():
+                total_s[rows, :] += more
+
+        return 0
+
+    lax.fori_loop(0, 4, forward, 0)
+    gate_copy.wait()
+    for half in range(2):
+        rows = pl.ds(half * 256, 256)
+        gates = jax.nn.sigmoid(
+            jnp.dot(
+                gate_in_ref[rows, :],
+                gate_w[...].reshape(1024, 1024),
+                preferred_element_type=jnp.float32,
+            )
+        )
+        value = total_s[rows, :]
+        grads = grad_ref[rows, :].astype(jnp.float32)
+        out_ref[rows, :] = (middle_ref[rows, :] + gates * value).astype(jnp.bfloat16)
+        value_grad_ref[rows, :] = (grads * gates).astype(jnp.bfloat16)
+        gate_grad_ref[rows, :] = (grads * value * gates * (1.0 - gates)).astype(jnp.bfloat16)
+
+    def backward(q, _):
+        for half in range(2):
+            rows = pl.ds(half * 256, 256)
+            pre_s[q, rows, :] = (
+                dot_nt(value_grad_ref[rows, :], value_w[pl.ds(q * 8, 8)].reshape(1024, 1024))
+                * 2.0
+                * relu_s[q, rows, :]
+            ).astype(jnp.bfloat16)
+        pre_copy(q).start()
+        for half in range(2):
+            rows = pl.ds(half * 256, 256)
+            more = dot_nt(pre_s[q, rows, :], key_w[q].reshape(1024, 1024))
+
+            @pl.when(q == 0)
+            def _():
+                key_back_ref[rows, :] = more
+
+            @pl.when(q > 0)
+            def _():
+                key_back_ref[rows, :] += more
+
+        return 0
+
+    lax.fori_loop(0, 4, backward, 0)
+    for half in range(2):
+        rows = pl.ds(half * 256, 256)
+        gate_back_ref[rows, :] = dot_nt(gate_grad_ref[rows, :], gate_w[...].reshape(1024, 1024))
+    for q in range(4):
+        for k in range(8):
+            hidden_copy(q, k, hidden_ref.at[0, :, pl.ds(0, 128)]).wait()
+        pre_copy(q).wait()
+
+
+def channel_mix(slots, key_in, gate_in, middle, grads, late):
+    tokens = key_in.shape[0]
+    wide_rows = jax.ShapeDtypeStruct((tokens, 1024), jnp.float32)
+    half_rows = jax.ShapeDtypeStruct((tokens, 1024), jnp.bfloat16)
+    whole = pl.BlockSpec(memory_space=pltpu.VMEM)
+    far = pl.BlockSpec(memory_space=pltpu.HBM)
     return pl.pallas_call(
-        pick_kernel,
-        out_shape=jax.ShapeDtypeStruct(rows_in.shape, rows_in.dtype),
-        in_specs=[pl.BlockSpec(memory_space=pltpu.SMEM), pl.BlockSpec(memory_space=pl.ANY)],
-        out_specs=pl.BlockSpec(memory_space=pltpu.VMEM),
-        scratch_shapes=[pltpu.SemaphoreType.DMA((32,))],
-        compiler_params=pltpu.CompilerParams(vmem_limit_bytes=24 * 1024 * 1024),
-    )(order, rows_in)
-
-
-def chip_grad(own_in, other_in, grads, other_grads):
-    total = jnp.einsum(
-        "td,te->de", own_in, grads, preferred_element_type=jnp.float32
-    ) + jnp.einsum("td,te->de", other_in, other_grads, preferred_element_type=jnp.float32)
-    return total.astype(jnp.bfloat16).reshape(16, own_in.shape[1] // 16, grads.shape[1])
+        channel_kernel,
+        out_shape=(
+            half_rows,
+            half_rows,
+            half_rows,
+            wide_rows,
+            wide_rows,
+            jax.ShapeDtypeStruct((4, tokens, 512), jnp.bfloat16),
+            jax.ShapeDtypeStruct((4, tokens, 512), jnp.bfloat16),
+            jax.ShapeDtypeStruct((tokens, 4096), jnp.bfloat16),
+        ),
+        in_specs=[pl.BlockSpec(memory_space=pltpu.SMEM), whole, whole, whole, whole, far],
+        out_specs=(whole,) * 5 + (far,) * 3,
+        scratch_shapes=[
+            pltpu.VMEM((4, 32, 32, 1024), jnp.bfloat16),
+            pltpu.VMEM((32, 128, 1024), jnp.bfloat16),
+            pltpu.VMEM((32, 32, 1024), jnp.bfloat16),
+            pltpu.VMEM((4, tokens, 1024), jnp.float32),
+            pltpu.VMEM((4, tokens, 1024), jnp.bfloat16),
+            pltpu.VMEM((4, tokens, 1024), jnp.bfloat16),
+            pltpu.VMEM((tokens, 1024), jnp.float32),
+            pltpu.SemaphoreType.DMA((9,)),
+            pltpu.SemaphoreType.DMA((4, 8)),
+            pltpu.SemaphoreType.DMA((4,)),
+        ],
+        compiler_params=pltpu.CompilerParams(vmem_limit_bytes=54 * 1024 * 1024),
+        cost_estimate=pl.CostEstimate(
+            flops=2 * tokens * 1024 * 1024 * 18, transcendentals=0, bytes_accessed=40 * 1024 * 1024
+        ),
+    )(slots, key_in, gate_in, middle, grads, late)
+
+
+def owner_slots(flat):
+    other = jnp.arange(32)
+    apart = other ^ flat
+    dz = ((other >> 1) - (flat >> 1)) & 3
+    return ((apart & 1) * 16 + ((apart >> 4) & 1) * 8 + ((apart >> 3) & 1) * 4 + dz).astype(jnp.int32)
+
+
+def dot_tn(left, right):
+    return lax.dot_general(
+        left, right, (((0,), (0,)), ((), ())), preferred_element_type=jnp.float32
+    )
+
+
+def chip_rows(own_in, own_grads, other_in, other_grads):
+    return (dot_tn(own_in, own_grads) + dot_tn(other_in, other_grads)).astype(jnp.bfloat16)
+
+
+def value_part_kernel(own_ref, other_ref, grad_ref, other_grad_ref, near, side_x, side_y, far_a, far_b):
+    quarter = pl.program_id(0)
+    part = chip_rows(own_ref[0], grad_ref[...], other_ref[0], other_grad_ref[...])
+    part = part.reshape((4, part.shape[0] // 4, 1024))
+
+    @pl.when(quarter == 0)
+    def _():
+        near[...] = part
+
+    @pl.when(quarter == 1)
+    def _():
+        side_x[...] = part
+
+    @pl.when(quarter == 2)
+    def _():
+        side_y[...] = part
+
+    @pl.when(quarter == 3)
+    def _():
+        far_a[...] = part[:2]
+        far_b[...] = part[2:]
+
+
+def store_quarters(part, outs):
+    near, side_x, side_y, far_a, far_b = outs
+    quarters = part.reshape(4, 4, 32, 1024)
+    near[...] = quarters[0]
+    side_x[...] = quarters[1]
+    side_y[...] = quarters[2]
+    far_a[...] = quarters[3, :2]
+    far_b[...] = quarters[3, 2:]
+
+
+def key_part_kernel(key_ref, other_key_ref, gate_ref, other_gate_ref, *refs):
+    pre_ref, other_pre_ref, gate_grad_ref, other_gate_grad_ref = refs[:4]
+    step = pl.program_id(0)
+
+    @pl.when(step < 4)
+    def _():
+        store_quarters(
+            chip_rows(key_ref[...], pre_ref[...], other_key_ref[...], other_pre_ref[...]), refs[4:]
+        )
+
+    @pl.when(step == 4)
+    def _():
+        store_quarters(
+            chip_rows(
+                gate_ref[...], gate_grad_ref[...], other_gate_ref[...], other_gate_grad_ref[...]
+            ),
+            refs[4:],
+        )
+
+
+def time_part_kernel(own_ref, other_ref, grad_ref, other_grad_ref, *refs):
+    branch_ref, other_branch_ref = refs[:2]
+    step = pl.program_id(0)
+
+    @pl.when(step < 3)
+    def _():
+        store_quarters(
+            chip_rows(own_ref[...], grad_ref[...], other_ref[...], other_grad_ref[...]), refs[2:]
+        )
+
+    @pl.when(step == 3)
+    def _():
+        store_quarters(
+            chip_rows(own_ref[...], branch_ref[...], other_ref[...], other_branch_ref[...]), refs[2:]
+        )
+
+
+def quarters_call(kernel, steps, rows, in_specs, by_quarter, arguments):
+    if by_quarter:
+        outs = [pl.BlockSpec((n, rows, 1024), lambda i: (0, 0, 0)) for n in (4, 4, 4, 2, 2)]
+    else:
+        outs = [pl.BlockSpec((n, 32, 1024), lambda i: (0, i, 0)) for n in (4, 4, 4, 2, 2)]
+    return pl.pallas_call(
+        kernel,
+        grid=(steps,),
+        out_shape=tuple(
+            jax.ShapeDtypeStruct((n, rows, 1024), jnp.bfloat16) for n in (4, 4, 4, 2, 2)
+        ),
+        in_specs=in_specs,
+        out_specs=tuple(outs),
+        compiler_params=pltpu.CompilerParams(vmem_limit_bytes=48 * 1024 * 1024),
+        cost_estimate=pl.CostEstimate(
+            flops=2 * 1024 * 16 * rows * 1024,
+            transcendentals=0,
+            bytes_accessed=(16 * rows + 8 * 1024) * 2048,
+        ),
+    )(*arguments)
+
+
+def value_part(own_hidden, other_hidden, grads, other_grads):
+    tokens = grads.shape[0]
+    whole = pl.BlockSpec((tokens, 1024), lambda i: (0, 0))
+    block = pl.BlockSpec((1, tokens, 512), lambda i: (i, 0, 0))
+    return quarters_call(
+        value_part_kernel,
+        4,
+        128,
+        [block, block, whole, whole],
+        True,
+        (own_hidden, other_hidden, grads, other_grads),
+    )
+
+
+def key_part(key, other_key, gate, other_gate, pre, other_pre, gate_grad, other_gate_grad):
+    tokens = pre.shape[0]
+    half = pl.BlockSpec((tokens, 512), lambda i: (0, 0))
+    whole = pl.BlockSpec((tokens, 1024), lambda i: (0, 0))
+    block = pl.BlockSpec((tokens, 1024), lambda i: (0, jnp.minimum(i, 3)))
+    return quarters_call(
+        key_part_kernel,
+        5,
+        160,
+        [half, half, half, half, block, block, whole, whole],
+        False,
+        (key, other_key, gate, other_gate, pre, other_pre, gate_grad, other_gate_grad),
+    )
+
+
+def time_part(own, other, grads, other_grads, branch, other_branch):
+    tokens = grads.shape[0]
+    half = pl.BlockSpec((tokens, 512), lambda i: (0, i))
+    whole = pl.BlockSpec((tokens, 1024), lambda i: (0, 0))
+    block = pl.BlockSpec((tokens, 1024), lambda i: (0, jnp.minimum(i, 2)))
+    return quarters_call(
+        time_part_kernel,
+        4,
+        128,
+        [half, half, block, block, whole, whole],
+        False,
+        (own, other, grads, other_grads, branch, other_branch),
+    )
 
 
 def ordered_halves(rows_in, flat):
     width = rows_in.shape[-1]
     rows_in = rows_in.reshape(-1, width)
-    if width == 4096:
-        ordered = pick(rows_in, owner_order(flat))
-    else:
-        ordered = jnp.dot(
-            rows_in, choice(flat, width), preferred_element_type=jnp.bfloat16
-        )
+    ordered = jnp.dot(rows_in, choice(flat, width), preferred_element_type=jnp.bfloat16)
     return ordered[:, : width // 2], ordered[:, width // 2 :]
 
 
@@ -188,26 +473,22 @@
     return array.astype(jnp.bfloat16)
 
 
-def quarters(parts):
-    return parts.reshape((2, 2, 4) + parts.shape[1:])
-
-
-def add_corner(quad, add_a, add_b):
-    to_y = jnp.concatenate([narrow(wide(quad[1, 0, :2]) + wide(add_a)), quad[1, 0, 2:]])
-    to_x = jnp.concatenate([quad[0, 1, :2], narrow(wide(quad[0, 1, 2:]) + wide(add_b))])
+def send_corner(parts):
+    return sent(parts[3], FLIP_X), sent(parts[4], FLIP_Y)
+
+
+def add_corner(parts, add_a, add_b):
+    to_y = jnp.concatenate([narrow(wide(parts[2][:2]) + wide(add_a)), parts[2][2:]])
+    to_x = jnp.concatenate([parts[1][:2], narrow(wide(parts[1][2:]) + wide(add_b))])
     return to_y, to_x
-
-
-def send_corner(quad):
-    return sent(quad[1, 1, :2], FLIP_X), sent(quad[1, 1, 2:], FLIP_Y)
 
 
 def send_sides(to_y, to_x):
     return sent(to_y, FLIP_Y), sent(to_x, FLIP_X)
 
 
-def add_sides(quad, from_y, from_x):
-    column = wide(quad[0, 0]) + wide(from_y) + wide(from_x)
+def add_sides(parts, from_y, from_x):
+    column = wide(parts[0]) + wide(from_y) + wide(from_x)
     return column[0], [narrow(column[d]) for d in (1, 2, 3)]
 
 
@@ -222,10 +503,9 @@
 
 
 def sum_vectors(rows_in, flat):
-    total = rows_in
-    for pairs in (FLIP_C, FLIP_X, FLIP_Y):
+    total = rows_in + sum(sent(rows_in, turn_z(d)) for d in (1, 2, 3))
+    for pairs in (FLIP_X, FLIP_Y, FLIP_C):
         total = total + sent(total, pairs)
-    total = total + sum(sent(total, turn_z(d)) for d in (1, 2, 3))
     count = total.shape[1] // 32
     return lax.dynamic_slice_in_dim(total, flat * count, count, 1)
 
@@ -409,32 +689,31 @@
                     feature_lookup_projection,
                     feature_content_projection,
                     feature_receptance_projection,
-                    temporal_result_projection,
                 ]
             ),
             BOTH,
         )
-        packed = jnp.pad(vectors.reshape(1, -1), ((0, 15), (0, 1024 - vectors.size)))
+        spread = jnp.tile(jnp.pad(vectors, ((0, 5), (0, 0))), (1, 32))
+        packed = jnp.where(jnp.arange(1024) // 32 == flat, spread, jnp.zeros_like(spread))
         part = stacked(
             [
                 temporal_lookup_projection,
                 temporal_content_projection,
                 temporal_receptance_projection,
+                temporal_result_projection,
                 packed,
             ]
         )
         column = jnp.stack([part] + around(part))
         from_x, from_y = sent(column, FLIP_X), sent(column, FLIP_Y)
         early = both_cores([column, from_x, from_y, *send_far(from_x, from_y)])
-        vectors = vectors_of(assemble(early, order, 96, 16, 1).reshape(32, 16, 1024))
+        vectors = jnp.sum(
+            assemble(early, order, 128, 16, 1).reshape(32, 16, 1024).astype(jnp.float32), axis=0
+        )
         lookup_weight = assemble(early, order, 0, 32, 1)
         content_weight = assemble(early, order, 32, 32, 1)
         receptance_weight = assemble(early, order, 64, 32, 1)
-        in_turn = jnp.arange(32, dtype=jnp.int32)
-        ffn_key_weight = assemble([late], in_turn, 0, 32, 4)
-        ffn_value_weight = assemble([late], in_turn, 128, 128, 1)
-        ffn_gate_weight = assemble([late], in_turn, 256, 32, 1)
-        result_weight = assemble([late], in_turn, 288, 32, 1)
+        result_weight = assemble(early, order, 96, 32, 1)
     else:
         (
             lookup_weight,
@@ -527,9 +806,10 @@
         own_value, far_value = ordered_halves(value_in, flat)
         own_gate, far_gate = ordered_halves(gate_in, flat)
         own_gated, far_gated = ordered_halves(gated, flat)
-        other_key, other_value, other_gate, other_gated = sent_together(
-            [far_key, far_value, far_gate, far_gated]
-        )
+        other_time = sent(
+            jnp.concatenate([far_key, far_value, far_gate, far_gated], axis=1), FLIP_C
+        )
+        own_time = jnp.concatenate([own_key, own_value, own_gate, own_gated], axis=1)
     middle = inputs + project(gated, result_weight)
     normed_two, unit_two, inv_two = norm_forward(
         middle, closing_standardize_scale, closing_standardize_offset
@@ -542,56 +822,56 @@
     ffn_gate_in = (
         normed_two * feature_receptance_mixture + before_two * (1.0 - feature_receptance_mixture)
     ).astype(jnp.bfloat16)
-    hidden_pre = project(ffn_key_in, ffn_key_weight)
-    hidden = jnp.square(jax.nn.relu(hidden_pre)).astype(jnp.bfloat16)
+    grad_out = upstream_sensitivity.astype(jnp.float32)
     if tuned:
         own_ffn_key, far_ffn_key = ordered_halves(ffn_key_in, flat)
         own_ffn_gate, far_ffn_gate = ordered_halves(ffn_gate_in, flat)
-        own_hidden, far_hidden = ordered_halves(hidden, flat)
         other_ffn_key, other_ffn_gate = sent_together([far_ffn_key, far_ffn_gate])
-        (other_hidden,) = sent_together([far_hidden])
-    ffn_value = project(hidden, ffn_value_weight)
-    ffn_gates = jax.nn.sigmoid(project(ffn_gate_in, ffn_gate_weight))
-    output = (middle + ffn_gates * ffn_value).astype(jnp.bfloat16)
-    matrices = (
-        lookup_weight,
-        content_weight,
-        receptance_weight,
-        result_weight,
-        ffn_key_weight,
-        ffn_value_weight,
-        ffn_gate_weight,
-    )
-    grad_out = upstream_sensitivity.astype(jnp.float32)
-    value_grad = (grad_out * ffn_gates).astype(jnp.bfloat16)
-    ffn_gate_grad = (grad_out * ffn_value * ffn_gates * (1.0 - ffn_gates)).astype(jnp.bfloat16)
-    hidden_grad = project_back(value_grad, matrices[5])
-    pre_grad = (hidden_grad * 2.0 * jax.nn.relu(hidden_pre)).astype(jnp.bfloat16)
-    if tuned:
-        flat_value_grad = value_grad.reshape(-1, width)
-        flat_gate_grad = ffn_gate_grad.reshape(-1, width)
-        flat_pre_grad = pre_grad.reshape(-1, pre_grad.shape[2])
-        other_value_grad, other_gate_grad = sent_together([flat_value_grad, flat_gate_grad])
-        (other_pre_grad,) = sent_together([flat_pre_grad])
-        ffn_value_part = chip_grad(own_hidden, other_hidden, flat_value_grad, other_value_grad)
-        ffn_key_part = chip_grad(own_ffn_key, other_ffn_key, flat_pre_grad, other_pre_grad)
-        ffn_gate_part = chip_grad(own_ffn_gate, other_ffn_gate, flat_gate_grad, other_gate_grad)
-        value_quad = quarters(ffn_value_part)
-        value_corner = send_corner(value_quad)
-        key_quad = quarters(
-            jnp.concatenate(
-                [ffn_key_part[:, :, q : q + 1024] for q in range(0, 4096, 1024)] + [ffn_gate_part],
-                axis=1,
-            )
-        )
-        value_from = send_sides(*add_corner(value_quad, *value_corner))
-        value_first, value_outgoing = add_sides(value_quad, *value_from)
+        output, value_grad, ffn_gate_grad, key_two_grad, gate_two_grad, *kept = channel_mix(
+            owner_slots(flat),
+            ffn_key_in.reshape(-1, width),
+            ffn_gate_in.reshape(-1, width),
+            middle.reshape(-1, width),
+            upstream_sensitivity.reshape(-1, width),
+            late,
+        )
+        output, key_two_grad, gate_two_grad = (
+            a.reshape(rows, length, width) for a in (output, key_two_grad, gate_two_grad)
+        )
+        own_hidden, far_hidden, pre_grad = kept
+        other_value_grad = sent(value_grad, FLIP_C)
+        other_hidden = sent(far_hidden, FLIP_C)
+        other_gate_grad = sent(ffn_gate_grad, FLIP_C)
+        other_pre_grad = sent(pre_grad, FLIP_C)
+        value_parts = value_part(own_hidden, other_hidden, value_grad, other_value_grad)
+        value_corner = send_corner(value_parts)
+        key_parts = key_part(
+            own_ffn_key,
+            other_ffn_key,
+            own_ffn_gate,
+            other_ffn_gate,
+            pre_grad,
+            other_pre_grad,
+            ffn_gate_grad,
+            other_gate_grad,
+        )
+        value_sides = add_corner(value_parts, *all_tied(value_corner, key_parts[4]))
+        value_from = send_sides(*value_sides)
     else:
+        hidden_pre = project(ffn_key_in, ffn_key_weight)
+        hidden = jnp.square(jax.nn.relu(hidden_pre)).astype(jnp.bfloat16)
+        ffn_value = project(hidden, ffn_value_weight)
+        ffn_gates = jax.nn.sigmoid(project(ffn_gate_in, ffn_gate_weight))
+        output = (middle + ffn_gates * ffn_value).astype(jnp.bfloat16)
+        value_grad = (grad_out * ffn_gates).astype(jnp.bfloat16)
+        ffn_gate_grad = (grad_out * ffn_value * ffn_gates * (1.0 - ffn_gates)).astype(jnp.bfloat16)
+        hidden_grad = project_back(value_grad, ffn_value_weight)
+        pre_grad = (hidden_grad * 2.0 * jax.nn.relu(hidden_pre)).astype(jnp.bfloat16)
         grad_ffn_value = weight_grad(hidden, value_grad)
         grad_ffn_key = weight_grad(ffn_key_in, pre_grad)
         grad_ffn_gate = weight_grad(ffn_gate_in, ffn_gate_grad)
-    key_two_grad = project_back(tied(pre_grad, ffn_value_part, key_quad) if tuned else pre_grad, matrices[4])
-    gate_two_grad = project_back(ffn_gate_grad, matrices[6])
+        key_two_grad = project_back(pre_grad, ffn_key_weight)
+        gate_two_grad = project_back(ffn_gate_grad, ffn_gate_weight)
     spread_two = normed_two - before_two
     grad_ffn_mix_key = jnp.sum(key_two_grad * spread_two, axis=(0, 1))
     grad_ffn_mix_gate = jnp.sum(gate_two_grad * spread_two, axis=(0, 1))
@@ -613,19 +893,15 @@
     branch_grad = middle_grad.astype(jnp.bfloat16)
     if tuned:
         flat_branch_grad = branch_grad.reshape(-1, width)
-        (other_branch_grad,) = sent_together([flat_branch_grad])
-        output_part = chip_grad(own_gated, other_gated, flat_branch_grad, other_branch_grad)
-        value_got = send_column(value_outgoing)
-        key_sides = add_corner(key_quad, *send_corner(key_quad))
+        other_branch_grad = sent(flat_branch_grad, FLIP_C)
+        key_corner = send_corner(key_parts)
     else:
         grad_output = weight_grad(gated, branch_grad)
     gated_grad = project_back(
-        tied(branch_grad, *value_outgoing) if tuned else branch_grad, matrices[3]
+        tied(branch_grad, value_sides[0]) if tuned else branch_grad, result_weight
     )
     gate_pre_grad = (gated_grad * mixed * gates * (1.0 - gates)).astype(jnp.bfloat16)
     blended_gradient = gated_grad * gates
-    if tuned:
-        blended_gradient = tied(blended_gradient, *key_sides)
     (
         key_gradient,
         value_gradient,
@@ -634,12 +910,13 @@
         numerator_gradient,
         denominator_gradient,
     ) = weighted_value_backward(blended_gradient)
+    state_gradient = jnp.stack([numerator_gradient, denominator_gradient])
     if tuned:
+        value_first, value_outgoing = add_sides(value_parts, *all_tied(value_from, state_gradient))
+        key_sides = add_corner(key_parts, *all_tied(key_corner, state_gradient))
         key_from = send_sides(*key_sides)
-        key_first, key_outgoing = add_sides(key_quad, *key_from)
-    num_next, den_next = carried_in(
-        jnp.stack([numerator_gradient, denominator_gradient]), starts_in, decay_vec, length, True
-    )
+        state_gradient = tied(state_gradient, key_sides[0], value_outgoing[0])
+    num_next, den_next = carried_in(state_gradient, starts_in, decay_vec, length, True)
     num_tail = tail_fade * num_next[:, None, :]
     den_tail = tail_fade * den_next[:, None, :]
     tail_grad = powered_lookups * (value_row_block * num_tail + den_tail)
@@ -654,35 +931,25 @@
     key_grad16 = key_gradient.astype(jnp.bfloat16)
     val_grad16 = value_gradient.astype(jnp.bfloat16)
     if tuned:
-        flat_grads = [g.reshape(-1, width) for g in (key_grad16, val_grad16, gate_pre_grad)]
-        other_grads = sent_together(flat_grads)
-        key_part = chip_grad(own_key, other_key, flat_grads[0], other_grads[0])
-        value_part = chip_grad(own_value, other_value, flat_grads[1], other_grads[1])
-        gate_part = chip_grad(own_gate, other_gate, flat_grads[2], other_grads[2])
-        time_quad = quarters(
-            jnp.concatenate([key_part, value_part, gate_part, output_part], axis=1)
-        )
-        key_got = send_column(key_outgoing)
-        time_sides = add_corner(time_quad, *send_corner(time_quad))
-        time_from = send_sides(*time_sides)
-        time_first, time_outgoing = add_sides(time_quad, *time_from)
-        time_total = add_all(time_first, send_column(time_outgoing))
-        grad_key, grad_value, grad_gate, grad_output = (
-            time_total[i : i + 32] for i in (0, 32, 64, 96)
-        )
-        grad_ffn_value = add_all(value_first, value_got)
-        key_total = add_all(key_first, key_got)
-        grad_ffn_key = jnp.concatenate([key_total[i : i + 32] for i in (0, 32, 64, 96)], axis=1)
-        grad_ffn_gate = key_total[128:]
+        flat_grads = jnp.concatenate(
+            [g.reshape(-1, width) for g in (key_grad16, val_grad16, gate_pre_grad)], axis=1
+        )
+        other_grads = sent(flat_grads, FLIP_C)
+        time_parts = time_part(
+            own_time, other_time, flat_grads, other_grads, flat_branch_grad, other_branch_grad
+        )
+        value_got = all_tied(send_column(all_tied(value_outgoing, num_next)), time_parts[4])
+        key_first, key_outgoing = add_sides(key_parts, *all_tied(key_from, time_parts[4]))
+        time_corner = send_corner(time_parts)
     else:
         grad_key = weight_grad(key_in, key_grad16)
         grad_value = weight_grad(value_in, val_grad16)
         grad_gate = weight_grad(gate_in, gate_pre_grad)
-    key_in_grad = project_back(
-        tied(key_grad16, time_quad, *key_outgoing) if tuned else key_grad16, matrices[0]
-    )
-    value_in_grad = project_back(val_grad16, matrices[1])
-    gate_in_grad = project_back(gate_pre_grad, matrices[2])
+    if tuned:
+        key_grad16 = tied(key_grad16, key_outgoing[0])
+    key_in_grad = project_back(key_grad16, lookup_weight)
+    value_in_grad = project_back(val_grad16, content_weight)
+    gate_in_grad = project_back(gate_pre_grad, receptance_weight)
     spread_one = normed_one - before_one
     grad_mix_key = jnp.sum(key_in_grad * spread_one, axis=(0, 1))
     grad_mix_value = jnp.sum(value_in_grad * spread_one, axis=(0, 1))
@@ -697,13 +964,28 @@
         + value_in_grad * (1.0 - temporal_content_mixture)
         + gate_in_grad * (1.0 - temporal_receptance_mixture)
     ) * keep_mask
+    if tuned:
+        time_sides = add_corner(time_parts, *all_tied(time_corner, before_one_grad))
+        time_from = send_sides(*time_sides)
     from_next = shifted(before_one_grad[:, :1, :], "seq", -1)
+    if tuned:
+        key_got = send_column(all_tied(key_outgoing, from_next))
     normed_one_grad = normed_one_grad + jnp.concatenate(
         [before_one_grad[:, 1:, :], from_next], axis=1
     )
     input_norm_grad, grad_gain_one, grad_bias_one = norm_backward(
         normed_one_grad, unit_one, inv_one, opening_standardize_scale
     )
+    if tuned:
+        time_first, time_outgoing = add_sides(time_parts, *time_from)
+        time_total = add_all(time_first, send_column(time_outgoing))
+        grad_key, grad_value, grad_gate, grad_output = (
+            time_total[i : i + 32] for i in (0, 32, 64, 96)
+        )
+        grad_ffn_value = add_all(value_first, value_got)
+        key_total = add_all(key_first, key_got)
+        grad_ffn_key = jnp.concatenate([key_total[i : i + 32] for i in (0, 32, 64, 96)], axis=1)
+        grad_ffn_gate = key_total[128:]
     input_grad = middle_grad + input_norm_grad
     vector_grads = jnp.stack(
         [

time: 565 us -> 477 us (0.84)
  matrix products: 111 us -> 37.5 us
  Pallas kernels: 28.7 us -> 75.1 us
  waiting for transfers between devices: 186 us -> 154 us
  local copies, waits for them, and re-layouts: 63.7 us -> 42 us
  starting transfers between devices: 82.7 us -> 67.3 us
  other arithmetic: 61.2 us -> 70.7 us
    pallas_call x1 -> x4, Pallas kernels: 2.14 us -> 60 us  [the longest x1 33.1 us: channel_mix(): pl.pallas_call(channel_kernel, out_shape=(half_rows, half_rows, half_rows...]
    dot_general x14 -> x0, matrix products: 31.9 us -> none  [the longest x7 18.5 us: chip_grad(): jnp.einsum('td,te->de', other_in, other_grads, preferred_element_type=jnp...]
    dot_general x7 -> x4, matrix products: 31 us -> 5.3 us  [project_back(): jnp.einsum('rte,de->rtd', grads, weight, preferred_element_type=jnp.float32)]
    ppermute x54 -> x55, waiting for transfers between devices: 173 us -> 153 us  [sent(): return lax.ppermute(array, BOTH, pairs)]
    unnamed x362 -> x321, local copies, waits for them, and re-layouts: 38 us -> 19.2 us
    dot_general x7 -> x4, matrix products: 25.5 us -> 8.66 us  [project(): jnp.einsum('rtd,de->rte', rows_in, weight, preferred_element_type=jnp.flo...]
    ppermute x54 -> x55, starting transfers between devices: 75.7 us -> 61.6 us  [sent(): return lax.ppermute(array, BOTH, pairs)]
    all_gather x1, waiting for transfers between devices: 13 us -> 0.02 us  [shards(): lax.all_gather(stacked([feature_lookup_projection, feature_content_projec...]
  transfers between devices with their start and end apart: 59 -> 60, of which waited for: 26 -> 19; matrix products, arithmetic and copies ran while one was open for 29% -> 27% of each run, Pallas kernels for 4% -> 9%
where the time goes in v2:
time: 477 us; the launch traced here: 470 us
  waiting for transfers between devices  154 us (32%)
  Pallas kernels  75.1 us (16%)
  other arithmetic  70.7 us (15%)
  starting transfers between devices  67.3 us (14%)
  local copies, waits for them, and re-layouts  42 us (9%)
  matrix products  37.5 us (8%)
  between operations  23.8 us (5%)
    ppermute x55, waiting for transfers between devices, sent(): return lax.ppermute(array, BOTH, pairs)  153 us
    ppermute x55, starting transfers between devices, sent(): return lax.ppermute(array, BOTH, pairs)  61.6 us
    pallas_call x1, Pallas kernels, channel_mix(): pl.pallas_call(channel_kernel, out_shape=(half_rows, half_rows, half_rows...  33.1 us
    pallas_call x3, Pallas kernels, quarters_call(): pl.pallas_call(kernel, grid=(steps,), out_shape=tuple((jax.ShapeDtypeStru...  27 us
    unnamed x321, local copies, waits for them, and re-layouts  19.2 us
    pallas_call x5, Pallas kernels, assemble(): pl.pallas_call(partial(assemble_kernel, counts, start, columns), out_shap...  15.1 us
    dot_general x2, matrix products, weighted_value_local(): jnp.einsum('rti,rie->rte', pair_mask, weighted, precision=highest)  13.7 us
    dot_general x6, matrix products, ordered_halves(): jnp.dot(rows_in, choice(flat, width), preferred_element_type=jnp.bfloat16)  9.91 us
  transfers between devices with their start and end apart: 60, of which 19 were waited for; matrix products, arithmetic and copies ran while one was open for 27% of the time, Pallas kernels for 9%

profile of v2, /device:TPU:0, one launch (start us, length us, event | category | flops | bytes accessed | tf_op | source)
XLA Modules:
  0.0 470.3 jit_solution(16562402264030929)
XLA Ops:
  15.2 5.1 %collective-permute-start.2 = (bf16[144,1024]{1,0:T(8,128)(2,1)S(1)}, bf16[144,1024]{1,0:T(8,128)(2,1)S(1)}, u32[]{:S(2)}, u32[]{:S(2)}) collective-permute-start(bf16[144,1024]{1,0:T(8,128)(2,1)S(1)} %select_dynamic-update-slice_fusion), channel_id=1, source_target_pairs={{0,6},{1,7},{2,0},{3,1},{4,2},{5,3},{6,4},{7,5},{8,14},{9,15},{10,... | collective-permute-start | bytes 884744 | tf_op jit(solution)/shard_map/ppermute | solution.py:29
  29.7 28.3 %collective-permute-done.1 = bf16[144,1024]{1,0:T(8,128)(2,1)S(1)} collective-permute-done((bf16[144,1024]{1,0:T(8,128)(2,1)S(1)}, bf16[144,1024]{1,0:T(8,128)(2,1)S(1)}, u32[]{:S(2)}, u32[]{:S(2)}) %collective-permute-start.1) | collective-permute-done | bytes 294944 | tf_op jit(solution)/shard_map/ppermute | solution.py:29
  69.3 31.7 %collective-permute-done.3.refs_1_ = bf16[4,144,1024]{2,1,0:T(8,128)(2,1)S(1)} collective-permute-done((bf16[4,144,1024]{2,1,0:T(8,128)(2,1)S(1)}, bf16[4,144,1024]{2,1,0:T(8,128)(2,1)S(1)}, u32[]{:S(2)}, u32[]{:S(2)}) %collective-permute-start.3) | collective-permute-done | bytes 1179680 | tf_op jit(solution)/shard_map/ppermute | solution.py:29
  112.3 2.9 collective-permute-done.6.refs_4_
  115.5 2.7 collective-permute-done.11.refs_9_
  120.6 3.1 shard_map.358
  123.8 3.1 shard_map.359
  143.0 5.1 %broadcast_multiply_fusion = (f32[2,256,2048]{2,1,0:T(8,128)S(1)}, f32[2,256,2048]{2,1,0:T(8,128)}) fusion(f32[256,2048]{1,0:T(8,128)S(1)} %get-tuple-element.213, f32[2,256,1024]{2,1,0:T(8,128)S(1)} %convolution_exponential_fusion, f32[2,256,1024]{2,1,0:T(8,128)S(1)} %get-tuple-element.122, f32[256,2048]{1,0:T(8,128)S(1)} %get-tuple-element.212, ...), kind=kOutput, calls=%fused_computation.98 | convolution fusion | flops 3224633344 | bytes 16844800 | tf_op jit(solution)/shard_map/jvp(rti,rie->rte)/dot_general | solution.py:609
  148.3 10.3 %collective-permute-start.15 = (f32[2,2,1024]{2,1,0:T(2,128)S(1)}, f32[2,2,1024]{2,1,0:T(2,128)S(1)}, u32[]{:S(2)}, u32[]{:S(2)}) collective-permute-start(f32[2,2,1024]{2,1,0:T(2,128)S(1)} %select_add_fusion.1), channel_id=1, source_target_pairs={{0,4},{1,5},{2,6},{3,7},{4,0},{5,1},{6,2},{7,3},{8,12},{9,13},{10,... | collective-permute-start | bytes 49160 | tf_op jit(solution)/shard_map/ppermute | solution.py:29
  161.3 3.4 shard_map.357
  164.6 3.1 shard_map.360
  167.9 4.5 multiply_convert_fusion.1
  180.7 33.1 %shard_map.361 = (bf16[512,1024]{1,0:T(8,128)(2,1)}, bf16[512,1024]{1,0:T(8,128)(2,1)}, bf16[512,1024]{1,0:T(8,128)(2,1)}, f32[512,1024]{1,0:T(8,128)}, f32[512,...) custom-call(s32[32]{0:T(128)} %and_add_fusion.slots_ref, ...), custom_call_target="tpu_custom_call" | custom-call | flops 19327352832 | bytes 41943040 | tf_op jit(solution)/shard_map/pallas_call | solution.py:269
  228.7 3.1 multiply_reduce_fusion.4
  233.2 7.3 %shard_map.362 = (bf16[4,128,1024]{2,1,0:T(8,128)(2,1)S(1)}, bf16[4,128,1024]{2,1,0:T(8,128)(2,1)S(1)}, bf16[4,128,1024]{2,1,0:T(8,128)(2,1)S(1)}, bf16[2,128,10...) custom-call(bf16[4,512,512]{2,1,0:T(8,128)(2,1)} %get-tuple-element.46.own_ref, ...), custom_call_target="tpu_custom_call" | custom-call | flops 4294967296 | bytes 20971520 | tf_op jit(solution)/shard_map/pallas_call | solution.py:394
  240.6 2.7 collective-permute-start.21
  244.3 10.3 %shard_map.363 = (bf16[4,160,1024]{2,1,0:T(8,128)(2,1)}, bf16[4,160,1024]{2,1,0:T(8,128)(2,1)}, bf16[4,160,1024]{2,1,0:T(8,128)(2,1)}, bf16[2,160,1024]{2,1,0:T(8,128)(2,1)S(1)}, bf16[2,160,1024]{2,1,0:T(8,128)(2,1)S(1)}) custom-call(bf16[512,512]{1,0:T(8,128)(2,1)S(1)} %get-tuple-element.146.key_ref, bf16[512,512]{1,0:T(8,128)(2,1)S(1)} %get-tuple-element.142.other_key_ref, ...), custom_call_target="tpu_custom_call" | custom-call | flops 5368709120 | bytes 22020096 | tf_op jit(solution)/shard_map/pallas_call | solution.py:394
  265.1 3.4 fusion.33
  269.7 4.9 %collective-permute-done.25 = bf16[2,160,1024]{2,1,0:T(8,128)(2,1)S(1)} collective-permute-done((bf16[2,160,1024]{2,1,0:T(8,128)(2,1)S(1)}, bf16[2,160,1024]{2,1,0:T(8,128)(2,1)S(1)}, u32[]{:S(2)}, u32[]{:S(2)}) %collective-permute-start.25) | collective-permute-done | bytes 655392 | tf_op jit(solution)/shard_map/ppermute | solution.py:29
  275.9 21.0 %collective-permute-done.28 = bf16[4,128,1024]{2,1,0:T(8,128)(2,1)S(1)} collective-permute-done((bf16[4,128,1024]{2,1,0:T(8,128)(2,1)S(1)}, bf16[4,128,1024]{2,1,0:T(8,128)(2,1)S(1)}, u32[]{:S(2)}, u32[]{:S(2)}) %collective-permute-start.28) | collective-permute-done | bytes 1048608 | tf_op jit(solution)/shard_map/ppermute | solution.py:29
  311.7 8.6 %multiply_reduce_fusion = (f32[256,2048]{1,0:T(8,128)S(1)}, f32[2,256,2048]{2,1,0:T(8,128)S(1)}) fusion(f32[2,256,1024]{2,1,0:T(8,128)} %copy-done.20, f32[2,256,1024]{2,1,0:T(8,128)} %copy-done.31, f32[256,2048]{1,0:T(8,128)} %copy-done.26, f32[2,256,1024]{2,1,0:T(8,128)} %get-tuple-element.106, f32[2,256,1024]{2,1,0:T(8,128)} %get-tuple-element.105, ...), kind=kOutput, calls=%fused_computation.5 | convolution fusion | flops 3227254784 | bytes 18941952 | tf_op jit(solution)/shard_map/transpose(jvp(rti,rie->rte))/dot_general | solution.py:609
  320.5 2.7 multiply_reduce_fusion.5
  344.5 9.3 %shard_map.364 = (bf16[4,128,1024]{2,1,0:T(8,128)(2,1)S(1)}, bf16[4,128,1024]{2,1,0:T(8,128)(2,1)S(1)}, bf16[4,128,1024]{2,1,0:T(8,128)(2,1)S(1)}, bf16[2,128,1024]{2,1,0:T(8,128)(2,1)}, bf16[2,128,1024]{2,1,0:T(8,128)(2,1)}) custom-call(bf16[512,2048]{1,0:T(8,128)(2,1)} %pad_maximum_fusion.6.own_ref, bf16[512,2048]{1,0:T(8,128)(2,1)} %collective-permute-done.34.other_ref, ...), custom_call_target="tpu_custom_call" | custom-call | flops 4294967296 | bytes 20971520 | tf_op jit(solution)/shard_map/pallas_call | solution.py:394
  355.6 8.9 %collective-permute-done.38 = bf16[4,160,1024]{2,1,0:T(8,128)(2,1)} collective-permute-done((bf16[4,160,1024]{2,1,0:T(8,128)(2,1)}, bf16[4,160,1024]{2,1,0:T(8,128)(2,1)}, u32[]{:S(2)}, u32[]{:S(2)}) %collective-permute-start.38) | collective-permute-done | bytes 1310752 | tf_op jit(solution)/shard_map/ppermute | solution.py:29
  365.7 4.3 fusion.130
  384.3 4.1 fusion.23
  393.8 3.1 collective-permute-done.40
  403.1 4.6 fusion.22
  414.7 12.9 %collective-permute-done.54 = bf16[160,1024]{1,0:T(8,128)(2,1)S(1)} collective-permute-done((bf16[160,1024]{1,0:T(8,128)(2,1)S(1)}, bf16[160,1024]{1,0:T(8,128)(2,1)S(1)}, u32[]{:S(2)}, u32[]{:S(2)}) %collective-permute-start.54) | collective-permute-done | bytes 327712 | tf_op jit(solution)/shard_map/ppermute | solution.py:29
  429.5 5.2 %collective-permute-done.49 = bf16[4,128,1024]{2,1,0:T(8,128)(2,1)S(1)} collective-permute-done((bf16[4,128,1024]{2,1,0:T(8,128)(2,1)S(1)}, bf16[4,128,1024]{2,1,0:T(8,128)(2,1)S(1)}, u32[]{:S(2)}, u32[]{:S(2)}) %collective-permute-start.49) | collective-permute-done | bytes 1048608 | tf_op jit(solution)/shard_map/ppermute | solution.py:29
  442.0 4.2 collective-permute-done.52
  446.2 15.9 %collective-permute-done.51 = bf16[128,1024]{1,0:T(8,128)(2,1)S(1)} collective-permute-done((bf16[128,1024]{1,0:T(8,128)(2,1)S(1)}, bf16[128,1024]{1,0:T(8,128)(2,1)S(1)}, u32[]{:S(2)}, u32[]{:S(2)}) %collective-permute-start.51) | collective-permute-done | bytes 262176 | tf_op jit(solution)/shard_map/ppermute | solution.py:29
  (588 shorter events, 173.6 us)
Async XLA Ops:
  7.2 173.5 %all-gather.3.cloned.1.call-start = ((), (), s32[]{:S(2)}) async-start(), calls=%async_computation | async-start | bytes 19464192 | tf_op jit(solution)/shard_map/all_gather | solution.py:686
  20.4 37.6 %collective-permute-start.1 = (bf16[144,1024]{1,0:T(8,128)(2,1)S(1)}, bf16[144,1024]{1,0:T(8,128)(2,1)S(1)}, u32[]{:S(2)}, u32[]{:S(2)}) collective-permute-start(bf16[144,1024]{1,0:T(8,128)(2,1)S(1)} %select_dynamic-update-slice_fusion), channel_id=1, source_target_pairs={{0,4},{1,5},{2,6},{3,7},{4,0},{5,1},{6,2},{7,3},{8,12},{9,13},{10,... | collective-permute-start | bytes 884744 | tf_op jit(solution)/shard_map/ppermute | solution.py:29
  20.4 37.6 %collective-permute-start = (bf16[144,1024]{1,0:T(8,128)(2,1)S(1)}, bf16[144,1024]{1,0:T(8,128)(2,1)S(1)}, u32[]{:S(2)}, u32[]{:S(2)}) collective-permute-start(bf16[144,1024]{1,0:T(8,128)(2,1)S(1)} %select_dynamic-update-slice_fusion), channel_id=1, source_target_pairs={{0,2},{1,3},{2,4},{3,5},{4,6},{5,7},{6,0},{7,1},{8,10},{9,11},{10,... | collective-permute-start | bytes 884744 | tf_op jit(solution)/shard_map/ppermute | solution.py:29
  22.7 84.6 %collective-permute-start.12 = (bf16[2,1,1024]{2,1,0:T(2,128)(2,1)}, bf16[2,1,1024]{2,1,0:T(2,128)(2,1)S(1)}, u32[]{:S(2)}, u32[]{:S(2)}) collective-permute-start(bf16[2,1,1024]{2,1,0:T(2,128)(2,1)} %slice.326), channel_id=1, source_target_pairs={{0,1},{1,2},{2,3},{3,4},{4,5},{5,6},{6,7},{8,9},{9,10},{10,11},{11... | collective-permute-start | bytes 12296 | tf_op jit(solution)/shard_map/ppermute | solution.py:516
  58.2 42.8 %collective-permute-start.3 = (bf16[4,144,1024]{2,1,0:T(8,128)(2,1)S(1)}, bf16[4,144,1024]{2,1,0:T(8,128)(2,1)S(1)}, u32[]{:S(2)}, u32[]{:S(2)}) collective-permute-start(bf16[4,144,1024]{2,1,0:T(8,128)(2,1)S(1)} %pad_maximum_fusion.10.refs_0_), channel_id=1, source_target_pairs={{0,8},{1,9},{2,10},{3,11},{4,12},{5,13},{6,14},{7,15},{8,0},{9,1},... | collective-permute-start | bytes 3538952 | tf_op jit(solution)/shard_map/ppermute | solution.py:29
  59.7 44.4 %collective-permute-start.4 = (bf16[4,144,1024]{2,1,0:T(8,128)(2,1)S(1)}, bf16[4,144,1024]{2,1,0:T(8,128)(2,1)S(1)}, u32[]{:S(2)}, u32[]{:S(2)}) collective-permute-start(bf16[4,144,1024]{2,1,0:T(8,128)(2,1)S(1)} %pad_maximum_fusion.10.refs_0_), channel_id=1, source_target_pairs={{0,16},{1,17},{2,18},{3,19},{4,20},{5,21},{6,22},{7,23},{8,24},{9,... | collective-permute-start | bytes 3538952 | tf_op jit(solution)/shard_map/ppermute | solution.py:29
  148.2 19.6 %collective-permute-start.16 = (f32[2,2,1024]{2,1,0:T(2,128)S(1)}, f32[2,2,1024]{2,1,0:T(2,128)S(1)}, u32[]{:S(2)}, u32[]{:S(2)}) collective-permute-start(f32[2,2,1024]{2,1,0:T(2,128)S(1)} %select_add_fusion.1), channel_id=1, source_target_pairs={{0,6},{1,7},{2,0},{3,1},{4,2},{5,3},{6,4},{7,5},{8,14},{9,15},{10,... | collective-permute-start | bytes 49160 | tf_op jit(solution)/shard_map/ppermute | solution.py:29
  148.3 19.5 %collective-permute-start.15 = (f32[2,2,1024]{2,1,0:T(2,128)S(1)}, f32[2,2,1024]{2,1,0:T(2,128)S(1)}, u32[]{:S(2)}, u32[]{:S(2)}) collective-permute-start(f32[2,2,1024]{2,1,0:T(2,128)S(1)} %select_add_fusion.1), channel_id=1, source_target_pairs={{0,4},{1,5},{2,6},{3,7},{4,0},{5,1},{6,2},{7,3},{8,12},{9,13},{10,... | collective-permute-start | bytes 49160 | tf_op jit(solution)/shard_map/ppermute | solution.py:29
  213.8 30.4 %collective-permute-start.23 = (bf16[512,4096]{1,0:T(8,128)(2,1)}, bf16[512,4096]{1,0:T(8,128)(2,1)}, u32[]{:S(2)}, u32[]{:S(2)}) collective-permute-start(bf16[512,4096]{1,0:T(8,128)(2,1)} %get-tuple-element.51.refs_0_), channel_id=1, source_target_pairs={{0,1},{1,0},{2,3},{3,2},{4,5},{5,4},{6,7},{7,6},{8,9},{9,8},{10,11... | collective-permute-start | bytes 12582920 | tf_op jit(solution)/shard_map/ppermute | solution.py:29
  228.7 15.6 %collective-permute-start.24 = (bf16[512,1024]{1,0:T(8,128)(2,1)}, bf16[512,1024]{1,0:T(8,128)(2,1)}, u32[]{:S(2)}, u32[]{:S(2)}) collective-permute-start(bf16[512,1024]{1,0:T(8,128)(2,1)} %get-tuple-element.52.refs_2_), channel_id=1, source_target_pairs={{0,1},{1,0},{2,3},{3,2},{4,5},{5,4},{6,7},{7,6},{8,9},{9,8},{10,11... | collective-permute-start | bytes 3145736 | tf_op jit(solution)/shard_map/ppermute | solution.py:29
  240.6 15.3 %collective-permute-start.21 = (bf16[2,128,1024]{2,1,0:T(8,128)(2,1)S(1)}, bf16[2,128,1024]{2,1,0:T(8,128)(2,1)S(1)}, u32[]{:S(2)}, u32[]{:S(2)}) collective-permute-start(bf16[2,128,1024]{2,1,0:T(8,128)(2,1)S(1)} %get-tuple-element.50), channel_id=1, source_target_pairs={{0,8},{1,9},{2,10},{3,11},{4,12},{5,13},{6,14},{7,15},{8,0},{9,1},... | collective-permute-start | bytes 1572872 | tf_op jit(solution)/shard_map/ppermute | solution.py:29
  244.1 14.7 %collective-permute-start.27 = (bf16[2,128,1024]{2,1,0:T(8,128)(2,1)S(1)}, bf16[2,128,1024]{2,1,0:T(8,128)(2,1)S(1)}, u32[]{:S(2)}, u32[]{:S(2)}) collective-permute-start(bf16[2,128,1024]{2,1,0:T(8,128)(2,1)S(1)} %get-tuple-element.58), channel_id=1, source_target_pairs={{0,16},{1,17},{2,18},{3,19},{4,20},{5,21},{6,22},{7,23},{8,24},{9,... | collective-permute-start | bytes 1572872 | tf_op jit(solution)/shard_map/ppermute | solution.py:29
  257.2 17.3 %collective-permute-start.25 = (bf16[2,160,1024]{2,1,0:T(8,128)(2,1)S(1)}, bf16[2,160,1024]{2,1,0:T(8,128)(2,1)S(1)}, u32[]{:S(2)}, u32[]{:S(2)}) collective-permute-start(bf16[2,160,1024]{2,1,0:T(8,128)(2,1)S(1)} %get-tuple-element.55), channel_id=1, source_target_pairs={{0,8},{1,9},{2,10},{3,11},{4,12},{5,13},{6,14},{7,15},{8,0},{9,1},... | collective-permute-start | bytes 1966088 | tf_op jit(solution)/shard_map/ppermute | solution.py:29
  259.1 37.8 %collective-permute-start.28 = (bf16[4,128,1024]{2,1,0:T(8,128)(2,1)S(1)}, bf16[4,128,1024]{2,1,0:T(8,128)(2,1)S(1)}, u32[]{:S(2)}, u32[]{:S(2)}) collective-permute-start(bf16[4,128,1024]{2,1,0:T(8,128)(2,1)S(1)} %pad_maximum_fusion.13), channel_id=1, source_target_pairs={{0,8},{1,9},{2,10},{3,11},{4,12},{5,13},{6,14},{7,15},{8,0},{9,1},... | collective-permute-start | bytes 3145736 | tf_op jit(solution)/shard_map/ppermute | solution.py:29
  259.8 37.2 %collective-permute-start.26 = (bf16[4,128,1024]{2,1,0:T(8,128)(2,1)S(1)}, bf16[4,128,1024]{2,1,0:T(8,128)(2,1)S(1)}, u32[]{:S(2)}, u32[]{:S(2)}) collective-permute-start(bf16[4,128,1024]{2,1,0:T(8,128)(2,1)S(1)} %pad_maximum_fusion.12), channel_id=1, source_target_pairs={{0,16},{1,17},{2,18},{3,19},{4,20},{5,21},{6,22},{7,23},{8,24},{9,... | collective-permute-start | bytes 3145736 | tf_op jit(solution)/shard_map/ppermute | solution.py:29
  303.8 27.5 %collective-permute-start.37 = (bf16[2,160,1024]{2,1,0:T(8,128)(2,1)S(1)}, bf16[2,160,1024]{2,1,0:T(8,128)(2,1)}, u32[]{:S(2)}, u32[]{:S(2)}) collective-permute-start(bf16[2,160,1024]{2,1,0:T(8,128)(2,1)S(1)} %copy-done.12), channel_id=1, source_target_pairs={{0,16},{1,17},{2,18},{3,19},{4,20},{5,21},{6,22},{7,23},{8,24},{9,... | collective-permute-start | bytes 1966088 | tf_op jit(solution)/shard_map/ppermute | solution.py:29
  324.2 19.3 %collective-permute-start.35 = (bf16[512,3072]{1,0:T(8,128)(2,1)S(1)}, bf16[512,3072]{1,0:T(8,128)(2,1)}, u32[]{:S(2)}, u32[]{:S(2)}) collective-permute-start(bf16[512,3072]{1,0:T(8,128)(2,1)S(1)} %pad_maximum_fusion.2.grad_ref), channel_id=1, source_target_pairs={{0,1},{1,0},{2,3},{3,2},{4,5},{5,4},{6,7},{7,6},{8,9},{9,8},{10,11... | collective-permute-start | bytes 9437192 | tf_op jit(solution)/shard_map/ppermute | solution.py:29
  325.9 15.5 %collective-permute-start.34 = (bf16[512,2048]{1,0:T(8,128)(2,1)S(1)}, bf16[512,2048]{1,0:T(8,128)(2,1)}, u32[]{:S(2)}, u32[]{:S(2)}) collective-permute-start(bf16[512,2048]{1,0:T(8,128)(2,1)S(1)} %pad_maximum_fusion.7), channel_id=1, source_target_pairs={{0,1},{1,0},{2,3},{3,2},{4,5},{5,4},{6,7},{7,6},{8,9},{9,8},{10,11... | collective-permute-start | bytes 6291464 | tf_op jit(solution)/shard_map/ppermute | solution.py:29
  328.4 14.7 %collective-permute-start.36 = (bf16[512,1024]{1,0:T(8,128)(2,1)S(1)}, bf16[512,1024]{1,0:T(8,128)(2,1)}, u32[]{:S(2)}, u32[]{:S(2)}) collective-permute-start(bf16[512,1024]{1,0:T(8,128)(2,1)S(1)} %bitcast.249), channel_id=1, source_target_pairs={{0,1},{1,0},{2,3},{3,2},{4,5},{5,4},{6,7},{7,6},{8,9},{9,8},{10,11... | collective-permute-start | bytes 3145736 | tf_op jit(solution)/shard_map/ppermute | solution.py:29
  333.9 30.6 %collective-permute-start.38 = (bf16[4,160,1024]{2,1,0:T(8,128)(2,1)}, bf16[4,160,1024]{2,1,0:T(8,128)(2,1)}, u32[]{:S(2)}, u32[]{:S(2)}) collective-permute-start(bf16[4,160,1024]{2,1,0:T(8,128)(2,1)} %pad_maximum_fusion.9), channel_id=1, source_target_pairs={{0,8},{1,9},{2,10},{3,11},{4,12},{5,13},{6,14},{7,15},{8,0},{9,1},... | collective-permute-start | bytes 3932168 | tf_op jit(solution)/shard_map/ppermute | solution.py:29
  335.4 30.3 %collective-permute-start.33 = (bf16[4,160,1024]{2,1,0:T(8,128)(2,1)}, bf16[4,160,1024]{2,1,0:T(8,128)(2,1)}, u32[]{:S(2)}, u32[]{:S(2)}) collective-permute-start(bf16[4,160,1024]{2,1,0:T(8,128)(2,1)} %pad_maximum_fusion.8), channel_id=1, source_target_pairs={{0,16},{1,17},{2,18},{3,19},{4,20},{5,21},{6,22},{7,23},{8,24},{9,... | collective-permute-start | bytes 3932168 | tf_op jit(solution)/shard_map/ppermute | solution.py:29
  341.4 35.4 %collective-permute-start.58 = (bf16[128,1024]{1,0:T(8,128)(2,1)}, bf16[128,1024]{1,0:T(8,128)(2,1)}, u32[]{:S(2)}, u32[]{:S(2)}) collective-permute-start(bf16[128,1024]{1,0:T(8,128)(2,1)} %get-tuple-element.129), channel_id=1, source_target_pairs={{0,6},{1,7},{2,0},{3,1},{4,2},{5,3},{6,4},{7,5},{8,14},{9,15},{10,... | collective-permute-start | bytes 786440 | tf_op jit(solution)/shard_map/ppermute | solution.py:29
  343.1 36.4 %collective-permute-start.57 = (bf16[128,1024]{1,0:T(8,128)(2,1)}, bf16[128,1024]{1,0:T(8,128)(2,1)}, u32[]{:S(2)}, u32[]{:S(2)}) collective-permute-start(bf16[128,1024]{1,0:T(8,128)(2,1)} %get-tuple-element.128), channel_id=1, source_target_pairs={{0,4},{1,5},{2,6},{3,7},{4,0},{5,1},{6,2},{7,3},{8,12},{9,13},{10,... | collective-permute-start | bytes 786440 | tf_op jit(solution)/shard_map/ppermute | solution.py:29
  343.5 36.0 %collective-permute-start.56 = (bf16[128,1024]{1,0:T(8,128)(2,1)S(1)}, bf16[128,1024]{1,0:T(8,128)(2,1)}, u32[]{:S(2)}, u32[]{:S(2)}) collective-permute-start(bf16[128,1024]{1,0:T(8,128)(2,1)S(1)} %broadcast_add_fusion.1), channel_id=1, source_target_pairs={{0,2},{1,3},{2,4},{3,5},{4,6},{5,7},{6,0},{7,1},{8,10},{9,11},{10,... | collective-permute-start | bytes 786440 | tf_op jit(solution)/shard_map/ppermute | solution.py:29
  364.5 43.3 %collective-permute-start.48 = (bf16[2,128,1024]{2,1,0:T(8,128)(2,1)}, bf16[2,128,1024]{2,1,0:T(8,128)(2,1)}, u32[]{:S(2)}, u32[]{:S(2)}) collective-permute-start(bf16[2,128,1024]{2,1,0:T(8,128)(2,1)} %get-tuple-element.60), channel_id=1, source_target_pairs={{0,16},{1,17},{2,18},{3,19},{4,20},{5,21},{6,22},{7,23},{8,24},{9,... | collective-permute-start | bytes 1572872 | tf_op jit(solution)/shard_map/ppermute | solution.py:29
  376.8 33.2 %collective-permute-start.46 = (bf16[2,128,1024]{2,1,0:T(8,128)(2,1)}, bf16[2,128,1024]{2,1,0:T(8,128)(2,1)}, u32[]{:S(2)}, u32[]{:S(2)}) collective-permute-start(bf16[2,128,1024]{2,1,0:T(8,128)(2,1)} %get-tuple-element.64), channel_id=1, source_target_pairs={{0,8},{1,9},{2,10},{3,11},{4,12},{5,13},{6,14},{7,15},{8,0},{9,1},... | collective-permute-start | bytes 1572872 | tf_op jit(solution)/shard_map/ppermute | solution.py:29
  399.0 15.7 %collective-permute-start.55 = (bf16[160,1024]{1,0:T(8,128)(2,1)S(1)}, bf16[160,1024]{1,0:T(8,128)(2,1)S(1)}, u32[]{:S(2)}, u32[]{:S(2)}) collective-permute-start(bf16[160,1024]{1,0:T(8,128)(2,1)S(1)} %get-tuple-element.127), channel_id=1, source_target_pairs={{0,6},{1,7},{2,0},{3,1},{4,2},{5,3},{6,4},{7,5},{8,14},{9,15},{10,... | collective-permute-start | bytes 983048 | tf_op jit(solution)/shard_map/ppermute | solution.py:29
  400.6 27.0 %collective-permute-start.54 = (bf16[160,1024]{1,0:T(8,128)(2,1)S(1)}, bf16[160,1024]{1,0:T(8,128)(2,1)S(1)}, u32[]{:S(2)}, u32[]{:S(2)}) collective-permute-start(bf16[160,1024]{1,0:T(8,128)(2,1)S(1)} %get-tuple-element.126), channel_id=1, source_target_pairs={{0,4},{1,5},{2,6},{3,7},{4,0},{5,1},{6,2},{7,3},{8,12},{9,13},{10,... | collective-permute-start | bytes 983048 | tf_op jit(solution)/shard_map/ppermute | solution.py:29
  409.2 25.6 %collective-permute-start.49 = (bf16[4,128,1024]{2,1,0:T(8,128)(2,1)S(1)}, bf16[4,128,1024]{2,1,0:T(8,128)(2,1)S(1)}, u32[]{:S(2)}, u32[]{:S(2)}) collective-permute-start(bf16[4,128,1024]{2,1,0:T(8,128)(2,1)S(1)} %pad_maximum_fusion.15), channel_id=1, source_target_pairs={{0,8},{1,9},{2,10},{3,11},{4,12},{5,13},{6,14},{7,15},{8,0},{9,1},... | collective-permute-start | bytes 3145736 | tf_op jit(solution)/shard_map/ppermute | solution.py:29
  411.4 25.3 %collective-permute-start.47 = (bf16[4,128,1024]{2,1,0:T(8,128)(2,1)S(1)}, bf16[4,128,1024]{2,1,0:T(8,128)(2,1)S(1)}, u32[]{:S(2)}, u32[]{:S(2)}) collective-permute-start(bf16[4,128,1024]{2,1,0:T(8,128)(2,1)S(1)} %pad_maximum_fusion.14), channel_id=1, source_target_pairs={{0,16},{1,17},{2,18},{3,19},{4,20},{5,21},{6,22},{7,23},{8,24},{9,... | collective-permute-start | bytes 3145736 | tf_op jit(solution)/shard_map/ppermute | solution.py:29
  439.4 22.7 %collective-permute-start.51 = (bf16[128,1024]{1,0:T(8,128)(2,1)S(1)}, bf16[128,1024]{1,0:T(8,128)(2,1)S(1)}, u32[]{:S(2)}, u32[]{:S(2)}) collective-permute-start(bf16[128,1024]{1,0:T(8,128)(2,1)S(1)} %get-tuple-element.132), channel_id=1, source_target_pairs={{0,4},{1,5},{2,6},{3,7},{4,0},{5,1},{6,2},{7,3},{8,12},{9,13},{10,... | collective-permute-start | bytes 786440 | tf_op jit(solution)/shard_map/ppermute | solution.py:29
  439.4 22.7 %collective-permute-start.50 = (bf16[128,1024]{1,0:T(8,128)(2,1)S(1)}, bf16[128,1024]{1,0:T(8,128)(2,1)S(1)}, u32[]{:S(2)}, u32[]{:S(2)}) collective-permute-start(bf16[128,1024]{1,0:T(8,128)(2,1)S(1)} %get-tuple-element.130), channel_id=1, source_target_pairs={{0,2},{1,3},{2,4},{3,5},{4,6},{5,7},{6,0},{7,1},{8,10},{9,11},{10,... | collective-permute-start | bytes 786440 | tf_op jit(solution)/shard_map/ppermute | solution.py:29
  (183 other events, 1639.0 us)
Sparse Core Ops, SparseCore 0:
  13.5 163.3 all-gather.2

commit v3 on v2

--- a/solution.py
+++ b/solution.py
@@ -178,8 +178,8 @@
 
     def forward(q, _):
         key_copy(q).wait()
-        for half in range(2):
-            rows = pl.ds(half * 256, 256)
+        for half in range(1):
+            rows = pl.ds(half * 512, 512)
             relu_s[q, rows, :] = jnp.maximum(
                 jnp.dot(
                     key_in_ref[rows, :],
@@ -192,8 +192,8 @@
         for k in range(8):
             hidden_start(q, k)
         value_copy(q).wait()
-        for half in range(2):
-            rows = pl.ds(half * 256, 256)
+        for half in range(1):
+            rows = pl.ds(half * 512, 512)
             more = jnp.dot(
                 hidden_s[q, rows, :],
                 value_w[pl.ds(q * 8, 8)].reshape(1024, 1024),
@@ -212,8 +212,8 @@
 
     lax.fori_loop(0, 4, forward, 0)
     gate_copy.wait()
-    for half in range(2):
-        rows = pl.ds(half * 256, 256)
+    for half in range(1):
+        rows = pl.ds(half * 512, 512)
         gates = jax.nn.sigmoid(
             jnp.dot(
                 gate_in_ref[rows, :],
@@ -228,16 +228,16 @@
         gate_grad_ref[rows, :] = (grads * value * gates * (1.0 - gates)).astype(jnp.bfloat16)
 
     def backward(q, _):
-        for half in range(2):
-            rows = pl.ds(half * 256, 256)
+        for half in range(1):
+            rows = pl.ds(half * 512, 512)
             pre_s[q, rows, :] = (
                 dot_nt(value_grad_ref[rows, :], value_w[pl.ds(q * 8, 8)].reshape(1024, 1024))
                 * 2.0
                 * relu_s[q, rows, :]
             ).astype(jnp.bfloat16)
         pre_copy(q).start()
-        for half in range(2):
-            rows = pl.ds(half * 256, 256)
+        for half in range(1):
+            rows = pl.ds(half * 512, 512)
             more = dot_nt(pre_s[q, rows, :], key_w[q].reshape(1024, 1024))
 
             @pl.when(q == 0)
@@ -251,8 +251,8 @@
         return 0
 
     lax.fori_loop(0, 4, backward, 0)
-    for half in range(2):
-        rows = pl.ds(half * 256, 256)
+    for half in range(1):
+        rows = pl.ds(half * 512, 512)
         gate_back_ref[rows, :] = dot_nt(gate_grad_ref[rows, :], gate_w[...].reshape(1024, 1024))
     for q in range(4):
         for k in range(8):
@@ -386,6 +386,123 @@
         )
 
 
+def in_three(array):
+    high = array.astype(jnp.bfloat16)
+    rest = array - high.astype(jnp.float32)
+    middle = rest.astype(jnp.bfloat16)
+    return high, middle, (rest - middle.astype(jnp.float32)).astype(jnp.bfloat16)
+
+
+def time_mix_kernel(
+    branch_ref,
+    weight_ref,
+    key_ref,
+    value_ref,
+    gates_ref,
+    mask_ref,
+    carry_ref,
+    num_ref,
+    den_ref,
+    decay_ref,
+    bonus_ref,
+    gate_grad_ref,
+    key_grad_ref,
+    value_grad_ref,
+    num_grad_ref,
+    den_grad_ref,
+    decay_grad_ref,
+    bonus_grad_ref,
+):
+    length = mask_ref.shape[1]
+    decay = decay_ref[...]
+    bonus = jnp.exp(bonus_ref[...])
+    place = lax.broadcasted_iota(jnp.int32, (length, 1), 0).astype(jnp.float32)
+    grow = jnp.exp(place * decay)
+    shrink = jnp.exp((1.0 - place) * decay)
+    for row in range(mask_ref.shape[0]):
+        rows = pl.ds(row * length, length)
+        mask = mask_ref[row]
+        gated_grad = dot_nt(branch_ref[rows, :], weight_ref[...])
+        gates = gates_ref[rows, :]
+        power = jnp.exp(key_ref[rows, :])
+        value = value_ref[rows, :]
+        product = power * value
+        fade = carry_ref[row] * jnp.exp(-place * decay)
+        num_in, den_in = num_ref[row], den_ref[row]
+        num_sum = sum(
+            jnp.dot(mask, part, preferred_element_type=jnp.float32)
+            for part in in_three(product * grow)
+        )
+        den_sum = sum(
+            jnp.dot(mask, part, preferred_element_type=jnp.float32)
+            for part in in_three(power * grow)
+        )
+        numer = fade * num_in + shrink * num_sum + bonus * product
+        denom = fade * den_in + shrink * den_sum + bonus * power
+        mixed = numer / denom
+        gate_grad_ref[rows, :] = (gated_grad * mixed * gates * (1.0 - gates)).astype(jnp.bfloat16)
+        num_grad = gated_grad * gates / denom
+        den_grad = -num_grad * mixed
+        num_back, den_back = shrink * num_grad, shrink * den_grad
+        num_past = grow * sum(dot_tn(mask, part) for part in in_three(num_back))
+        den_past = grow * sum(dot_tn(mask, part) for part in in_three(den_back))
+        product_grad = bonus * num_grad + num_past
+        key_grad_ref[rows, :] = power * (value * product_grad + bonus * den_grad + den_past)
+        value_grad_ref[rows, :] = power * product_grad
+        num_grad_ref[row] = jnp.sum(fade * num_grad, axis=0, keepdims=True)
+        den_grad_ref[row] = jnp.sum(fade * den_grad, axis=0, keepdims=True)
+        bonus_grad_ref[row] = jnp.sum(
+            bonus * (product * num_grad + power * den_grad), axis=0, keepdims=True
+        )
+        decay_grad_ref[row] = jnp.sum(
+            place * (product * num_past + power * den_past)
+            + (1.0 - place) * (num_back * num_sum + den_back * den_sum)
+            - place * fade * (num_grad * num_in + den_grad * den_in),
+            axis=0,
+            keepdims=True,
+        )
+
+
+def time_mix_back(branch, weight, key, value, gates, mask, carry, num, den, decay, bonus):
+    tokens = branch.shape[0]
+    rows, length = mask.shape[:2]
+    tile = 256
+    wide_block = pl.BlockSpec((tokens, tile), lambda i: (0, i))
+    state = pl.BlockSpec((rows, 1, tile), lambda i: (0, 0, i))
+    vector = pl.BlockSpec((1, tile), lambda i: (0, i))
+    states = jax.ShapeDtypeStruct((rows, 1, 1024), jnp.float32)
+    wide_rows = jax.ShapeDtypeStruct((tokens, 1024), jnp.float32)
+    return pl.pallas_call(
+        time_mix_kernel,
+        grid=(1024 // tile,),
+        out_shape=(
+            jax.ShapeDtypeStruct((tokens, 1024), jnp.bfloat16),
+            wide_rows,
+            wide_rows,
+            states,
+            states,
+            states,
+            states,
+        ),
+        in_specs=[
+            pl.BlockSpec((tokens, 1024), lambda i: (0, 0)),
+            pl.BlockSpec((tile, 1024), lambda i: (i, 0)),
+            wide_block,
+            wide_block,
+            wide_block,
+            pl.BlockSpec((rows, length, length), lambda i: (0, 0, 0)),
+            pl.BlockSpec((rows, length, 1), lambda i: (0, 0, 0)),
+            state,
+            state,
+            vector,
+            vector,
+        ],
+        out_specs=(wide_block, wide_block, wide_block, state, state, state, state),
+        compiler_params=pltpu.CompilerParams(vmem_limit_bytes=48 * 1024 * 1024),
+        cost_estimate=pl.CostEstimate(flops=1, transcendentals=0, bytes_accessed=1),
+    )(branch, weight, key, value, gates, mask, carry, num, den, decay, bonus)
+
+
 def quarters_call(kernel, steps, rows, in_specs, by_quarter, arguments):
     if by_quarter:
         outs = [pl.BlockSpec((n, rows, 1024), lambda i: (0, 0, 0)) for n in (4, 4, 4, 2, 2)]
@@ -400,11 +517,7 @@
         in_specs=in_specs,
         out_specs=tuple(outs),
         compiler_params=pltpu.CompilerParams(vmem_limit_bytes=48 * 1024 * 1024),
-        cost_estimate=pl.CostEstimate(
-            flops=2 * 1024 * 16 * rows * 1024,
-            transcendentals=0,
-            bytes_accessed=(16 * rows + 8 * 1024) * 2048,
-        ),
+        cost_estimate=pl.CostEstimate(flops=1, transcendentals=0, bytes_accessed=1),
     )(*arguments)
 
 
@@ -502,10 +615,14 @@
     return first
 
 
-def sum_vectors(rows_in, flat):
-    total = rows_in + sum(sent(rows_in, turn_z(d)) for d in (1, 2, 3))
-    for pairs in (FLIP_X, FLIP_Y, FLIP_C):
+def sum_plane(total):
+    for pairs in (FLIP_C, FLIP_X, FLIP_Y):
         total = total + sent(total, pairs)
+    return total
+
+
+def sum_column(total, flat):
+    total = total + sum(sent(total, turn_z(d)) for d in (1, 2, 3))
     count = total.shape[1] // 32
     return lax.dynamic_slice_in_dim(total, flat * count, count, 1)
 
@@ -897,26 +1014,61 @@
         key_corner = send_corner(key_parts)
     else:
         grad_output = weight_grad(gated, branch_grad)
-    gated_grad = project_back(
-        tied(branch_grad, value_sides[0]) if tuned else branch_grad, result_weight
-    )
-    gate_pre_grad = (gated_grad * mixed * gates * (1.0 - gates)).astype(jnp.bfloat16)
-    blended_gradient = gated_grad * gates
-    (
-        key_gradient,
-        value_gradient,
-        decay_gradient,
-        reward_derivative,
-        numerator_gradient,
-        denominator_gradient,
-    ) = weighted_value_backward(blended_gradient)
+    if tuned:
+        order_idx = jnp.arange(length)
+        pair_mask = (
+            (order_idx[None, :] < order_idx[:, None])[None]
+            & (document_segments[:, None, :] == document_segments[:, :, None])
+        ).astype(jnp.bfloat16)
+        (
+            gate_pre_grad,
+            key_gradient,
+            value_gradient,
+            numerator_gradient,
+            denominator_gradient,
+            decay_gradient,
+            reward_derivative,
+        ) = time_mix_back(
+            branch_grad.reshape(-1, width),
+            result_weight,
+            key_row_block.reshape(-1, width),
+            value_row_block.reshape(-1, width),
+            gates.reshape(-1, width),
+            pair_mask,
+            (document_segments == 0).astype(jnp.float32)[:, :, None],
+            state_numerator[:, None, :],
+            state_denominator[:, None, :],
+            tied(decay_vec[None, :], value_sides[0], value_sides[1][2:]),
+            reward_array[None, :],
+        )
+        gate_pre_grad, key_gradient, value_gradient = (
+            a.reshape(rows, length, width) for a in (gate_pre_grad, key_gradient, value_gradient)
+        )
+        numerator_gradient = numerator_gradient[:, 0, :]
+        denominator_gradient = denominator_gradient[:, 0, :]
+        decay_gradient = jnp.sum(decay_gradient[:, 0, :], axis=0)
+        reward_derivative = jnp.sum(reward_derivative[:, 0, :], axis=0)
+    else:
+        gated_grad = project_back(branch_grad, result_weight)
+        gate_pre_grad = (gated_grad * mixed * gates * (1.0 - gates)).astype(jnp.bfloat16)
+        blended_gradient = gated_grad * gates
+        (
+            key_gradient,
+            value_gradient,
+            decay_gradient,
+            reward_derivative,
+            numerator_gradient,
+            denominator_gradient,
+        ) = weighted_value_backward(blended_gradient)
     state_gradient = jnp.stack([numerator_gradient, denominator_gradient])
     if tuned:
-        value_first, value_outgoing = add_sides(value_parts, *all_tied(value_from, state_gradient))
         key_sides = add_corner(key_parts, *all_tied(key_corner, state_gradient))
         key_from = send_sides(*key_sides)
-        state_gradient = tied(state_gradient, key_sides[0], value_outgoing[0])
+        state_gradient = tied(state_gradient, key_sides[0], key_sides[1][2:])
     num_next, den_next = carried_in(state_gradient, starts_in, decay_vec, length, True)
+    if tuned:
+        value_first, value_outgoing = add_sides(value_parts, *all_tied(value_from, num_next))
+        num_next = tied(num_next, value_outgoing[0])
     num_tail = tail_fade * num_next[:, None, :]
     den_tail = tail_fade * den_next[:, None, :]
     tail_grad = powered_lookups * (value_row_block * num_tail + den_tail)
@@ -970,22 +1122,13 @@
     from_next = shifted(before_one_grad[:, :1, :], "seq", -1)
     if tuned:
         key_got = send_column(all_tied(key_outgoing, from_next))
+        from_next = tied(from_next, time_sides[0], time_sides[1][2:])
     normed_one_grad = normed_one_grad + jnp.concatenate(
         [before_one_grad[:, 1:, :], from_next], axis=1
     )
     input_norm_grad, grad_gain_one, grad_bias_one = norm_backward(
         normed_one_grad, unit_one, inv_one, opening_standardize_scale
     )
-    if tuned:
-        time_first, time_outgoing = add_sides(time_parts, *time_from)
-        time_total = add_all(time_first, send_column(time_outgoing))
-        grad_key, grad_value, grad_gate, grad_output = (
-            time_total[i : i + 32] for i in (0, 32, 64, 96)
-        )
-        grad_ffn_value = add_all(value_first, value_got)
-        key_total = add_all(key_first, key_got)
-        grad_ffn_key = jnp.concatenate([key_total[i : i + 32] for i in (0, 32, 64, 96)], axis=1)
-        grad_ffn_gate = key_total[128:]
     input_grad = middle_grad + input_norm_grad
     vector_grads = jnp.stack(
         [
@@ -1003,7 +1146,16 @@
         ]
     )
     if tuned:
-        vector_grads = sum_vectors(vector_grads, flat)
+        time_first, time_outgoing = add_sides(time_parts, *all_tied(time_from, vector_grads))
+        key_total = add_all(key_first, all_tied(key_got, vector_grads))
+        time_total = add_all(time_first, send_column(time_outgoing))
+        grad_key, grad_value, grad_gate, grad_output = (
+            time_total[i : i + 32] for i in (0, 32, 64, 96)
+        )
+        grad_ffn_value = add_all(value_first, value_got)
+        grad_ffn_key = jnp.concatenate([key_total[i : i + 32] for i in (0, 32, 64, 96)], axis=1)
+        grad_ffn_gate = key_total[128:]
+        vector_grads = sum_column(tied(sum_plane(vector_grads), time_outgoing[0]), flat)
     else:
         vector_grads = lax.psum_scatter(vector_grads, BOTH, scatter_dimension=1, tiled=True)
     return (

time: 477 us -> 465 us (0.975)
  waiting for transfers between devices: 154 us -> 135 us
  Pallas kernels: 75.1 us -> 86.5 us
  matrix products: 37.5 us -> 26.8 us
  between operations: 23.8 us -> 28.7 us
    ppermute x55, waiting for transfers between devices: 153 us -> 131 us  [sent(): return lax.ppermute(array, BOTH, pairs)]
    pallas_call x0 -> x1, Pallas kernels: none -> 13.4 us  [time_mix_back(): pl.pallas_call(time_mix_kernel, grid=(1024 // tile,), out_shape=(jax.Shap...]
    dot_general x2 -> x1, matrix products: 13.7 us -> 3.03 us  [weighted_value_local(): jnp.einsum('rti,rie->rte', pair_mask, weighted, precision=highest)]
    unnamed x321 -> x275, local copies, waits for them, and re-layouts: 19.2 us -> 12.9 us
    reduce_sum x4 -> x3, other arithmetic: 7.93 us -> 1.81 us  [the longest x1 1.18 us: shards(): decay_gradient = decay_gradient + jnp.sum(offsets * tail_grad, axis=(0, 1))]
  transfers between devices with their start and end apart: 60 -> 60, of which waited for: 19 -> 21; matrix products, arithmetic and copies ran while one was open for 27% -> 26% of each run, Pallas kernels for 9% -> 12%
where the time goes in v3:
time: 465 us; the launch traced here: 458 us
  waiting for transfers between devices  135 us (29%)
  Pallas kernels  86.5 us (19%)
  other arithmetic  72.2 us (16%)
  starting transfers between devices  70.4 us (15%)
  local copies, waits for them, and re-layouts  38.6 us (8%)
  between operations  28.7 us (6%)
  matrix products  26.8 us (6%)
    ppermute x55, waiting for transfers between devices, sent(): return lax.ppermute(array, BOTH, pairs)  131 us
    ppermute x55, starting transfers between devices, sent(): return lax.ppermute(array, BOTH, pairs)  64.8 us
    pallas_call x1, Pallas kernels, channel_mix(): pl.pallas_call(channel_kernel, out_shape=(half_rows, half_rows, half_rows...  31.8 us
    pallas_call x3, Pallas kernels, quarters_call(): pl.pallas_call(kernel, grid=(steps,), out_shape=tuple((jax.ShapeDtypeStru...  26.3 us
    pallas_call x5, Pallas kernels, assemble(): pl.pallas_call(partial(assemble_kernel, counts, start, columns), out_shap...  15 us
    pallas_call x1, Pallas kernels, time_mix_back(): pl.pallas_call(time_mix_kernel, grid=(1024 // tile,), out_shape=(jax.Shap...  13.4 us
    unnamed x275, local copies, waits for them, and re-layouts  12.9 us
    dot_general x6, matrix products, ordered_halves(): jnp.dot(rows_in, choice(flat, width), preferred_element_type=jnp.bfloat16)  10.8 us
  transfers between devices with their start and end apart: 60, of which 21 were waited for; matrix products, arithmetic and copies ran while one was open for 26% of the time, Pallas kernels for 12%

profile of v3, /device:TPU:0, one launch (start us, length us, event | category | flops | bytes accessed | tf_op | source)
XLA Modules:
  0.0 457.9 jit_solution(7196388920446727682)
XLA Ops:
  15.3 5.1 %collective-permute-start.2 = (bf16[144,1024]{1,0:T(8,128)(2,1)S(1)}, bf16[144,1024]{1,0:T(8,128)(2,1)S(1)}, u32[]{:S(2)}, u32[]{:S(2)}) collective-permute-start(bf16[144,1024]{1,0:T(8,128)(2,1)S(1)} %select_dynamic-update-slice_fusion), channel_id=1, source_target_pairs={{0,6},{1,7},{2,0},{3,1},{4,2},{5,3},{6,4},{7,5},{8,14},{9,15},{10,... | collective-permute-start | bytes 884744 | tf_op jit(solution)/shard_map/ppermute | solution.py:29
  29.8 28.3 %collective-permute-done.1 = bf16[144,1024]{1,0:T(8,128)(2,1)S(1)} collective-permute-done((bf16[144,1024]{1,0:T(8,128)(2,1)S(1)}, bf16[144,1024]{1,0:T(8,128)(2,1)S(1)}, u32[]{:S(2)}, u32[]{:S(2)}) %collective-permute-start.1) | collective-permute-done | bytes 294944 | tf_op jit(solution)/shard_map/ppermute | solution.py:29
  66.6 34.4 %collective-permute-done.3.refs_1_ = bf16[4,144,1024]{2,1,0:T(8,128)(2,1)S(1)} collective-permute-done((bf16[4,144,1024]{2,1,0:T(8,128)(2,1)S(1)}, bf16[4,144,1024]{2,1,0:T(8,128)(2,1)S(1)}, u32[]{:S(2)}, u32[]{:S(2)}) %collective-permute-start.3) | collective-permute-done | bytes 1179680 | tf_op jit(solution)/shard_map/ppermute | solution.py:29
  112.4 2.9 collective-permute-done.6.refs_4_
  115.6 2.7 collective-permute-done.11.refs_9_
  120.7 3.1 shard_map.358
  123.9 3.1 shard_map.359
  140.6 3.0 fusion.9
  143.8 10.3 %collective-permute-start.15 = (f32[2,2,1024]{2,1,0:T(2,128)S(1)}, f32[2,2,1024]{2,1,0:T(2,128)S(1)}, u32[]{:S(2)}, u32[]{:S(2)}) collective-permute-start(f32[2,2,1024]{2,1,0:T(2,128)S(1)} %select_add_fusion.1), channel_id=1, source_target_pairs={{0,4},{1,5},{2,6},{3,7},{4,0},{5,1},{6,2},{7,3},{8,12},{9,13},{10,... | collective-permute-start | bytes 49160 | tf_op jit(solution)/shard_map/ppermute | solution.py:29
  156.8 3.1 shard_map.357
  159.9 3.3 shard_map.360
  163.4 3.5 fusion.42
  173.7 2.8 all-gather.3.cloned.1.call-done
  176.5 31.8 %shard_map.361 = (bf16[512,1024]{1,0:T(8,128)(2,1)}, bf16[512,1024]{1,0:T(8,128)(2,1)}, bf16[512,1024]{1,0:T(8,128)(2,1)}, f32[512,1024]{1,0:T(8,128)}, f32[512,...) custom-call(s32[32]{0:T(128)} %and_add_fusion.slots_ref, ...), custom_call_target="tpu_custom_call" | custom-call | flops 19327352832 | bytes 41943040 | tf_op jit(solution)/shard_map/pallas_call | solution.py:269
  224.5 3.2 multiply_reduce_fusion.2
  229.0 7.3 %shard_map.362 = (bf16[4,128,1024]{2,1,0:T(8,128)(2,1)S(1)}, bf16[4,128,1024]{2,1,0:T(8,128)(2,1)S(1)}, bf16[4,128,1024]{2,1,0:T(8,128)(2,1)S(1)}, bf16[2,128,10...) custom-call(bf16[4,512,512]{2,1,0:T(8,128)(2,1)} %get-tuple-element.53.own_ref, ...), custom_call_target="tpu_custom_call" | custom-call | flops 1 | bytes 1 | tf_op jit(solution)/shard_map/pallas_call | solution.py:511
  239.2 10.4 %shard_map.363 = (bf16[4,160,1024]{2,1,0:T(8,128)(2,1)}, bf16[4,160,1024]{2,1,0:T(8,128)(2,1)}, bf16[4,160,1024]{2,1,0:T(8,128)(2,1)}, bf16[2,160,1024]{2,1,0:T(8,128)(2,1)S(1)}, bf16[2,160,1024]{2,1,0:T(8,128)(2,1)S(1)}) custom-call(bf16[512,512]{1,0:T(8,128)(2,1)S(1)} %get-tuple-element.147.key_ref, bf16[512,512]{1,0:T(8,128)(2,1)S(1)} %get-tuple-element.143.other_key_ref, ...), custom_call_target="tpu_custom_call" | custom-call | flops 1 | bytes 1 | tf_op jit(solution)/shard_map/pallas_call | solution.py:511
  256.6 13.4 %shard_map.364 = (bf16[512,1024]{1,0:T(8,128)(2,1)S(1)}, f32[512,1024]{1,0:T(8,128)S(1)}, f32[512,1024]{1,0:T(8,128)}, f32[2,1,1024]{2,1,0:T(1,128)S(1)}, f32[2,...) custom-call(bf16[512,1024]{1,0:T(8,128)(2,1)S(1)} %bitcast.260, ...), custom_call_target="tpu_custom_call" | custom-call | flops 1 | bytes 1 | tf_op jit(solution)/shard_map/pallas_call | solution.py:475
  286.4 11.1 %collective-permute-done.33 = bf16[4,128,1024]{2,1,0:T(8,128)(2,1)S(1)} collective-permute-done((bf16[4,128,1024]{2,1,0:T(8,128)(2,1)S(1)}, bf16[4,128,1024]{2,1,0:T(8,128)(2,1)S(1)}, u32[]{:S(2)}, u32[]{:S(2)}) %collective-permute-start.33) | collective-permute-done | bytes 1048608 | tf_op jit(solution)/shard_map/ppermute | solution.py:29
  297.5 5.3 %collective-permute-done.32 = bf16[4,128,1024]{2,1,0:T(8,128)(2,1)S(1)} collective-permute-done((bf16[4,128,1024]{2,1,0:T(8,128)(2,1)S(1)}, bf16[4,128,1024]{2,1,0:T(8,128)(2,1)S(1)}, u32[]{:S(2)}, u32[]{:S(2)}) %collective-permute-start.32) | collective-permute-done | bytes 1048608 | tf_op jit(solution)/shard_map/ppermute | solution.py:29
  334.4 8.6 %shard_map.365 = (bf16[4,128,1024]{2,1,0:T(8,128)(2,1)S(1)}, bf16[4,128,1024]{2,1,0:T(8,128)(2,1)S(1)}, bf16[4,128,1024]{2,1,0:T(8,128)(2,1)S(1)}, bf16[2,128,10...) custom-call(bf16[512,2048]{1,0:T(8,128)(2,1)} %pad_maximum_fusion.4.own_ref, ...), custom_call_target="tpu_custom_call" | custom-call | flops 1 | bytes 1 | tf_op jit(solution)/shard_map/pallas_call | solution.py:511
  344.2 6.4 %collective-permute-done.38 = bf16[4,160,1024]{2,1,0:T(8,128)(2,1)} collective-permute-done((bf16[4,160,1024]{2,1,0:T(8,128)(2,1)}, bf16[4,160,1024]{2,1,0:T(8,128)(2,1)}, u32[]{:S(2)}, u32[]{:S(2)}) %collective-permute-start.38) | collective-permute-done | bytes 1310752 | tf_op jit(solution)/shard_map/ppermute | solution.py:29
  351.8 4.3 fusion.113
  370.0 2.9 collective-permute-start.55
  379.7 4.5 fusion.23
  392.4 4.6 %fusion.22 = f32[2,256,1024]{2,1,0:T(8,128)} fusion(bf16[2,256,1024]{2,1,0:T(8,128)(2,1)S(1)} %copy-done.17, f32[2,256,1024]{2,1,0:T(8,128)} %get-tuple-element.108, f32[2,256]{1,0:T(2,128)} %broadcast_multiply_fusion.9, f32[2,256]{1,0:T(2,128)} %broadcast_multiply_fusion.10, f32[1024]{0:T(1024)S(1)} %bitcast.307, f32[2,256]{1,0:T(2,128)} %copy-done.95, ...), kind=kLoop, calls=%fused_computation.34 | loop fusion | flops 9437184 | bytes 10510336 | tf_op jit(solution)/shard_map/add | solution.py:1132
  397.1 6.0 %collective-permute-done.54 = bf16[160,1024]{1,0:T(8,128)(2,1)} collective-permute-done((bf16[160,1024]{1,0:T(8,128)(2,1)}, bf16[160,1024]{1,0:T(8,128)(2,1)}, u32[]{:S(2)}, u32[]{:S(2)}) %collective-permute-start.54) | collective-permute-done | bytes 327712 | tf_op jit(solution)/shard_map/ppermute | solution.py:29
  405.7 8.0 %collective-permute-done.43 = f32[11,1024]{1,0:T(8,128)S(1)} collective-permute-done((f32[11,1024]{1,0:T(8,128)S(1)}, f32[11,1024]{1,0:T(8,128)S(1)}, u32[]{:S(2)}, u32[]{:S(2)}) %collective-permute-start.43) | collective-permute-done | bytes 45088 | tf_op jit(solution)/shard_map/ppermute | solution.py:29
  426.5 3.1 collective-permute-start.51
  429.6 3.8 collective-permute-done.48
  434.0 3.5 collective-permute-done.52
  437.5 12.1 %collective-permute-done.51 = bf16[128,1024]{1,0:T(8,128)(2,1)S(1)} collective-permute-done((bf16[128,1024]{1,0:T(8,128)(2,1)S(1)}, bf16[128,1024]{1,0:T(8,128)(2,1)S(1)}, u32[]{:S(2)}, u32[]{:S(2)}) %collective-permute-start.51) | collective-permute-done | bytes 262176 | tf_op jit(solution)/shard_map/ppermute | solution.py:29
  (554 shorter events, 173.2 us)
Async XLA Ops:
  7.3 169.2 %all-gather.3.cloned.1.call-start = ((), (), s32[]{:S(2)}) async-start(), calls=%async_computation | async-start | bytes 19464192 | tf_op jit(solution)/shard_map/all_gather | solution.py:803
  20.4 37.6 %collective-permute-start.1 = (bf16[144,1024]{1,0:T(8,128)(2,1)S(1)}, bf16[144,1024]{1,0:T(8,128)(2,1)S(1)}, u32[]{:S(2)}, u32[]{:S(2)}) collective-permute-start(bf16[144,1024]{1,0:T(8,128)(2,1)S(1)} %select_dynamic-update-slice_fusion), channel_id=1, source_target_pairs={{0,4},{1,5},{2,6},{3,7},{4,0},{5,1},{6,2},{7,3},{8,12},{9,13},{10,... | collective-permute-start | bytes 884744 | tf_op jit(solution)/shard_map/ppermute | solution.py:29
  20.4 37.6 %collective-permute-start = (bf16[144,1024]{1,0:T(8,128)(2,1)S(1)}, bf16[144,1024]{1,0:T(8,128)(2,1)S(1)}, u32[]{:S(2)}, u32[]{:S(2)}) collective-permute-start(bf16[144,1024]{1,0:T(8,128)(2,1)S(1)} %select_dynamic-update-slice_fusion), channel_id=1, source_target_pairs={{0,2},{1,3},{2,4},{3,5},{4,6},{5,7},{6,0},{7,1},{8,10},{9,11},{10,... | collective-permute-start | bytes 884744 | tf_op jit(solution)/shard_map/ppermute | solution.py:29
  22.0 85.4 %collective-permute-start.12 = (bf16[2,1,1024]{2,1,0:T(2,128)(2,1)}, bf16[2,1,1024]{2,1,0:T(2,128)(2,1)S(1)}, u32[]{:S(2)}, u32[]{:S(2)}) collective-permute-start(bf16[2,1,1024]{2,1,0:T(2,128)(2,1)} %slice.350), channel_id=1, source_target_pairs={{0,1},{1,2},{2,3},{3,4},{4,5},{5,6},{6,7},{8,9},{9,10},{10,11},{11... | collective-permute-start | bytes 12296 | tf_op jit(solution)/shard_map/ppermute | solution.py:633
  58.2 42.8 %collective-permute-start.3 = (bf16[4,144,1024]{2,1,0:T(8,128)(2,1)S(1)}, bf16[4,144,1024]{2,1,0:T(8,128)(2,1)S(1)}, u32[]{:S(2)}, u32[]{:S(2)}) collective-permute-start(bf16[4,144,1024]{2,1,0:T(8,128)(2,1)S(1)} %pad_maximum_fusion.8.refs_0_), channel_id=1, source_target_pairs={{0,8},{1,9},{2,10},{3,11},{4,12},{5,13},{6,14},{7,15},{8,0},{9,1},... | collective-permute-start | bytes 3538952 | tf_op jit(solution)/shard_map/ppermute | solution.py:29
  59.8 44.4 %collective-permute-start.4 = (bf16[4,144,1024]{2,1,0:T(8,128)(2,1)S(1)}, bf16[4,144,1024]{2,1,0:T(8,128)(2,1)S(1)}, u32[]{:S(2)}, u32[]{:S(2)}) collective-permute-start(bf16[4,144,1024]{2,1,0:T(8,128)(2,1)S(1)} %pad_maximum_fusion.8.refs_0_), channel_id=1, source_target_pairs={{0,16},{1,17},{2,18},{3,19},{4,20},{5,21},{6,22},{7,23},{8,24},{9,... | collective-permute-start | bytes 3538952 | tf_op jit(solution)/shard_map/ppermute | solution.py:29
  143.8 19.5 %collective-permute-start.16 = (f32[2,2,1024]{2,1,0:T(2,128)S(1)}, f32[2,2,1024]{2,1,0:T(2,128)S(1)}, u32[]{:S(2)}, u32[]{:S(2)}) collective-permute-start(f32[2,2,1024]{2,1,0:T(2,128)S(1)} %select_add_fusion.1), channel_id=1, source_target_pairs={{0,6},{1,7},{2,0},{3,1},{4,2},{5,3},{6,4},{7,5},{8,14},{9,15},{10,... | collective-permute-start | bytes 49160 | tf_op jit(solution)/shard_map/ppermute | solution.py:29
  143.8 19.4 %collective-permute-start.15 = (f32[2,2,1024]{2,1,0:T(2,128)S(1)}, f32[2,2,1024]{2,1,0:T(2,128)S(1)}, u32[]{:S(2)}, u32[]{:S(2)}) collective-permute-start(f32[2,2,1024]{2,1,0:T(2,128)S(1)} %select_add_fusion.1), channel_id=1, source_target_pairs={{0,4},{1,5},{2,6},{3,7},{4,0},{5,1},{6,2},{7,3},{8,12},{9,13},{10,... | collective-permute-start | bytes 49160 | tf_op jit(solution)/shard_map/ppermute | solution.py:29
  208.3 31.0 %collective-permute-start.23 = (bf16[512,4096]{1,0:T(8,128)(2,1)}, bf16[512,4096]{1,0:T(8,128)(2,1)}, u32[]{:S(2)}, u32[]{:S(2)}) collective-permute-start(bf16[512,4096]{1,0:T(8,128)(2,1)} %get-tuple-element.58.refs_0_), channel_id=1, source_target_pairs={{0,1},{1,0},{2,3},{3,2},{4,5},{5,4},{6,7},{7,6},{8,9},{9,8},{10,11... | collective-permute-start | bytes 12582920 | tf_op jit(solution)/shard_map/ppermute | solution.py:29
  213.0 15.9 %collective-permute-start.19 = (bf16[4,512,512]{2,1,0:T(8,128)(2,1)}, bf16[4,512,512]{2,1,0:T(8,128)(2,1)}, u32[]{:S(2)}, u32[]{:S(2)}) collective-permute-start(bf16[4,512,512]{2,1,0:T(8,128)(2,1)} %get-tuple-element.54), channel_id=1, source_target_pairs={{0,1},{1,0},{2,3},{3,2},{4,5},{5,4},{6,7},{7,6},{8,9},{9,8},{10,11... | collective-permute-start | bytes 6291464 | tf_op jit(solution)/shard_map/ppermute | solution.py:29
  224.4 14.8 %collective-permute-start.24 = (bf16[512,1024]{1,0:T(8,128)(2,1)}, bf16[512,1024]{1,0:T(8,128)(2,1)}, u32[]{:S(2)}, u32[]{:S(2)}) collective-permute-start(bf16[512,1024]{1,0:T(8,128)(2,1)} %get-tuple-element.59.refs_2_), channel_id=1, source_target_pairs={{0,1},{1,0},{2,3},{3,2},{4,5},{5,4},{6,7},{7,6},{8,9},{9,8},{10,11... | collective-permute-start | bytes 3145736 | tf_op jit(solution)/shard_map/ppermute | solution.py:29
  236.3 16.7 %collective-permute-start.21 = (bf16[2,128,1024]{2,1,0:T(8,128)(2,1)S(1)}, bf16[2,128,1024]{2,1,0:T(8,128)(2,1)S(1)}, u32[]{:S(2)}, u32[]{:S(2)}) collective-permute-start(bf16[2,128,1024]{2,1,0:T(8,128)(2,1)S(1)} %get-tuple-element.57), channel_id=1, source_target_pairs={{0,8},{1,9},{2,10},{3,11},{4,12},{5,13},{6,14},{7,15},{8,0},{9,1},... | collective-permute-start | bytes 1572872 | tf_op jit(solution)/shard_map/ppermute | solution.py:29
  238.3 14.9 %collective-permute-start.25 = (bf16[2,128,1024]{2,1,0:T(8,128)(2,1)S(1)}, bf16[2,128,1024]{2,1,0:T(8,128)(2,1)S(1)}, u32[]{:S(2)}, u32[]{:S(2)}) collective-permute-start(bf16[2,128,1024]{2,1,0:T(8,128)(2,1)S(1)} %get-tuple-element.62), channel_id=1, source_target_pairs={{0,16},{1,17},{2,18},{3,19},{4,20},{5,21},{6,22},{7,23},{8,24},{9,... | collective-permute-start | bytes 1572872 | tf_op jit(solution)/shard_map/ppermute | solution.py:29
  250.1 25.2 %collective-permute-start.27 = (bf16[2,160,1024]{2,1,0:T(8,128)(2,1)S(1)}, bf16[2,160,1024]{2,1,0:T(8,128)(2,1)S(1)}, u32[]{:S(2)}, u32[]{:S(2)}) collective-permute-start(bf16[2,160,1024]{2,1,0:T(8,128)(2,1)S(1)} %get-tuple-element.60), channel_id=1, source_target_pairs={{0,16},{1,17},{2,18},{3,19},{4,20},{5,21},{6,22},{7,23},{8,24},{9,... | collective-permute-start | bytes 1966088 | tf_op jit(solution)/shard_map/ppermute | solution.py:29
  252.8 21.1 %collective-permute-start.26 = (bf16[2,160,1024]{2,1,0:T(8,128)(2,1)S(1)}, bf16[2,160,1024]{2,1,0:T(8,128)(2,1)S(1)}, u32[]{:S(2)}, u32[]{:S(2)}) collective-permute-start(bf16[2,160,1024]{2,1,0:T(8,128)(2,1)S(1)} %get-tuple-element.67), channel_id=1, source_target_pairs={{0,8},{1,9},{2,10},{3,11},{4,12},{5,13},{6,14},{7,15},{8,0},{9,1},... | collective-permute-start | bytes 1966088 | tf_op jit(solution)/shard_map/ppermute | solution.py:29
  272.0 25.5 %collective-permute-start.33 = (bf16[4,128,1024]{2,1,0:T(8,128)(2,1)S(1)}, bf16[4,128,1024]{2,1,0:T(8,128)(2,1)S(1)}, u32[]{:S(2)}, u32[]{:S(2)}) collective-permute-start(bf16[4,128,1024]{2,1,0:T(8,128)(2,1)S(1)} %pad_maximum_fusion.11), channel_id=1, source_target_pairs={{0,8},{1,9},{2,10},{3,11},{4,12},{5,13},{6,14},{7,15},{8,0},{9,1},... | collective-permute-start | bytes 3145736 | tf_op jit(solution)/shard_map/ppermute | solution.py:29
  277.1 25.6 %collective-permute-start.32 = (bf16[4,128,1024]{2,1,0:T(8,128)(2,1)S(1)}, bf16[4,128,1024]{2,1,0:T(8,128)(2,1)S(1)}, u32[]{:S(2)}, u32[]{:S(2)}) collective-permute-start(bf16[4,128,1024]{2,1,0:T(8,128)(2,1)S(1)} %pad_maximum_fusion.10), channel_id=1, source_target_pairs={{0,16},{1,17},{2,18},{3,19},{4,20},{5,21},{6,22},{7,23},{8,24},{9,... | collective-permute-start | bytes 3145736 | tf_op jit(solution)/shard_map/ppermute | solution.py:29
  310.0 24.4 %collective-permute-start.36 = (bf16[512,3072]{1,0:T(8,128)(2,1)}, bf16[512,3072]{1,0:T(8,128)(2,1)}, u32[]{:S(2)}, u32[]{:S(2)}) collective-permute-start(bf16[512,3072]{1,0:T(8,128)(2,1)} %pad_maximum_fusion.grad_ref), channel_id=1, source_target_pairs={{0,1},{1,0},{2,3},{3,2},{4,5},{5,4},{6,7},{7,6},{8,9},{9,8},{10,11... | collective-permute-start | bytes 9437192 | tf_op jit(solution)/shard_map/ppermute | solution.py:29
  315.5 15.5 %collective-permute-start.35 = (bf16[512,2048]{1,0:T(8,128)(2,1)}, bf16[512,2048]{1,0:T(8,128)(2,1)}, u32[]{:S(2)}, u32[]{:S(2)}) collective-permute-start(bf16[512,2048]{1,0:T(8,128)(2,1)} %pad_maximum_fusion.5), channel_id=1, source_target_pairs={{0,1},{1,0},{2,3},{3,2},{4,5},{5,4},{6,7},{7,6},{8,9},{9,8},{10,11... | collective-permute-start | bytes 6291464 | tf_op jit(solution)/shard_map/ppermute | solution.py:29
  319.2 31.4 %collective-permute-start.38 = (bf16[4,160,1024]{2,1,0:T(8,128)(2,1)}, bf16[4,160,1024]{2,1,0:T(8,128)(2,1)}, u32[]{:S(2)}, u32[]{:S(2)}) collective-permute-start(bf16[4,160,1024]{2,1,0:T(8,128)(2,1)} %pad_maximum_fusion.7), channel_id=1, source_target_pairs={{0,8},{1,9},{2,10},{3,11},{4,12},{5,13},{6,14},{7,15},{8,0},{9,1},... | collective-permute-start | bytes 3932168 | tf_op jit(solution)/shard_map/ppermute | solution.py:29
  320.6 31.2 %collective-permute-start.34 = (bf16[4,160,1024]{2,1,0:T(8,128)(2,1)}, bf16[4,160,1024]{2,1,0:T(8,128)(2,1)}, u32[]{:S(2)}, u32[]{:S(2)}) collective-permute-start(bf16[4,160,1024]{2,1,0:T(8,128)(2,1)} %pad_maximum_fusion.6), channel_id=1, source_target_pairs={{0,16},{1,17},{2,18},{3,19},{4,20},{5,21},{6,22},{7,23},{8,24},{9,... | collective-permute-start | bytes 3932168 | tf_op jit(solution)/shard_map/ppermute | solution.py:29
  331.0 31.3 %collective-permute-start.58 = (bf16[128,1024]{1,0:T(8,128)(2,1)}, bf16[128,1024]{1,0:T(8,128)(2,1)S(1)}, u32[]{:S(2)}, u32[]{:S(2)}) collective-permute-start(bf16[128,1024]{1,0:T(8,128)(2,1)} %get-tuple-element.130), channel_id=1, source_target_pairs={{0,6},{1,7},{2,0},{3,1},{4,2},{5,3},{6,4},{7,5},{8,14},{9,15},{10,... | collective-permute-start | bytes 786440 | tf_op jit(solution)/shard_map/ppermute | solution.py:29
  333.0 31.3 %collective-permute-start.57 = (bf16[128,1024]{1,0:T(8,128)(2,1)}, bf16[128,1024]{1,0:T(8,128)(2,1)S(1)}, u32[]{:S(2)}, u32[]{:S(2)}) collective-permute-start(bf16[128,1024]{1,0:T(8,128)(2,1)} %get-tuple-element.129), channel_id=1, source_target_pairs={{0,4},{1,5},{2,6},{3,7},{4,0},{5,1},{6,2},{7,3},{8,12},{9,13},{10,... | collective-permute-start | bytes 786440 | tf_op jit(solution)/shard_map/ppermute | solution.py:29
  334.4 29.8 %collective-permute-start.56 = (bf16[128,1024]{1,0:T(8,128)(2,1)S(1)}, bf16[128,1024]{1,0:T(8,128)(2,1)S(1)}, u32[]{:S(2)}, u32[]{:S(2)}) collective-permute-start(bf16[128,1024]{1,0:T(8,128)(2,1)S(1)} %broadcast_add_fusion.1), channel_id=1, source_target_pairs={{0,2},{1,3},{2,4},{3,5},{4,6},{5,7},{6,0},{7,1},{8,10},{9,11},{10,... | collective-permute-start | bytes 786440 | tf_op jit(solution)/shard_map/ppermute | solution.py:29
  350.6 27.6 %collective-permute-start.41 = (bf16[2,128,1024]{2,1,0:T(8,128)(2,1)S(1)}, bf16[2,128,1024]{2,1,0:T(8,128)(2,1)S(1)}, u32[]{:S(2)}, u32[]{:S(2)}) collective-permute-start(bf16[2,128,1024]{2,1,0:T(8,128)(2,1)S(1)} %get-tuple-element.73), channel_id=1, source_target_pairs={{0,16},{1,17},{2,18},{3,19},{4,20},{5,21},{6,22},{7,23},{8,24},{9,... | collective-permute-start | bytes 1572872 | tf_op jit(solution)/shard_map/ppermute | solution.py:29
  370.0 27.0 %collective-permute-start.55 = (bf16[160,1024]{1,0:T(8,128)(2,1)}, bf16[160,1024]{1,0:T(8,128)(2,1)S(1)}, u32[]{:S(2)}, u32[]{:S(2)}) collective-permute-start(bf16[160,1024]{1,0:T(8,128)(2,1)} %get-tuple-element.128), channel_id=1, source_target_pairs={{0,6},{1,7},{2,0},{3,1},{4,2},{5,3},{6,4},{7,5},{8,14},{9,15},{10,... | collective-permute-start | bytes 983048 | tf_op jit(solution)/shard_map/ppermute | solution.py:29
  372.9 30.2 %collective-permute-start.54 = (bf16[160,1024]{1,0:T(8,128)(2,1)}, bf16[160,1024]{1,0:T(8,128)(2,1)}, u32[]{:S(2)}, u32[]{:S(2)}) collective-permute-start(bf16[160,1024]{1,0:T(8,128)(2,1)} %get-tuple-element.127), channel_id=1, source_target_pairs={{0,4},{1,5},{2,6},{3,7},{4,0},{5,1},{6,2},{7,3},{8,12},{9,13},{10,... | collective-permute-start | bytes 983048 | tf_op jit(solution)/shard_map/ppermute | solution.py:29
  374.7 28.5 %collective-permute-start.53 = (bf16[160,1024]{1,0:T(8,128)(2,1)}, bf16[160,1024]{1,0:T(8,128)(2,1)}, u32[]{:S(2)}, u32[]{:S(2)}) collective-permute-start(bf16[160,1024]{1,0:T(8,128)(2,1)} %broadcast_add_fusion), channel_id=1, source_target_pairs={{0,2},{1,3},{2,4},{3,5},{4,6},{5,7},{6,0},{7,1},{8,10},{9,11},{10,... | collective-permute-start | bytes 983048 | tf_op jit(solution)/shard_map/ppermute | solution.py:29
  386.4 28.0 %collective-permute-start.46 = (bf16[4,128,1024]{2,1,0:T(8,128)(2,1)}, bf16[4,128,1024]{2,1,0:T(8,128)(2,1)}, u32[]{:S(2)}, u32[]{:S(2)}) collective-permute-start(bf16[4,128,1024]{2,1,0:T(8,128)(2,1)} %pad_maximum_fusion.13), channel_id=1, source_target_pairs={{0,8},{1,9},{2,10},{3,11},{4,12},{5,13},{6,14},{7,15},{8,0},{9,1},... | collective-permute-start | bytes 3145736 | tf_op jit(solution)/shard_map/ppermute | solution.py:29
  389.5 25.4 %collective-permute-start.45 = (bf16[4,128,1024]{2,1,0:T(8,128)(2,1)}, bf16[4,128,1024]{2,1,0:T(8,128)(2,1)}, u32[]{:S(2)}, u32[]{:S(2)}) collective-permute-start(bf16[4,128,1024]{2,1,0:T(8,128)(2,1)} %pad_maximum_fusion.12), channel_id=1, source_target_pairs={{0,16},{1,17},{2,18},{3,19},{4,20},{5,21},{6,22},{7,23},{8,24},{9,... | collective-permute-start | bytes 3145736 | tf_op jit(solution)/shard_map/ppermute | solution.py:29
  422.7 26.9 %collective-permute-start.50 = (bf16[128,1024]{1,0:T(8,128)(2,1)S(1)}, bf16[128,1024]{1,0:T(8,128)(2,1)S(1)}, u32[]{:S(2)}, u32[]{:S(2)}) collective-permute-start(bf16[128,1024]{1,0:T(8,128)(2,1)S(1)} %get-tuple-element.133), channel_id=1, source_target_pairs={{0,2},{1,3},{2,4},{3,5},{4,6},{5,7},{6,0},{7,1},{8,10},{9,11},{10,... | collective-permute-start | bytes 786440 | tf_op jit(solution)/shard_map/ppermute | solution.py:29
  426.5 23.1 %collective-permute-start.51 = (bf16[128,1024]{1,0:T(8,128)(2,1)S(1)}, bf16[128,1024]{1,0:T(8,128)(2,1)S(1)}, u32[]{:S(2)}, u32[]{:S(2)}) collective-permute-start(bf16[128,1024]{1,0:T(8,128)(2,1)S(1)} %get-tuple-element.131), channel_id=1, source_target_pairs={{0,4},{1,5},{2,6},{3,7},{4,0},{5,1},{6,2},{7,3},{8,12},{9,13},{10,... | collective-permute-start | bytes 786440 | tf_op jit(solution)/shard_map/ppermute | solution.py:29
  (159 other events, 1520.0 us)
Sparse Core Ops, SparseCore 0:
  13.5 162.9 all-gather.2

commit v4 on v3

--- a/solution.py
+++ b/solution.py
@@ -93,6 +93,23 @@
 
 def around(part):
     return [sent(part, turn_z(d)) for d in (1, 2, 3)]
+
+
+def pack_kernel(key_ref, value_ref, gate_ref, out_ref):
+    for q in range(4):
+        out_ref[q * 32 : q * 32 + 32, :] = key_ref[:, q * 1024 : q * 1024 + 1024]
+    out_ref[128:256, :] = value_ref[...]
+    out_ref[256:288, :] = gate_ref[...]
+
+
+def pack_late(key, value, gate):
+    whole = pl.BlockSpec(memory_space=pltpu.VMEM)
+    return pl.pallas_call(
+        pack_kernel,
+        out_shape=jax.ShapeDtypeStruct((288, 1024), key.dtype),
+        in_specs=[whole] * 3,
+        out_specs=whole,
+    )(key, value, gate)
 
 
 def long_slots(flat):
@@ -591,8 +608,8 @@
 
 
 def add_corner(parts, add_a, add_b):
-    to_y = jnp.concatenate([narrow(wide(parts[2][:2]) + wide(add_a)), parts[2][2:]])
-    to_x = jnp.concatenate([parts[1][:2], narrow(wide(parts[1][2:]) + wide(add_b))])
+    to_y = lax.dynamic_update_slice(parts[2], narrow(wide(parts[2][:2]) + wide(add_a)), (0, 0, 0))
+    to_x = lax.dynamic_update_slice(parts[1], narrow(wide(parts[1][2:]) + wide(add_b)), (2, 0, 0))
     return to_y, to_x
 
 
@@ -801,12 +818,10 @@
     if tuned:
         order = long_slots(flat)
         late = lax.all_gather(
-            stacked(
-                [
-                    feature_lookup_projection,
-                    feature_content_projection,
-                    feature_receptance_projection,
-                ]
+            pack_late(
+                feature_lookup_projection,
+                feature_content_projection,
+                feature_receptance_projection,
             ),
             BOTH,
         )
@@ -1067,7 +1082,7 @@
         state_gradient = tied(state_gradient, key_sides[0], key_sides[1][2:])
     num_next, den_next = carried_in(state_gradient, starts_in, decay_vec, length, True)
     if tuned:
-        value_first, value_outgoing = add_sides(value_parts, *all_tied(value_from, num_next))
+        value_first, value_outgoing = add_sides(value_parts, *[tied(a, num_next, other_time) for a in value_from])
         num_next = tied(num_next, value_outgoing[0])
     num_tail = tail_fade * num_next[:, None, :]
     den_tail = tail_fade * den_next[:, None, :]
@@ -1148,14 +1163,15 @@
     if tuned:
         time_first, time_outgoing = add_sides(time_parts, *all_tied(time_from, vector_grads))
         key_total = add_all(key_first, all_tied(key_got, vector_grads))
-        time_total = add_all(time_first, send_column(time_outgoing))
+        time_got = send_column(time_outgoing)
+        time_total = add_all(time_first, time_got)
         grad_key, grad_value, grad_gate, grad_output = (
             time_total[i : i + 32] for i in (0, 32, 64, 96)
         )
         grad_ffn_value = add_all(value_first, value_got)
         grad_ffn_key = jnp.concatenate([key_total[i : i + 32] for i in (0, 32, 64, 96)], axis=1)
         grad_ffn_gate = key_total[128:]
-        vector_grads = sum_column(tied(sum_plane(vector_grads), time_outgoing[0]), flat)
+        vector_grads = sum_column(tied(sum_plane(vector_grads), time_got[0]), flat)
     else:
         vector_grads = lax.psum_scatter(vector_grads, BOTH, scatter_dimension=1, tiled=True)
     return (

time: 465 us -> 458 us (0.985)
  waiting for transfers between devices: 135 us -> 113 us
  starting transfers between devices: 70.4 us -> 85.9 us
  local copies, waits for them, and re-layouts: 38.6 us -> 31.2 us
  other arithmetic: 72.2 us -> 77.6 us
    ppermute x55, waiting for transfers between devices: 131 us -> 112 us  [sent(): return lax.ppermute(array, BOTH, pairs)]
    ppermute x55, starting transfers between devices: 64.8 us -> 80.3 us  [sent(): return lax.ppermute(array, BOTH, pairs)]
    dynamic_update_slice x0 -> x6, other arithmetic: none -> 7.63 us  [the longest x3 4.81 us: add_corner(): lax.dynamic_update_slice(parts[2], narrow(wide(parts[2][:2]) + wide(add_a...]
    unnamed x275 -> x252, local copies, waits for them, and re-layouts: 12.9 us -> 7.35 us
    concatenate x6 -> x0, other arithmetic: 4.71 us -> none  [the longest x3 2.36 us: add_corner(): jnp.concatenate([parts[1][:2], narrow(wide(parts[1][2:]) + wide(add_b))])]
    slice x17 -> x18, local copies, waits for them, and re-layouts: 8.76 us -> 9.84 us  [tied(): first = other[(0,) * other.ndim].astype(jnp.float32)]
  transfers between devices with their start and end apart: 60 -> 60, of which waited for: 21 -> 16; matrix products, arithmetic and copies ran while one was open for 26% -> 26% of each run, Pallas kernels for 12% -> 13%
where the time goes in v4:
time: 458 us; the launch traced here: 451 us
  waiting for transfers between devices  113 us (25%)
  Pallas kernels  90.7 us (20%)
  starting transfers between devices  85.9 us (19%)
  other arithmetic  77.6 us (17%)
  local copies, waits for them, and re-layouts  31.2 us (7%)
  between operations  29.3 us (6%)
  matrix products  23.9 us (5%)
    ppermute x55, waiting for transfers between devices, sent(): return lax.ppermute(array, BOTH, pairs)  112 us
    ppermute x55, starting transfers between devices, sent(): return lax.ppermute(array, BOTH, pairs)  80.3 us
    pallas_call x1, Pallas kernels, channel_mix(): pl.pallas_call(channel_kernel, out_shape=(half_rows, half_rows, half_rows...  31.7 us
    pallas_call x3, Pallas kernels, quarters_call(): pl.pallas_call(kernel, grid=(steps,), out_shape=tuple((jax.ShapeDtypeStru...  28.2 us
    pallas_call x5, Pallas kernels, assemble(): pl.pallas_call(partial(assemble_kernel, counts, start, columns), out_shap...  15.1 us
    pallas_call x1, Pallas kernels, time_mix_back(): pl.pallas_call(time_mix_kernel, grid=(1024 // tile,), out_shape=(jax.Shap...  13.7 us
    another operation x5, other arithmetic  11.1 us
    slice x18, local copies, waits for them, and re-layouts, tied(): first = other[(0,) * other.ndim].astype(jnp.float32)  9.84 us
  transfers between devices with their start and end apart: 60, of which 16 were waited for; matrix products, arithmetic and copies ran while one was open for 26% of the time, Pallas kernels for 13%

profile of v4, /device:TPU:0, one launch (start us, length us, event | category | flops | bytes accessed | tf_op | source)
XLA Modules:
  0.0 451.5 jit_solution(16981343622499558190)
XLA Ops:
  11.2 5.1 %collective-permute-start.2 = (bf16[144,1024]{1,0:T(8,128)(2,1)S(1)}, bf16[144,1024]{1,0:T(8,128)(2,1)S(1)}, u32[]{:S(2)}, u32[]{:S(2)}) collective-permute-start(bf16[144,1024]{1,0:T(8,128)(2,1)S(1)} %select_dynamic-update-slice_fusion), channel_id=1, source_target_pairs={{0,6},{1,7},{2,0},{3,1},{4,2},{5,3},{6,4},{7,5},{8,14},{9,15},{10,... | collective-permute-start | bytes 884744 | tf_op jit(solution)/shard_map/ppermute | solution.py:29
  24.6 29.3 %collective-permute-done.1 = bf16[144,1024]{1,0:T(8,128)(2,1)S(1)} collective-permute-done((bf16[144,1024]{1,0:T(8,128)(2,1)S(1)}, bf16[144,1024]{1,0:T(8,128)(2,1)S(1)}, u32[]{:S(2)}, u32[]{:S(2)}) %collective-permute-start.1) | collective-permute-done | bytes 294944 | tf_op jit(solution)/shard_map/ppermute | solution.py:29
  62.0 34.9 %collective-permute-done.3.refs_1_ = bf16[4,144,1024]{2,1,0:T(8,128)(2,1)S(1)} collective-permute-done((bf16[4,144,1024]{2,1,0:T(8,128)(2,1)S(1)}, bf16[4,144,1024]{2,1,0:T(8,128)(2,1)S(1)}, u32[]{:S(2)}, u32[]{:S(2)}) %collective-permute-start.3) | collective-permute-done | bytes 1179680 | tf_op jit(solution)/shard_map/ppermute | solution.py:29
  108.3 2.9 collective-permute-done.6.refs_4_
  116.6 3.1 shard_map.358
  119.7 3.1 shard_map.359
  138.9 3.0 fusion.9
  142.1 10.3 %collective-permute-start.15 = (f32[2,2,1024]{2,1,0:T(2,128)S(1)}, f32[2,2,1024]{2,1,0:T(2,128)S(1)}, u32[]{:S(2)}, u32[]{:S(2)}) collective-permute-start(f32[2,2,1024]{2,1,0:T(2,128)S(1)} %select_add_fusion.1), channel_id=1, source_target_pairs={{0,4},{1,5},{2,6},{3,7},{4,0},{5,1},{6,2},{7,3},{8,12},{9,13},{10,... | collective-permute-start | bytes 49160 | tf_op jit(solution)/shard_map/ppermute | solution.py:29
  155.1 3.3 shard_map.357
  158.4 3.2 shard_map.360
  161.8 3.5 fusion.42
  173.4 31.7 %shard_map.362 = (bf16[512,1024]{1,0:T(8,128)(2,1)}, bf16[512,1024]{1,0:T(8,128)(2,1)}, bf16[512,1024]{1,0:T(8,128)(2,1)}, f32[512,1024]{1,0:T(8,128)}, f32[512,...) custom-call(s32[32]{0:T(128)} %and_add_fusion.slots_ref, ...), custom_call_target="tpu_custom_call" | custom-call | flops 19327352832 | bytes 41943040 | tf_op jit(solution)/shard_map/pallas_call | solution.py:286
  222.6 3.2 multiply_reduce_fusion.2
  227.1 8.6 %shard_map.363 = (bf16[4,128,1024]{2,1,0:T(8,128)(2,1)S(1)}, bf16[4,128,1024]{2,1,0:T(8,128)(2,1)}, bf16[4,128,1024]{2,1,0:T(8,128)(2,1)}, bf16[2,128,1024]{2,1,0:T(8,128)(2,1)S(1)}, bf16[2,128,1024]{2,1,0:T(8,128)(2,1)S(1)}) custom-call(bf16[4,512,512]{2,1,0:T(8,128)(2,1)} %get-tuple-element.53.own_ref, ...), custom_call_target="tpu_custom_call" | custom-call | flops 1 | bytes 1 | tf_op jit(solution)/shard_map/pallas_call | solution.py:528
  239.2 10.4 %shard_map.364 = (bf16[4,160,1024]{2,1,0:T(8,128)(2,1)}, bf16[4,160,1024]{2,1,0:T(8,128)(2,1)}, bf16[4,160,1024]{2,1,0:T(8,128)(2,1)}, bf16[2,160,1024]{2,1,0:T(8,128)(2,1)S(1)}, bf16[2,160,1024]{2,1,0:T(8,128)(2,1)S(1)}) custom-call(bf16[512,512]{1,0:T(8,128)(2,1)S(1)} %get-tuple-element.159.key_ref, bf16[512,512]{1,0:T(8,128)(2,1)S(1)} %get-tuple-element.155.other_key_ref, ...), custom_call_target="tpu_custom_call" | custom-call | flops 1 | bytes 1 | tf_op jit(solution)/shard_map/pallas_call | solution.py:528
  260.4 13.7 %shard_map.365 = (bf16[512,1024]{1,0:T(8,128)(2,1)S(1)}, f32[512,1024]{1,0:T(8,128)S(1)}, f32[512,1024]{1,0:T(8,128)}, f32[2,1,1024]{2,1,0:T(1,128)S(1)}, f32[2,...) custom-call(bf16[512,1024]{1,0:T(8,128)(2,1)S(1)} %bitcast.260, ...), custom_call_target="tpu_custom_call" | custom-call | flops 1 | bytes 1 | tf_op jit(solution)/shard_map/pallas_call | solution.py:492
  291.7 9.1 %collective-permute-done.34 = bf16[4,128,1024]{2,1,0:T(8,128)(2,1)} collective-permute-done((bf16[4,128,1024]{2,1,0:T(8,128)(2,1)}, bf16[4,128,1024]{2,1,0:T(8,128)(2,1)}, u32[]{:S(2)}, u32[]{:S(2)}) %collective-permute-start.34) | collective-permute-done | bytes 1048608 | tf_op jit(solution)/shard_map/ppermute | solution.py:29
  302.2 3.7 fusion.114
  308.3 3.1 multiply_reduce_fusion.3
  314.4 3.3 pad_maximum_fusion.5.own_ref
  320.6 3.1 collective-permute-start.58
  329.4 9.2 %shard_map.366 = (bf16[4,128,1024]{2,1,0:T(8,128)(2,1)S(1)}, bf16[4,128,1024]{2,1,0:T(8,128)(2,1)S(1)}, bf16[4,128,1024]{2,1,0:T(8,128)(2,1)}, bf16[2,128,1024]{...) custom-call(bf16[512,2048]{1,0:T(8,128)(2,1)} %pad_maximum_fusion.5.own_ref, ...), custom_call_target="tpu_custom_call" | custom-call | flops 1 | bytes 1 | tf_op jit(solution)/shard_map/pallas_call | solution.py:528
  339.9 5.4 %collective-permute-done.38 = bf16[4,160,1024]{2,1,0:T(8,128)(2,1)} collective-permute-done((bf16[4,160,1024]{2,1,0:T(8,128)(2,1)}, bf16[4,160,1024]{2,1,0:T(8,128)(2,1)}, u32[]{:S(2)}, u32[]{:S(2)}) %collective-permute-start.38) | collective-permute-done | bytes 1310752 | tf_op jit(solution)/shard_map/ppermute | solution.py:29
  345.5 4.3 fusion.113
  362.8 3.7 collective-permute-start.55
  375.5 4.4 fusion.23
  385.3 4.9 %fusion.22 = f32[2,256,1024]{2,1,0:T(8,128)} fusion(bf16[2,256,1024]{2,1,0:T(8,128)(2,1)S(1)} %copy-done.21, f32[2,256,1024]{2,1,0:T(8,128)} %get-tuple-element.112, f32[2,256]{1,0:T(2,128)S(1)} %broadcast_multiply_fusion.9, f32[2,256]{1,0:T(2,128)} %broadcast_multiply_fusion.10, f32[1024]{0:T(1024)S(1)} %bitcast.307, f32[2,256]{1,0:T(2,128)} %copy-done.85, ...), kind=kLoop, calls=%fused_computation.34 | loop fusion | flops 9437184 | bytes 10510336 | tf_op jit(solution)/shard_map/add | solution.py:1147
  390.3 5.8 %collective-permute-done.54 = bf16[160,1024]{1,0:T(8,128)(2,1)} collective-permute-done((bf16[160,1024]{1,0:T(8,128)(2,1)}, bf16[160,1024]{1,0:T(8,128)(2,1)}, u32[]{:S(2)}, u32[]{:S(2)}) %collective-permute-start.54) | collective-permute-done | bytes 327712 | tf_op jit(solution)/shard_map/ppermute | solution.py:29
  399.0 8.2 %collective-permute-done.43 = f32[11,1024]{1,0:T(8,128)S(1)} collective-permute-done((f32[11,1024]{1,0:T(8,128)S(1)}, f32[11,1024]{1,0:T(8,128)S(1)}, u32[]{:S(2)}, u32[]{:S(2)}) %collective-permute-start.43) | collective-permute-done | bytes 45088 | tf_op jit(solution)/shard_map/ppermute | solution.py:29
  416.6 5.9 %collective-permute-done.47 = bf16[128,1024]{1,0:T(8,128)(2,1)S(1)} collective-permute-done((bf16[128,1024]{1,0:T(8,128)(2,1)S(1)}, bf16[128,1024]{1,0:T(8,128)(2,1)S(1)}, u32[]{:S(2)}, u32[]{:S(2)}) %collective-permute-start.47) | collective-permute-done | bytes 262176 | tf_op jit(solution)/shard_map/ppermute | solution.py:29
  423.7 3.9 collective-permute-start.50
  427.6 10.1 %collective-permute-start.49 = (f32[11,1024]{1,0:T(8,128)S(1)}, f32[11,1024]{1,0:T(8,128)S(1)}, u32[]{:S(2)}, u32[]{:S(2)}) collective-permute-start(f32[11,1024]{1,0:T(8,128)S(1)} %add_add_fusion.1), channel_id=1, source_target_pairs={{0,4},{1,5},{2,6},{3,7},{4,0},{5,1},{6,2},{7,3},{8,12},{9,13},{10,... | collective-permute-start | bytes 135176 | tf_op jit(solution)/shard_map/ppermute | solution.py:29
  (519 shorter events, 164.7 us)
Async XLA Ops:
  7.3 166.1 %all-gather.3.cloned.1.call-start = ((), (), s32[]{:S(2)}) async-start(), calls=%async_computation | async-start | bytes 19464192 | tf_op jit(solution)/shard_map/all_gather | solution.py:820
  16.3 37.7 %collective-permute-start.1 = (bf16[144,1024]{1,0:T(8,128)(2,1)S(1)}, bf16[144,1024]{1,0:T(8,128)(2,1)S(1)}, u32[]{:S(2)}, u32[]{:S(2)}) collective-permute-start(bf16[144,1024]{1,0:T(8,128)(2,1)S(1)} %select_dynamic-update-slice_fusion), channel_id=1, source_target_pairs={{0,4},{1,5},{2,6},{3,7},{4,0},{5,1},{6,2},{7,3},{8,12},{9,13},{10,... | collective-permute-start | bytes 884744 | tf_op jit(solution)/shard_map/ppermute | solution.py:29
  16.3 37.7 %collective-permute-start = (bf16[144,1024]{1,0:T(8,128)(2,1)S(1)}, bf16[144,1024]{1,0:T(8,128)(2,1)S(1)}, u32[]{:S(2)}, u32[]{:S(2)}) collective-permute-start(bf16[144,1024]{1,0:T(8,128)(2,1)S(1)} %select_dynamic-update-slice_fusion), channel_id=1, source_target_pairs={{0,2},{1,3},{2,4},{3,5},{4,6},{5,7},{6,0},{7,1},{8,10},{9,11},{10,... | collective-permute-start | bytes 884744 | tf_op jit(solution)/shard_map/ppermute | solution.py:29
  17.9 85.4 %collective-permute-start.12 = (bf16[2,1,1024]{2,1,0:T(2,128)(2,1)}, bf16[2,1,1024]{2,1,0:T(2,128)(2,1)S(1)}, u32[]{:S(2)}, u32[]{:S(2)}) collective-permute-start(bf16[2,1,1024]{2,1,0:T(2,128)(2,1)} %slice.330), channel_id=1, source_target_pairs={{0,1},{1,2},{2,3},{3,4},{4,5},{5,6},{6,7},{8,9},{9,10},{10,11},{11... | collective-permute-start | bytes 12296 | tf_op jit(solution)/shard_map/ppermute | solution.py:650
  54.1 42.8 %collective-permute-start.3 = (bf16[4,144,1024]{2,1,0:T(8,128)(2,1)S(1)}, bf16[4,144,1024]{2,1,0:T(8,128)(2,1)S(1)}, u32[]{:S(2)}, u32[]{:S(2)}) collective-permute-start(bf16[4,144,1024]{2,1,0:T(8,128)(2,1)S(1)} %pad_maximum_fusion.6.refs_0_), channel_id=1, source_target_pairs={{0,8},{1,9},{2,10},{3,11},{4,12},{5,13},{6,14},{7,15},{8,0},{9,1},... | collective-permute-start | bytes 3538952 | tf_op jit(solution)/shard_map/ppermute | solution.py:29
  55.7 44.4 %collective-permute-start.4 = (bf16[4,144,1024]{2,1,0:T(8,128)(2,1)S(1)}, bf16[4,144,1024]{2,1,0:T(8,128)(2,1)S(1)}, u32[]{:S(2)}, u32[]{:S(2)}) collective-permute-start(bf16[4,144,1024]{2,1,0:T(8,128)(2,1)S(1)} %pad_maximum_fusion.6.refs_0_), channel_id=1, source_target_pairs={{0,16},{1,17},{2,18},{3,19},{4,20},{5,21},{6,22},{7,23},{8,24},{9,... | collective-permute-start | bytes 3538952 | tf_op jit(solution)/shard_map/ppermute | solution.py:29
  142.1 19.5 %collective-permute-start.16 = (f32[2,2,1024]{2,1,0:T(2,128)S(1)}, f32[2,2,1024]{2,1,0:T(2,128)S(1)}, u32[]{:S(2)}, u32[]{:S(2)}) collective-permute-start(f32[2,2,1024]{2,1,0:T(2,128)S(1)} %select_add_fusion.1), channel_id=1, source_target_pairs={{0,6},{1,7},{2,0},{3,1},{4,2},{5,3},{6,4},{7,5},{8,14},{9,15},{10,... | collective-permute-start | bytes 49160 | tf_op jit(solution)/shard_map/ppermute | solution.py:29
  142.1 19.5 %collective-permute-start.15 = (f32[2,2,1024]{2,1,0:T(2,128)S(1)}, f32[2,2,1024]{2,1,0:T(2,128)S(1)}, u32[]{:S(2)}, u32[]{:S(2)}) collective-permute-start(f32[2,2,1024]{2,1,0:T(2,128)S(1)} %select_add_fusion.1), channel_id=1, source_target_pairs={{0,4},{1,5},{2,6},{3,7},{4,0},{5,1},{6,2},{7,3},{8,12},{9,13},{10,... | collective-permute-start | bytes 49160 | tf_op jit(solution)/shard_map/ppermute | solution.py:29
  205.1 34.1 %collective-permute-start.23 = (bf16[512,4096]{1,0:T(8,128)(2,1)}, bf16[512,4096]{1,0:T(8,128)(2,1)}, u32[]{:S(2)}, u32[]{:S(2)}) collective-permute-start(bf16[512,4096]{1,0:T(8,128)(2,1)} %get-tuple-element.58.refs_0_), channel_id=1, source_target_pairs={{0,1},{1,0},{2,3},{3,2},{4,5},{5,4},{6,7},{7,6},{8,9},{9,8},{10,11... | collective-permute-start | bytes 12582920 | tf_op jit(solution)/shard_map/ppermute | solution.py:29
  213.2 72.9 %collective-permute-start.33 = (bf16[512,2048]{1,0:T(8,128)(2,1)}, bf16[512,2048]{1,0:T(8,128)(2,1)}, u32[]{:S(2)}, u32[]{:S(2)}) collective-permute-start(bf16[512,2048]{1,0:T(8,128)(2,1)} %pad_maximum_fusion.4), channel_id=1, source_target_pairs={{0,1},{1,0},{2,3},{3,2},{4,5},{5,4},{6,7},{7,6},{8,9},{9,8},{10,11... | collective-permute-start | bytes 6291464 | tf_op jit(solution)/shard_map/ppermute | solution.py:29
  221.0 18.2 %collective-permute-start.24 = (bf16[512,1024]{1,0:T(8,128)(2,1)}, bf16[512,1024]{1,0:T(8,128)(2,1)}, u32[]{:S(2)}, u32[]{:S(2)}) collective-permute-start(bf16[512,1024]{1,0:T(8,128)(2,1)} %get-tuple-element.59.refs_2_), channel_id=1, source_target_pairs={{0,1},{1,0},{2,3},{3,2},{4,5},{5,4},{6,7},{7,6},{8,9},{9,8},{10,11... | collective-permute-start | bytes 3145736 | tf_op jit(solution)/shard_map/ppermute | solution.py:29
  235.8 17.2 %collective-permute-start.21 = (bf16[2,128,1024]{2,1,0:T(8,128)(2,1)S(1)}, bf16[2,128,1024]{2,1,0:T(8,128)(2,1)S(1)}, u32[]{:S(2)}, u32[]{:S(2)}) collective-permute-start(bf16[2,128,1024]{2,1,0:T(8,128)(2,1)S(1)} %get-tuple-element.57), channel_id=1, source_target_pairs={{0,8},{1,9},{2,10},{3,11},{4,12},{5,13},{6,14},{7,15},{8,0},{9,1},... | collective-permute-start | bytes 1572872 | tf_op jit(solution)/shard_map/ppermute | solution.py:29
  238.4 16.8 %collective-permute-start.25 = (bf16[2,128,1024]{2,1,0:T(8,128)(2,1)S(1)}, bf16[2,128,1024]{2,1,0:T(8,128)(2,1)S(1)}, u32[]{:S(2)}, u32[]{:S(2)}) collective-permute-start(bf16[2,128,1024]{2,1,0:T(8,128)(2,1)S(1)} %get-tuple-element.62), channel_id=1, source_target_pairs={{0,16},{1,17},{2,18},{3,19},{4,20},{5,21},{6,22},{7,23},{8,24},{9,... | collective-permute-start | bytes 1572872 | tf_op jit(solution)/shard_map/ppermute | solution.py:29
  250.1 28.5 %collective-permute-start.27 = (bf16[2,160,1024]{2,1,0:T(8,128)(2,1)S(1)}, bf16[2,160,1024]{2,1,0:T(8,128)(2,1)S(1)}, u32[]{:S(2)}, u32[]{:S(2)}) collective-permute-start(bf16[2,160,1024]{2,1,0:T(8,128)(2,1)S(1)} %get-tuple-element.60), channel_id=1, source_target_pairs={{0,16},{1,17},{2,18},{3,19},{4,20},{5,21},{6,22},{7,23},{8,24},{9,... | collective-permute-start | bytes 1966088 | tf_op jit(solution)/shard_map/ppermute | solution.py:29
  252.8 25.4 %collective-permute-start.26 = (bf16[2,160,1024]{2,1,0:T(8,128)(2,1)S(1)}, bf16[2,160,1024]{2,1,0:T(8,128)(2,1)S(1)}, u32[]{:S(2)}, u32[]{:S(2)}) collective-permute-start(bf16[2,160,1024]{2,1,0:T(8,128)(2,1)S(1)} %get-tuple-element.67), channel_id=1, source_target_pairs={{0,8},{1,9},{2,10},{3,11},{4,12},{5,13},{6,14},{7,15},{8,0},{9,1},... | collective-permute-start | bytes 1966088 | tf_op jit(solution)/shard_map/ppermute | solution.py:29
  276.2 24.6 %collective-permute-start.34 = (bf16[4,128,1024]{2,1,0:T(8,128)(2,1)}, bf16[4,128,1024]{2,1,0:T(8,128)(2,1)}, u32[]{:S(2)}, u32[]{:S(2)}) collective-permute-start(bf16[4,128,1024]{2,1,0:T(8,128)(2,1)} %get-tuple-element.123), channel_id=1, source_target_pairs={{0,8},{1,9},{2,10},{3,11},{4,12},{5,13},{6,14},{7,15},{8,0},{9,1},... | collective-permute-start | bytes 3145736 | tf_op jit(solution)/shard_map/ppermute | solution.py:29
  278.2 24.0 %collective-permute-start.32 = (bf16[4,128,1024]{2,1,0:T(8,128)(2,1)}, bf16[4,128,1024]{2,1,0:T(8,128)(2,1)}, u32[]{:S(2)}, u32[]{:S(2)}) collective-permute-start(bf16[4,128,1024]{2,1,0:T(8,128)(2,1)} %get-tuple-element.121), channel_id=1, source_target_pairs={{0,16},{1,17},{2,18},{3,19},{4,20},{5,21},{6,22},{7,23},{8,24},{9,... | collective-permute-start | bytes 3145736 | tf_op jit(solution)/shard_map/ppermute | solution.py:29
  313.7 31.5 %collective-permute-start.38 = (bf16[4,160,1024]{2,1,0:T(8,128)(2,1)}, bf16[4,160,1024]{2,1,0:T(8,128)(2,1)}, u32[]{:S(2)}, u32[]{:S(2)}) collective-permute-start(bf16[4,160,1024]{2,1,0:T(8,128)(2,1)} %copy-done.47), channel_id=1, source_target_pairs={{0,8},{1,9},{2,10},{3,11},{4,12},{5,13},{6,14},{7,15},{8,0},{9,1},... | collective-permute-start | bytes 3932168 | tf_op jit(solution)/shard_map/ppermute | solution.py:29
  314.1 31.4 %collective-permute-start.35 = (bf16[4,160,1024]{2,1,0:T(8,128)(2,1)}, bf16[4,160,1024]{2,1,0:T(8,128)(2,1)}, u32[]{:S(2)}, u32[]{:S(2)}) collective-permute-start(bf16[4,160,1024]{2,1,0:T(8,128)(2,1)} %copy-done.49), channel_id=1, source_target_pairs={{0,16},{1,17},{2,18},{3,19},{4,20},{5,21},{6,22},{7,23},{8,24},{9,... | collective-permute-start | bytes 3932168 | tf_op jit(solution)/shard_map/ppermute | solution.py:29
  320.6 35.1 %collective-permute-start.58 = (bf16[128,1024]{1,0:T(8,128)(2,1)S(1)}, bf16[128,1024]{1,0:T(8,128)(2,1)S(1)}, u32[]{:S(2)}, u32[]{:S(2)}) collective-permute-start(bf16[128,1024]{1,0:T(8,128)(2,1)S(1)} %get-tuple-element.142), channel_id=1, source_target_pairs={{0,6},{1,7},{2,0},{3,1},{4,2},{5,3},{6,4},{7,5},{8,14},{9,15},{10,... | collective-permute-start | bytes 786440 | tf_op jit(solution)/shard_map/ppermute | solution.py:29
  327.8 29.4 %collective-permute-start.57 = (bf16[128,1024]{1,0:T(8,128)(2,1)S(1)}, bf16[128,1024]{1,0:T(8,128)(2,1)S(1)}, u32[]{:S(2)}, u32[]{:S(2)}) collective-permute-start(bf16[128,1024]{1,0:T(8,128)(2,1)S(1)} %get-tuple-element.141), channel_id=1, source_target_pairs={{0,4},{1,5},{2,6},{3,7},{4,0},{5,1},{6,2},{7,3},{8,12},{9,13},{10,... | collective-permute-start | bytes 786440 | tf_op jit(solution)/shard_map/ppermute | solution.py:29
  328.3 28.9 %collective-permute-start.56 = (bf16[128,1024]{1,0:T(8,128)(2,1)S(1)}, bf16[128,1024]{1,0:T(8,128)(2,1)S(1)}, u32[]{:S(2)}, u32[]{:S(2)}) collective-permute-start(bf16[128,1024]{1,0:T(8,128)(2,1)S(1)} %broadcast_add_fusion.1), channel_id=1, source_target_pairs={{0,2},{1,3},{2,4},{3,5},{4,6},{5,7},{6,0},{7,1},{8,10},{9,11},{10,... | collective-permute-start | bytes 786440 | tf_op jit(solution)/shard_map/ppermute | solution.py:29
  345.2 28.7 %collective-permute-start.41 = (bf16[2,128,1024]{2,1,0:T(8,128)(2,1)S(1)}, bf16[2,128,1024]{2,1,0:T(8,128)(2,1)S(1)}, u32[]{:S(2)}, u32[]{:S(2)}) collective-permute-start(bf16[2,128,1024]{2,1,0:T(8,128)(2,1)S(1)} %get-tuple-element.73), channel_id=1, source_target_pairs={{0,16},{1,17},{2,18},{3,19},{4,20},{5,21},{6,22},{7,23},{8,24},{9,... | collective-permute-start | bytes 1572872 | tf_op jit(solution)/shard_map/ppermute | solution.py:29
  362.8 27.3 %collective-permute-start.55 = (bf16[160,1024]{1,0:T(8,128)(2,1)}, bf16[160,1024]{1,0:T(8,128)(2,1)S(1)}, u32[]{:S(2)}, u32[]{:S(2)}) collective-permute-start(bf16[160,1024]{1,0:T(8,128)(2,1)} %get-tuple-element.140), channel_id=1, source_target_pairs={{0,6},{1,7},{2,0},{3,1},{4,2},{5,3},{6,4},{7,5},{8,14},{9,15},{10,... | collective-permute-start | bytes 983048 | tf_op jit(solution)/shard_map/ppermute | solution.py:29
  366.5 29.6 %collective-permute-start.54 = (bf16[160,1024]{1,0:T(8,128)(2,1)}, bf16[160,1024]{1,0:T(8,128)(2,1)}, u32[]{:S(2)}, u32[]{:S(2)}) collective-permute-start(bf16[160,1024]{1,0:T(8,128)(2,1)} %get-tuple-element.139), channel_id=1, source_target_pairs={{0,4},{1,5},{2,6},{3,7},{4,0},{5,1},{6,2},{7,3},{8,12},{9,13},{10,... | collective-permute-start | bytes 983048 | tf_op jit(solution)/shard_map/ppermute | solution.py:29
  367.7 28.4 %collective-permute-start.53 = (bf16[160,1024]{1,0:T(8,128)(2,1)}, bf16[160,1024]{1,0:T(8,128)(2,1)}, u32[]{:S(2)}, u32[]{:S(2)}) collective-permute-start(bf16[160,1024]{1,0:T(8,128)(2,1)} %broadcast_add_fusion), channel_id=1, source_target_pairs={{0,2},{1,3},{2,4},{3,5},{4,6},{5,7},{6,0},{7,1},{8,10},{9,11},{10,... | collective-permute-start | bytes 983048 | tf_op jit(solution)/shard_map/ppermute | solution.py:29
  380.5 28.6 %collective-permute-start.46 = (bf16[4,128,1024]{2,1,0:T(8,128)(2,1)S(1)}, bf16[4,128,1024]{2,1,0:T(8,128)(2,1)}, u32[]{:S(2)}, u32[]{:S(2)}) collective-permute-start(bf16[4,128,1024]{2,1,0:T(8,128)(2,1)S(1)} %get-tuple-element.108), channel_id=1, source_target_pairs={{0,8},{1,9},{2,10},{3,11},{4,12},{5,13},{6,14},{7,15},{8,0},{9,1},... | collective-permute-start | bytes 3145736 | tf_op jit(solution)/shard_map/ppermute | solution.py:29
  381.9 27.1 %collective-permute-start.45 = (bf16[4,128,1024]{2,1,0:T(8,128)(2,1)}, bf16[4,128,1024]{2,1,0:T(8,128)(2,1)}, u32[]{:S(2)}, u32[]{:S(2)}) collective-permute-start(bf16[4,128,1024]{2,1,0:T(8,128)(2,1)} %get-tuple-element.106), channel_id=1, source_target_pairs={{0,16},{1,17},{2,18},{3,19},{4,20},{5,21},{6,22},{7,23},{8,24},{9,... | collective-permute-start | bytes 3145736 | tf_op jit(solution)/shard_map/ppermute | solution.py:29
  407.2 16.4 %collective-permute-start.44 = (f32[11,1024]{1,0:T(8,128)S(1)}, f32[11,1024]{1,0:T(8,128)S(1)}, u32[]{:S(2)}, u32[]{:S(2)}) collective-permute-start(f32[11,1024]{1,0:T(8,128)S(1)} %add.745), channel_id=1, source_target_pairs={{0,16},{1,17},{2,18},{3,19},{4,20},{5,21},{6,22},{7,23},{8,24},{9,... | collective-permute-start | bytes 135176 | tf_op jit(solution)/shard_map/ppermute | solution.py:29
  413.2 26.4 %collective-permute-start.52 = (bf16[128,1024]{1,0:T(8,128)(2,1)S(1)}, bf16[128,1024]{1,0:T(8,128)(2,1)S(1)}, u32[]{:S(2)}, u32[]{:S(2)}) collective-permute-start(bf16[128,1024]{1,0:T(8,128)(2,1)S(1)} %get-tuple-element.144), channel_id=1, source_target_pairs={{0,6},{1,7},{2,0},{3,1},{4,2},{5,3},{6,4},{7,5},{8,14},{9,15},{10,... | collective-permute-start | bytes 786440 | tf_op jit(solution)/shard_map/ppermute | solution.py:29
  415.2 24.4 %collective-permute-start.51 = (bf16[128,1024]{1,0:T(8,128)(2,1)S(1)}, bf16[128,1024]{1,0:T(8,128)(2,1)S(1)}, u32[]{:S(2)}, u32[]{:S(2)}) collective-permute-start(bf16[128,1024]{1,0:T(8,128)(2,1)S(1)} %get-tuple-element.143), channel_id=1, source_target_pairs={{0,4},{1,5},{2,6},{3,7},{4,0},{5,1},{6,2},{7,3},{8,12},{9,13},{10,... | collective-permute-start | bytes 786440 | tf_op jit(solution)/shard_map/ppermute | solution.py:29
  423.7 16.9 %collective-permute-start.50 = (f32[11,1024]{1,0:T(8,128)S(1)}, f32[11,1024]{1,0:T(8,128)S(1)}, u32[]{:S(2)}, u32[]{:S(2)}) collective-permute-start(f32[11,1024]{1,0:T(8,128)S(1)} %add_add_fusion.1), channel_id=1, source_target_pairs={{0,6},{1,7},{2,0},{3,1},{4,2},{5,3},{6,4},{7,5},{8,14},{9,15},{10,... | collective-permute-start | bytes 135176 | tf_op jit(solution)/shard_map/ppermute | solution.py:29
  (150 other events, 1450.9 us)
Sparse Core Ops, SparseCore 0:
  11.1 161.6 all-gather.2

commit v5 on v4

--- a/solution.py
+++ b/solution.py
@@ -650,7 +650,7 @@
     return lax.ppermute(shard, axis, pairs)
 
 
-def carried_in(part, starts_in, decay_vec, length, reverse):
+def carried_in(part, starts_in, decay_vec, length, reverse, between=None):
     count = lax.axis_size("seq")
     place = lax.axis_index("seq")
     clear = 1.0 - starts_in.astype(jnp.float32)
@@ -667,6 +667,8 @@
         last = jnp.where(is_far, part, other)
         first_block, second_block = chip * 2 + (1 if reverse else 0), chip * 2 + (0 if reverse else 1)
         joined = clear_of(second_block) * block_fade * near + last
+        if between is not None:
+            joined = between(joined)
         step = -1 if reverse else 1
         entering = jnp.zeros_like(part)
         open_way = jnp.ones((part.shape[1], 1), jnp.float32)
@@ -1080,10 +1082,19 @@
         key_sides = add_corner(key_parts, *all_tied(key_corner, state_gradient))
         key_from = send_sides(*key_sides)
         state_gradient = tied(state_gradient, key_sides[0], key_sides[1][2:])
-    num_next, den_next = carried_in(state_gradient, starts_in, decay_vec, length, True)
+    summed = []
+
+    def beside_sides(joined):
+        summed.extend(
+            add_sides(value_parts, *[tied(a, joined, other_time) for a in value_from])
+        )
+        return tied(joined, summed[1][0])
+
+    num_next, den_next = carried_in(
+        state_gradient, starts_in, decay_vec, length, True, beside_sides if tuned else None
+    )
     if tuned:
-        value_first, value_outgoing = add_sides(value_parts, *[tied(a, num_next, other_time) for a in value_from])
-        num_next = tied(num_next, value_outgoing[0])
+        value_first, value_outgoing = summed
     num_tail = tail_fade * num_next[:, None, :]
     den_tail = tail_fade * den_next[:, None, :]
     tail_grad = powered_lookups * (value_row_block * num_tail + den_tail)

time: 458 us -> 454 us (level)
  no operation moved by 1% of the time
where the time goes in v5:
time: 454 us; the launch traced here: 447 us
  waiting for transfers between devices  112 us (25%)
  Pallas kernels  90.7 us (20%)
  starting transfers between devices  81.9 us (18%)
  other arithmetic  77.6 us (17%)
  local copies, waits for them, and re-layouts  31.8 us (7%)
  between operations  29.2 us (6%)
  matrix products  23.9 us (5%)
    ppermute x55, waiting for transfers between devices, sent(): return lax.ppermute(array, BOTH, pairs)  111 us
    ppermute x55, starting transfers between devices, sent(): return lax.ppermute(array, BOTH, pairs)  76.3 us
    pallas_call x1, Pallas kernels, channel_mix(): pl.pallas_call(channel_kernel, out_shape=(half_rows, half_rows, half_rows...  31.7 us
    pallas_call x3, Pallas kernels, quarters_call(): pl.pallas_call(kernel, grid=(steps,), out_shape=tuple((jax.ShapeDtypeStru...  28.2 us
    pallas_call x5, Pallas kernels, assemble(): pl.pallas_call(partial(assemble_kernel, counts, start, columns), out_shap...  15.1 us
    pallas_call x1, Pallas kernels, time_mix_back(): pl.pallas_call(time_mix_kernel, grid=(1024 // tile,), out_shape=(jax.Shap...  13.7 us
    another operation x5, other arithmetic  11.1 us
    slice x18, local copies, waits for them, and re-layouts, tied(): first = other[(0,) * other.ndim].astype(jnp.float32)  9.97 us
  transfers between devices with their start and end apart: 60, of which 16 were waited for; matrix products, arithmetic and copies ran while one was open for 26% of the time, Pallas kernels for 13%

profile of v5, /device:TPU:0, one launch (start us, length us, event | category | flops | bytes accessed | tf_op | source)
XLA Modules:
  0.0 447.4 jit_solution(8500373089798842914)
XLA Ops:
  11.2 5.1 %collective-permute-start.2 = (bf16[144,1024]{1,0:T(8,128)(2,1)S(1)}, bf16[144,1024]{1,0:T(8,128)(2,1)S(1)}, u32[]{:S(2)}, u32[]{:S(2)}) collective-permute-start(bf16[144,1024]{1,0:T(8,128)(2,1)S(1)} %select_dynamic-update-slice_fusion), channel_id=1, source_target_pairs={{0,6},{1,7},{2,0},{3,1},{4,2},{5,3},{6,4},{7,5},{8,14},{9,15},{10,... | collective-permute-start | bytes 884744 | tf_op jit(solution)/shard_map/ppermute | solution.py:29
  24.6 29.4 %collective-permute-done.1 = bf16[144,1024]{1,0:T(8,128)(2,1)S(1)} collective-permute-done((bf16[144,1024]{1,0:T(8,128)(2,1)S(1)}, bf16[144,1024]{1,0:T(8,128)(2,1)S(1)}, u32[]{:S(2)}, u32[]{:S(2)}) %collective-permute-start.1) | collective-permute-done | bytes 294944 | tf_op jit(solution)/shard_map/ppermute | solution.py:29
  62.0 34.9 %collective-permute-done.3.refs_1_ = bf16[4,144,1024]{2,1,0:T(8,128)(2,1)S(1)} collective-permute-done((bf16[4,144,1024]{2,1,0:T(8,128)(2,1)S(1)}, bf16[4,144,1024]{2,1,0:T(8,128)(2,1)S(1)}, u32[]{:S(2)}, u32[]{:S(2)}) %collective-permute-start.3) | collective-permute-done | bytes 1179680 | tf_op jit(solution)/shard_map/ppermute | solution.py:29
  116.6 3.1 shard_map.358
  119.7 3.1 shard_map.359
  138.9 3.0 fusion.9
  142.1 10.3 %collective-permute-start.15 = (f32[2,2,1024]{2,1,0:T(2,128)S(1)}, f32[2,2,1024]{2,1,0:T(2,128)S(1)}, u32[]{:S(2)}, u32[]{:S(2)}) collective-permute-start(f32[2,2,1024]{2,1,0:T(2,128)S(1)} %select_add_fusion.1), channel_id=1, source_target_pairs={{0,4},{1,5},{2,6},{3,7},{4,0},{5,1},{6,2},{7,3},{8,12},{9,13},{10,... | collective-permute-start | bytes 49160 | tf_op jit(solution)/shard_map/ppermute | solution.py:29
  155.1 3.3 shard_map.357
  158.4 3.2 shard_map.360
  161.8 3.5 fusion.42
  173.4 31.7 %shard_map.362 = (bf16[512,1024]{1,0:T(8,128)(2,1)}, bf16[512,1024]{1,0:T(8,128)(2,1)}, bf16[512,1024]{1,0:T(8,128)(2,1)}, f32[512,1024]{1,0:T(8,128)}, f32[512,...) custom-call(s32[32]{0:T(128)} %and_add_fusion.slots_ref, ...), custom_call_target="tpu_custom_call" | custom-call | flops 19327352832 | bytes 41943040 | tf_op jit(solution)/shard_map/pallas_call | solution.py:286
  222.6 3.2 multiply_reduce_fusion.2
  227.1 8.6 %shard_map.363 = (bf16[4,128,1024]{2,1,0:T(8,128)(2,1)S(1)}, bf16[4,128,1024]{2,1,0:T(8,128)(2,1)}, bf16[4,128,1024]{2,1,0:T(8,128)(2,1)}, bf16[2,128,1024]{2,1,0:T(8,128)(2,1)S(1)}, bf16[2,128,1024]{2,1,0:T(8,128)(2,1)S(1)}) custom-call(bf16[4,512,512]{2,1,0:T(8,128)(2,1)} %get-tuple-element.53.own_ref, ...), custom_call_target="tpu_custom_call" | custom-call | flops 1 | bytes 1 | tf_op jit(solution)/shard_map/pallas_call | solution.py:528
  239.2 10.3 %shard_map.364 = (bf16[4,160,1024]{2,1,0:T(8,128)(2,1)}, bf16[4,160,1024]{2,1,0:T(8,128)(2,1)}, bf16[4,160,1024]{2,1,0:T(8,128)(2,1)}, bf16[2,160,1024]{2,1,0:T(8,128)(2,1)S(1)}, bf16[2,160,1024]{2,1,0:T(8,128)(2,1)S(1)}) custom-call(bf16[512,512]{1,0:T(8,128)(2,1)S(1)} %get-tuple-element.157.key_ref, bf16[512,512]{1,0:T(8,128)(2,1)S(1)} %get-tuple-element.153.other_key_ref, ...), custom_call_target="tpu_custom_call" | custom-call | flops 1 | bytes 1 | tf_op jit(solution)/shard_map/pallas_call | solution.py:528
  262.3 13.7 %shard_map.365 = (bf16[512,1024]{1,0:T(8,128)(2,1)S(1)}, f32[512,1024]{1,0:T(8,128)S(1)}, f32[512,1024]{1,0:T(8,128)}, f32[2,1,1024]{2,1,0:T(1,128)S(1)}, f32[2,...) custom-call(bf16[512,1024]{1,0:T(8,128)(2,1)S(1)} %bitcast.260, ...), custom_call_target="tpu_custom_call" | custom-call | flops 1 | bytes 1 | tf_op jit(solution)/shard_map/pallas_call | solution.py:492
  285.1 6.1 %collective-permute-done.31 = bf16[4,128,1024]{2,1,0:T(8,128)(2,1)} collective-permute-done((bf16[4,128,1024]{2,1,0:T(8,128)(2,1)}, bf16[4,128,1024]{2,1,0:T(8,128)(2,1)}, u32[]{:S(2)}, u32[]{:S(2)}) %collective-permute-start.31) | collective-permute-done | bytes 1048608 | tf_op jit(solution)/shard_map/ppermute | solution.py:29
  291.2 3.7 fusion.114
  304.9 3.1 multiply_reduce_fusion.3
  311.1 3.3 pad_maximum_fusion.5.own_ref
  317.3 3.7 collective-permute-start.58
  325.8 9.3 %shard_map.366 = (bf16[4,128,1024]{2,1,0:T(8,128)(2,1)S(1)}, bf16[4,128,1024]{2,1,0:T(8,128)(2,1)S(1)}, bf16[4,128,1024]{2,1,0:T(8,128)(2,1)}, bf16[2,128,1024]{...) custom-call(bf16[512,2048]{1,0:T(8,128)(2,1)} %pad_maximum_fusion.5.own_ref, ...), custom_call_target="tpu_custom_call" | custom-call | flops 1 | bytes 1 | tf_op jit(solution)/shard_map/pallas_call | solution.py:528
  336.3 5.6 %collective-permute-done.38 = bf16[4,160,1024]{2,1,0:T(8,128)(2,1)} collective-permute-done((bf16[4,160,1024]{2,1,0:T(8,128)(2,1)}, bf16[4,160,1024]{2,1,0:T(8,128)(2,1)}, u32[]{:S(2)}, u32[]{:S(2)}) %collective-permute-start.38) | collective-permute-done | bytes 1310752 | tf_op jit(solution)/shard_map/ppermute | solution.py:29
  342.2 4.3 fusion.113
  359.5 4.3 collective-permute-start.55
  372.2 4.4 fusion.23
  382.0 4.9 %fusion.22 = f32[2,256,1024]{2,1,0:T(8,128)} fusion(bf16[2,256,1024]{2,1,0:T(8,128)(2,1)S(1)} %copy-done.21, f32[2,256,1024]{2,1,0:T(8,128)} %get-tuple-element.110, f32[2,256]{1,0:T(2,128)S(1)} %broadcast_multiply_fusion.9, f32[2,256]{1,0:T(2,128)} %broadcast_multiply_fusion.10, f32[1024]{0:T(1024)S(1)} %bitcast.307, f32[2,256]{1,0:T(2,128)} %copy-done.85, ...), kind=kLoop, calls=%fused_computation.34 | loop fusion | flops 9437184 | bytes 10510336 | tf_op jit(solution)/shard_map/add | solution.py:1158
  387.0 4.6 %collective-permute-done.54 = bf16[160,1024]{1,0:T(8,128)(2,1)} collective-permute-done((bf16[160,1024]{1,0:T(8,128)(2,1)}, bf16[160,1024]{1,0:T(8,128)(2,1)}, u32[]{:S(2)}, u32[]{:S(2)}) %collective-permute-start.54) | collective-permute-done | bytes 327712 | tf_op jit(solution)/shard_map/ppermute | solution.py:29
  394.4 9.5 %collective-permute-done.43 = f32[11,1024]{1,0:T(8,128)S(1)} collective-permute-done((f32[11,1024]{1,0:T(8,128)S(1)}, f32[11,1024]{1,0:T(8,128)S(1)}, u32[]{:S(2)}, u32[]{:S(2)}) %collective-permute-start.43) | collective-permute-done | bytes 45088 | tf_op jit(solution)/shard_map/ppermute | solution.py:29
  408.3 3.6 collective-permute-start.52
  413.0 6.1 %collective-permute-done.47 = bf16[128,1024]{1,0:T(8,128)(2,1)S(1)} collective-permute-done((bf16[128,1024]{1,0:T(8,128)(2,1)S(1)}, bf16[128,1024]{1,0:T(8,128)(2,1)S(1)}, u32[]{:S(2)}, u32[]{:S(2)}) %collective-permute-start.47) | collective-permute-done | bytes 262176 | tf_op jit(solution)/shard_map/ppermute | solution.py:29
  420.3 6.6 %collective-permute-start.50 = (f32[11,1024]{1,0:T(8,128)S(1)}, f32[11,1024]{1,0:T(8,128)S(1)}, u32[]{:S(2)}, u32[]{:S(2)}) collective-permute-start(f32[11,1024]{1,0:T(8,128)S(1)} %add_add_fusion.1), channel_id=1, source_target_pairs={{0,6},{1,7},{2,0},{3,1},{4,2},{5,3},{6,4},{7,5},{8,14},{9,15},{10,... | collective-permute-start | bytes 135176 | tf_op jit(solution)/shard_map/ppermute | solution.py:29
  426.9 4.5 %collective-permute-start.49 = (f32[11,1024]{1,0:T(8,128)S(1)}, f32[11,1024]{1,0:T(8,128)S(1)}, u32[]{:S(2)}, u32[]{:S(2)}) collective-permute-start(f32[11,1024]{1,0:T(8,128)S(1)} %add_add_fusion.1), channel_id=1, source_target_pairs={{0,4},{1,5},{2,6},{3,7},{4,0},{5,1},{6,2},{7,3},{8,12},{9,13},{10,... | collective-permute-start | bytes 135176 | tf_op jit(solution)/shard_map/ppermute | solution.py:29
  (520 shorter events, 164.3 us)
Async XLA Ops:
  7.3 166.1 %all-gather.3.cloned.1.call-start = ((), (), s32[]{:S(2)}) async-start(), calls=%async_computation | async-start | bytes 19464192 | tf_op jit(solution)/shard_map/all_gather | solution.py:822
  16.3 37.7 %collective-permute-start.1 = (bf16[144,1024]{1,0:T(8,128)(2,1)S(1)}, bf16[144,1024]{1,0:T(8,128)(2,1)S(1)}, u32[]{:S(2)}, u32[]{:S(2)}) collective-permute-start(bf16[144,1024]{1,0:T(8,128)(2,1)S(1)} %select_dynamic-update-slice_fusion), channel_id=1, source_target_pairs={{0,4},{1,5},{2,6},{3,7},{4,0},{5,1},{6,2},{7,3},{8,12},{9,13},{10,... | collective-permute-start | bytes 884744 | tf_op jit(solution)/shard_map/ppermute | solution.py:29
  16.3 37.7 %collective-permute-start = (bf16[144,1024]{1,0:T(8,128)(2,1)S(1)}, bf16[144,1024]{1,0:T(8,128)(2,1)S(1)}, u32[]{:S(2)}, u32[]{:S(2)}) collective-permute-start(bf16[144,1024]{1,0:T(8,128)(2,1)S(1)} %select_dynamic-update-slice_fusion), channel_id=1, source_target_pairs={{0,2},{1,3},{2,4},{3,5},{4,6},{5,7},{6,0},{7,1},{8,10},{9,11},{10,... | collective-permute-start | bytes 884744 | tf_op jit(solution)/shard_map/ppermute | solution.py:29
  17.9 85.4 %collective-permute-start.12 = (bf16[2,1,1024]{2,1,0:T(2,128)(2,1)}, bf16[2,1,1024]{2,1,0:T(2,128)(2,1)S(1)}, u32[]{:S(2)}, u32[]{:S(2)}) collective-permute-start(bf16[2,1,1024]{2,1,0:T(2,128)(2,1)} %slice.330), channel_id=1, source_target_pairs={{0,1},{1,2},{2,3},{3,4},{4,5},{5,6},{6,7},{8,9},{9,10},{10,11},{11... | collective-permute-start | bytes 12296 | tf_op jit(solution)/shard_map/ppermute | solution.py:650
  54.1 42.8 %collective-permute-start.3 = (bf16[4,144,1024]{2,1,0:T(8,128)(2,1)S(1)}, bf16[4,144,1024]{2,1,0:T(8,128)(2,1)S(1)}, u32[]{:S(2)}, u32[]{:S(2)}) collective-permute-start(bf16[4,144,1024]{2,1,0:T(8,128)(2,1)S(1)} %pad_maximum_fusion.6.refs_0_), channel_id=1, source_target_pairs={{0,8},{1,9},{2,10},{3,11},{4,12},{5,13},{6,14},{7,15},{8,0},{9,1},... | collective-permute-start | bytes 3538952 | tf_op jit(solution)/shard_map/ppermute | solution.py:29
  55.7 44.4 %collective-permute-start.4 = (bf16[4,144,1024]{2,1,0:T(8,128)(2,1)S(1)}, bf16[4,144,1024]{2,1,0:T(8,128)(2,1)S(1)}, u32[]{:S(2)}, u32[]{:S(2)}) collective-permute-start(bf16[4,144,1024]{2,1,0:T(8,128)(2,1)S(1)} %pad_maximum_fusion.6.refs_0_), channel_id=1, source_target_pairs={{0,16},{1,17},{2,18},{3,19},{4,20},{5,21},{6,22},{7,23},{8,24},{9,... | collective-permute-start | bytes 3538952 | tf_op jit(solution)/shard_map/ppermute | solution.py:29
  142.1 19.6 %collective-permute-start.16 = (f32[2,2,1024]{2,1,0:T(2,128)S(1)}, f32[2,2,1024]{2,1,0:T(2,128)S(1)}, u32[]{:S(2)}, u32[]{:S(2)}) collective-permute-start(f32[2,2,1024]{2,1,0:T(2,128)S(1)} %select_add_fusion.1), channel_id=1, source_target_pairs={{0,6},{1,7},{2,0},{3,1},{4,2},{5,3},{6,4},{7,5},{8,14},{9,15},{10,... | collective-permute-start | bytes 49160 | tf_op jit(solution)/shard_map/ppermute | solution.py:29
  142.1 19.5 %collective-permute-start.15 = (f32[2,2,1024]{2,1,0:T(2,128)S(1)}, f32[2,2,1024]{2,1,0:T(2,128)S(1)}, u32[]{:S(2)}, u32[]{:S(2)}) collective-permute-start(f32[2,2,1024]{2,1,0:T(2,128)S(1)} %select_add_fusion.1), channel_id=1, source_target_pairs={{0,4},{1,5},{2,6},{3,7},{4,0},{5,1},{6,2},{7,3},{8,12},{9,13},{10,... | collective-permute-start | bytes 49160 | tf_op jit(solution)/shard_map/ppermute | solution.py:29
  205.1 34.1 %collective-permute-start.23 = (bf16[512,4096]{1,0:T(8,128)(2,1)}, bf16[512,4096]{1,0:T(8,128)(2,1)}, u32[]{:S(2)}, u32[]{:S(2)}) collective-permute-start(bf16[512,4096]{1,0:T(8,128)(2,1)} %get-tuple-element.58.refs_0_), channel_id=1, source_target_pairs={{0,1},{1,0},{2,3},{3,2},{4,5},{5,4},{6,7},{7,6},{8,9},{9,8},{10,11... | collective-permute-start | bytes 12582920 | tf_op jit(solution)/shard_map/ppermute | solution.py:29
  213.2 68.8 %collective-permute-start.30 = (bf16[512,2048]{1,0:T(8,128)(2,1)}, bf16[512,2048]{1,0:T(8,128)(2,1)}, u32[]{:S(2)}, u32[]{:S(2)}) collective-permute-start(bf16[512,2048]{1,0:T(8,128)(2,1)} %pad_maximum_fusion.4), channel_id=1, source_target_pairs={{0,1},{1,0},{2,3},{3,2},{4,5},{5,4},{6,7},{7,6},{8,9},{9,8},{10,11... | collective-permute-start | bytes 6291464 | tf_op jit(solution)/shard_map/ppermute | solution.py:29
  221.0 18.2 %collective-permute-start.24 = (bf16[512,1024]{1,0:T(8,128)(2,1)}, bf16[512,1024]{1,0:T(8,128)(2,1)}, u32[]{:S(2)}, u32[]{:S(2)}) collective-permute-start(bf16[512,1024]{1,0:T(8,128)(2,1)} %get-tuple-element.59.refs_2_), channel_id=1, source_target_pairs={{0,1},{1,0},{2,3},{3,2},{4,5},{5,4},{6,7},{7,6},{8,9},{9,8},{10,11... | collective-permute-start | bytes 3145736 | tf_op jit(solution)/shard_map/ppermute | solution.py:29
  235.7 17.1 %collective-permute-start.21 = (bf16[2,128,1024]{2,1,0:T(8,128)(2,1)S(1)}, bf16[2,128,1024]{2,1,0:T(8,128)(2,1)S(1)}, u32[]{:S(2)}, u32[]{:S(2)}) collective-permute-start(bf16[2,128,1024]{2,1,0:T(8,128)(2,1)S(1)} %get-tuple-element.57), channel_id=1, source_target_pairs={{0,8},{1,9},{2,10},{3,11},{4,12},{5,13},{6,14},{7,15},{8,0},{9,1},... | collective-permute-start | bytes 1572872 | tf_op jit(solution)/shard_map/ppermute | solution.py:29
  238.3 16.7 %collective-permute-start.25 = (bf16[2,128,1024]{2,1,0:T(8,128)(2,1)S(1)}, bf16[2,128,1024]{2,1,0:T(8,128)(2,1)S(1)}, u32[]{:S(2)}, u32[]{:S(2)}) collective-permute-start(bf16[2,128,1024]{2,1,0:T(8,128)(2,1)S(1)} %get-tuple-element.62), channel_id=1, source_target_pairs={{0,16},{1,17},{2,18},{3,19},{4,20},{5,21},{6,22},{7,23},{8,24},{9,... | collective-permute-start | bytes 1572872 | tf_op jit(solution)/shard_map/ppermute | solution.py:29
  250.0 29.7 %collective-permute-start.27 = (bf16[2,160,1024]{2,1,0:T(8,128)(2,1)S(1)}, bf16[2,160,1024]{2,1,0:T(8,128)(2,1)S(1)}, u32[]{:S(2)}, u32[]{:S(2)}) collective-permute-start(bf16[2,160,1024]{2,1,0:T(8,128)(2,1)S(1)} %get-tuple-element.60), channel_id=1, source_target_pairs={{0,16},{1,17},{2,18},{3,19},{4,20},{5,21},{6,22},{7,23},{8,24},{9,... | collective-permute-start | bytes 1966088 | tf_op jit(solution)/shard_map/ppermute | solution.py:29
  252.7 25.4 %collective-permute-start.26 = (bf16[2,160,1024]{2,1,0:T(8,128)(2,1)S(1)}, bf16[2,160,1024]{2,1,0:T(8,128)(2,1)S(1)}, u32[]{:S(2)}, u32[]{:S(2)}) collective-permute-start(bf16[2,160,1024]{2,1,0:T(8,128)(2,1)S(1)} %get-tuple-element.67), channel_id=1, source_target_pairs={{0,8},{1,9},{2,10},{3,11},{4,12},{5,13},{6,14},{7,15},{8,0},{9,1},... | collective-permute-start | bytes 1966088 | tf_op jit(solution)/shard_map/ppermute | solution.py:29
  259.4 31.7 %collective-permute-start.31 = (bf16[4,128,1024]{2,1,0:T(8,128)(2,1)}, bf16[4,128,1024]{2,1,0:T(8,128)(2,1)}, u32[]{:S(2)}, u32[]{:S(2)}) collective-permute-start(bf16[4,128,1024]{2,1,0:T(8,128)(2,1)} %get-tuple-element.121), channel_id=1, source_target_pairs={{0,8},{1,9},{2,10},{3,11},{4,12},{5,13},{6,14},{7,15},{8,0},{9,1},... | collective-permute-start | bytes 3145736 | tf_op jit(solution)/shard_map/ppermute | solution.py:29
  261.5 29.7 %collective-permute-start.29 = (bf16[4,128,1024]{2,1,0:T(8,128)(2,1)}, bf16[4,128,1024]{2,1,0:T(8,128)(2,1)}, u32[]{:S(2)}, u32[]{:S(2)}) collective-permute-start(bf16[4,128,1024]{2,1,0:T(8,128)(2,1)} %get-tuple-element.119), channel_id=1, source_target_pairs={{0,16},{1,17},{2,18},{3,19},{4,20},{5,21},{6,22},{7,23},{8,24},{9,... | collective-permute-start | bytes 3145736 | tf_op jit(solution)/shard_map/ppermute | solution.py:29
  310.4 31.5 %collective-permute-start.38 = (bf16[4,160,1024]{2,1,0:T(8,128)(2,1)}, bf16[4,160,1024]{2,1,0:T(8,128)(2,1)}, u32[]{:S(2)}, u32[]{:S(2)}) collective-permute-start(bf16[4,160,1024]{2,1,0:T(8,128)(2,1)} %copy-done.47), channel_id=1, source_target_pairs={{0,8},{1,9},{2,10},{3,11},{4,12},{5,13},{6,14},{7,15},{8,0},{9,1},... | collective-permute-start | bytes 3932168 | tf_op jit(solution)/shard_map/ppermute | solution.py:29
  310.8 31.4 %collective-permute-start.35 = (bf16[4,160,1024]{2,1,0:T(8,128)(2,1)}, bf16[4,160,1024]{2,1,0:T(8,128)(2,1)}, u32[]{:S(2)}, u32[]{:S(2)}) collective-permute-start(bf16[4,160,1024]{2,1,0:T(8,128)(2,1)} %copy-done.49), channel_id=1, source_target_pairs={{0,16},{1,17},{2,18},{3,19},{4,20},{5,21},{6,22},{7,23},{8,24},{9,... | collective-permute-start | bytes 3932168 | tf_op jit(solution)/shard_map/ppermute | solution.py:29
  317.3 35.1 %collective-permute-start.58 = (bf16[128,1024]{1,0:T(8,128)(2,1)S(1)}, bf16[128,1024]{1,0:T(8,128)(2,1)S(1)}, u32[]{:S(2)}, u32[]{:S(2)}) collective-permute-start(bf16[128,1024]{1,0:T(8,128)(2,1)S(1)} %get-tuple-element.140), channel_id=1, source_target_pairs={{0,6},{1,7},{2,0},{3,1},{4,2},{5,3},{6,4},{7,5},{8,14},{9,15},{10,... | collective-permute-start | bytes 786440 | tf_op jit(solution)/shard_map/ppermute | solution.py:29
  325.2 28.7 %collective-permute-start.57 = (bf16[128,1024]{1,0:T(8,128)(2,1)S(1)}, bf16[128,1024]{1,0:T(8,128)(2,1)S(1)}, u32[]{:S(2)}, u32[]{:S(2)}) collective-permute-start(bf16[128,1024]{1,0:T(8,128)(2,1)S(1)} %get-tuple-element.139), channel_id=1, source_target_pairs={{0,4},{1,5},{2,6},{3,7},{4,0},{5,1},{6,2},{7,3},{8,12},{9,13},{10,... | collective-permute-start | bytes 786440 | tf_op jit(solution)/shard_map/ppermute | solution.py:29
  325.3 28.6 %collective-permute-start.56 = (bf16[128,1024]{1,0:T(8,128)(2,1)S(1)}, bf16[128,1024]{1,0:T(8,128)(2,1)S(1)}, u32[]{:S(2)}, u32[]{:S(2)}) collective-permute-start(bf16[128,1024]{1,0:T(8,128)(2,1)S(1)} %broadcast_add_fusion.1), channel_id=1, source_target_pairs={{0,2},{1,3},{2,4},{3,5},{4,6},{5,7},{6,0},{7,1},{8,10},{9,11},{10,... | collective-permute-start | bytes 786440 | tf_op jit(solution)/shard_map/ppermute | solution.py:29
  341.9 28.7 %collective-permute-start.41 = (bf16[2,128,1024]{2,1,0:T(8,128)(2,1)S(1)}, bf16[2,128,1024]{2,1,0:T(8,128)(2,1)S(1)}, u32[]{:S(2)}, u32[]{:S(2)}) collective-permute-start(bf16[2,128,1024]{2,1,0:T(8,128)(2,1)S(1)} %get-tuple-element.73), channel_id=1, source_target_pairs={{0,16},{1,17},{2,18},{3,19},{4,20},{5,21},{6,22},{7,23},{8,24},{9,... | collective-permute-start | bytes 1572872 | tf_op jit(solution)/shard_map/ppermute | solution.py:29
  359.5 27.4 %collective-permute-start.55 = (bf16[160,1024]{1,0:T(8,128)(2,1)}, bf16[160,1024]{1,0:T(8,128)(2,1)S(1)}, u32[]{:S(2)}, u32[]{:S(2)}) collective-permute-start(bf16[160,1024]{1,0:T(8,128)(2,1)} %get-tuple-element.138), channel_id=1, source_target_pairs={{0,6},{1,7},{2,0},{3,1},{4,2},{5,3},{6,4},{7,5},{8,14},{9,15},{10,... | collective-permute-start | bytes 983048 | tf_op jit(solution)/shard_map/ppermute | solution.py:29
  363.8 27.8 %collective-permute-start.54 = (bf16[160,1024]{1,0:T(8,128)(2,1)}, bf16[160,1024]{1,0:T(8,128)(2,1)}, u32[]{:S(2)}, u32[]{:S(2)}) collective-permute-start(bf16[160,1024]{1,0:T(8,128)(2,1)} %get-tuple-element.137), channel_id=1, source_target_pairs={{0,4},{1,5},{2,6},{3,7},{4,0},{5,1},{6,2},{7,3},{8,12},{9,13},{10,... | collective-permute-start | bytes 983048 | tf_op jit(solution)/shard_map/ppermute | solution.py:29
  364.5 27.0 %collective-permute-start.53 = (bf16[160,1024]{1,0:T(8,128)(2,1)}, bf16[160,1024]{1,0:T(8,128)(2,1)}, u32[]{:S(2)}, u32[]{:S(2)}) collective-permute-start(bf16[160,1024]{1,0:T(8,128)(2,1)} %broadcast_add_fusion), channel_id=1, source_target_pairs={{0,2},{1,3},{2,4},{3,5},{4,6},{5,7},{6,0},{7,1},{8,10},{9,11},{10,... | collective-permute-start | bytes 983048 | tf_op jit(solution)/shard_map/ppermute | solution.py:29
  377.1 28.5 %collective-permute-start.46 = (bf16[4,128,1024]{2,1,0:T(8,128)(2,1)S(1)}, bf16[4,128,1024]{2,1,0:T(8,128)(2,1)}, u32[]{:S(2)}, u32[]{:S(2)}) collective-permute-start(bf16[4,128,1024]{2,1,0:T(8,128)(2,1)S(1)} %get-tuple-element.108), channel_id=1, source_target_pairs={{0,8},{1,9},{2,10},{3,11},{4,12},{5,13},{6,14},{7,15},{8,0},{9,1},... | collective-permute-start | bytes 3145736 | tf_op jit(solution)/shard_map/ppermute | solution.py:29
  378.6 27.1 %collective-permute-start.45 = (bf16[4,128,1024]{2,1,0:T(8,128)(2,1)}, bf16[4,128,1024]{2,1,0:T(8,128)(2,1)}, u32[]{:S(2)}, u32[]{:S(2)}) collective-permute-start(bf16[4,128,1024]{2,1,0:T(8,128)(2,1)} %get-tuple-element.106), channel_id=1, source_target_pairs={{0,16},{1,17},{2,18},{3,19},{4,20},{5,21},{6,22},{7,23},{8,24},{9,... | collective-permute-start | bytes 3145736 | tf_op jit(solution)/shard_map/ppermute | solution.py:29
  403.9 16.4 %collective-permute-start.44 = (f32[11,1024]{1,0:T(8,128)S(1)}, f32[11,1024]{1,0:T(8,128)S(1)}, u32[]{:S(2)}, u32[]{:S(2)}) collective-permute-start(f32[11,1024]{1,0:T(8,128)S(1)} %add.737), channel_id=1, source_target_pairs={{0,16},{1,17},{2,18},{3,19},{4,20},{5,21},{6,22},{7,23},{8,24},{9,... | collective-permute-start | bytes 135176 | tf_op jit(solution)/shard_map/ppermute | solution.py:29
  408.3 25.0 %collective-permute-start.52 = (bf16[128,1024]{1,0:T(8,128)(2,1)S(1)}, bf16[128,1024]{1,0:T(8,128)(2,1)S(1)}, u32[]{:S(2)}, u32[]{:S(2)}) collective-permute-start(bf16[128,1024]{1,0:T(8,128)(2,1)S(1)} %get-tuple-element.142), channel_id=1, source_target_pairs={{0,6},{1,7},{2,0},{3,1},{4,2},{5,3},{6,4},{7,5},{8,14},{9,15},{10,... | collective-permute-start | bytes 786440 | tf_op jit(solution)/shard_map/ppermute | solution.py:29
  411.9 24.5 %collective-permute-start.51 = (bf16[128,1024]{1,0:T(8,128)(2,1)S(1)}, bf16[128,1024]{1,0:T(8,128)(2,1)S(1)}, u32[]{:S(2)}, u32[]{:S(2)}) collective-permute-start(bf16[128,1024]{1,0:T(8,128)(2,1)S(1)} %get-tuple-element.141), channel_id=1, source_target_pairs={{0,4},{1,5},{2,6},{3,7},{4,0},{5,1},{6,2},{7,3},{8,12},{9,13},{10,... | collective-permute-start | bytes 786440 | tf_op jit(solution)/shard_map/ppermute | solution.py:29
  420.3 17.0 %collective-permute-start.50 = (f32[11,1024]{1,0:T(8,128)S(1)}, f32[11,1024]{1,0:T(8,128)S(1)}, u32[]{:S(2)}, u32[]{:S(2)}) collective-permute-start(f32[11,1024]{1,0:T(8,128)S(1)} %add_add_fusion.1), channel_id=1, source_target_pairs={{0,6},{1,7},{2,0},{3,1},{4,2},{5,3},{6,4},{7,5},{8,14},{9,15},{10,... | collective-permute-start | bytes 135176 | tf_op jit(solution)/shard_map/ppermute | solution.py:29
  (150 other events, 1474.6 us)
Sparse Core Ops, SparseCore 0:
  11.1 161.7 all-gather.2

commit v6 on v5

--- a/solution.py
+++ b/solution.py
@@ -1117,14 +1117,13 @@
             own_time, other_time, flat_grads, other_grads, flat_branch_grad, other_branch_grad
         )
         value_got = all_tied(send_column(all_tied(value_outgoing, num_next)), time_parts[4])
-        key_first, key_outgoing = add_sides(key_parts, *all_tied(key_from, time_parts[4]))
         time_corner = send_corner(time_parts)
     else:
         grad_key = weight_grad(key_in, key_grad16)
         grad_value = weight_grad(value_in, val_grad16)
         grad_gate = weight_grad(gate_in, gate_pre_grad)
     if tuned:
-        key_grad16 = tied(key_grad16, key_outgoing[0])
+        key_grad16 = tied(key_grad16, time_parts[4])
     key_in_grad = project_back(key_grad16, lookup_weight)
     value_in_grad = project_back(val_grad16, content_weight)
     gate_in_grad = project_back(gate_pre_grad, receptance_weight)
@@ -1143,6 +1142,7 @@
         + gate_in_grad * (1.0 - temporal_receptance_mixture)
     ) * keep_mask
     if tuned:
+        key_first, key_outgoing = add_sides(key_parts, *all_tied(key_from, before_one_grad))
         time_sides = add_corner(time_parts, *all_tied(time_corner, before_one_grad))
         time_from = send_sides(*time_sides)
     from_next = shifted(before_one_grad[:, :1, :], "seq", -1)

time: 454 us -> 453 us (level)
    slice x18 -> x17, local copies, waits for them, and re-layouts: 9.97 us -> 9.41 us  [tied(): first = other[(0,) * other.ndim].astype(jnp.float32)]
where the time goes in v6:
time: 453 us; the launch traced here: 446 us
  waiting for transfers between devices  112 us (25%)
  Pallas kernels  91 us (20%)
  starting transfers between devices  82.2 us (18%)
  other arithmetic  77.3 us (17%)
  local copies, waits for them, and re-layouts  31.5 us (7%)
  between operations  28.6 us (6%)
  matrix products  23.9 us (5%)
    ppermute x55, waiting for transfers between devices, sent(): return lax.ppermute(array, BOTH, pairs)  111 us
    ppermute x55, starting transfers between devices, sent(): return lax.ppermute(array, BOTH, pairs)  76.4 us
    pallas_call x1, Pallas kernels, channel_mix(): pl.pallas_call(channel_kernel, out_shape=(half_rows, half_rows, half_rows...  31.7 us
    pallas_call x3, Pallas kernels, quarters_call(): pl.pallas_call(kernel, grid=(steps,), out_shape=tuple((jax.ShapeDtypeStru...  28.5 us
    pallas_call x5, Pallas kernels, assemble(): pl.pallas_call(partial(assemble_kernel, counts, start, columns), out_shap...  15 us
    pallas_call x1, Pallas kernels, time_mix_back(): pl.pallas_call(time_mix_kernel, grid=(1024 // tile,), out_shape=(jax.Shap...  13.7 us
    another operation x5, other arithmetic  10.6 us
    slice x17, local copies, waits for them, and re-layouts, tied(): first = other[(0,) * other.ndim].astype(jnp.float32)  9.41 us
  transfers between devices with their start and end apart: 60, of which 16 were waited for; matrix products, arithmetic and copies ran while one was open for 26% of the time, Pallas kernels for 13%

profile of v6, /device:TPU:0, one launch (start us, length us, event | category | flops | bytes accessed | tf_op | source)
XLA Modules:
  0.0 446.1 jit_solution(11188173556461541920)
XLA Ops:
  11.2 5.1 %collective-permute-start.2 = (bf16[144,1024]{1,0:T(8,128)(2,1)S(1)}, bf16[144,1024]{1,0:T(8,128)(2,1)S(1)}, u32[]{:S(2)}, u32[]{:S(2)}) collective-permute-start(bf16[144,1024]{1,0:T(8,128)(2,1)S(1)} %select_dynamic-update-slice_fusion), channel_id=1, source_target_pairs={{0,6},{1,7},{2,0},{3,1},{4,2},{5,3},{6,4},{7,5},{8,14},{9,15},{10,... | collective-permute-start | bytes 884744 | tf_op jit(solution)/shard_map/ppermute | solution.py:29
  24.6 29.3 %collective-permute-done.1 = bf16[144,1024]{1,0:T(8,128)(2,1)S(1)} collective-permute-done((bf16[144,1024]{1,0:T(8,128)(2,1)S(1)}, bf16[144,1024]{1,0:T(8,128)(2,1)S(1)}, u32[]{:S(2)}, u32[]{:S(2)}) %collective-permute-start.1) | collective-permute-done | bytes 294944 | tf_op jit(solution)/shard_map/ppermute | solution.py:29
  62.0 34.9 %collective-permute-done.3.refs_1_ = bf16[4,144,1024]{2,1,0:T(8,128)(2,1)S(1)} collective-permute-done((bf16[4,144,1024]{2,1,0:T(8,128)(2,1)S(1)}, bf16[4,144,1024]{2,1,0:T(8,128)(2,1)S(1)}, u32[]{:S(2)}, u32[]{:S(2)}) %collective-permute-start.3) | collective-permute-done | bytes 1179680 | tf_op jit(solution)/shard_map/ppermute | solution.py:29
  116.6 3.1 shard_map.358
  119.7 3.1 shard_map.359
  142.3 10.3 %collective-permute-start.15 = (f32[2,2,1024]{2,1,0:T(2,128)S(1)}, f32[2,2,1024]{2,1,0:T(2,128)S(1)}, u32[]{:S(2)}, u32[]{:S(2)}) collective-permute-start(f32[2,2,1024]{2,1,0:T(2,128)S(1)} %select_add_fusion.1), channel_id=1, source_target_pairs={{0,4},{1,5},{2,6},{3,7},{4,0},{5,1},{6,2},{7,3},{8,12},{9,13},{10,... | collective-permute-start | bytes 49160 | tf_op jit(solution)/shard_map/ppermute | solution.py:29
  155.2 3.3 shard_map.357
  158.6 3.1 shard_map.360
  161.8 3.5 fusion.42
  173.7 31.7 %shard_map.362 = (bf16[512,1024]{1,0:T(8,128)(2,1)}, bf16[512,1024]{1,0:T(8,128)(2,1)}, bf16[512,1024]{1,0:T(8,128)(2,1)}, f32[512,1024]{1,0:T(8,128)}, f32[512,...) custom-call(s32[32]{0:T(128)} %and_add_fusion.slots_ref, ...), custom_call_target="tpu_custom_call" | custom-call | flops 19327352832 | bytes 41943040 | tf_op jit(solution)/shard_map/pallas_call | solution.py:286
  222.7 3.2 multiply_reduce_fusion.2
  227.3 8.6 %shard_map.363 = (bf16[4,128,1024]{2,1,0:T(8,128)(2,1)S(1)}, bf16[4,128,1024]{2,1,0:T(8,128)(2,1)}, bf16[4,128,1024]{2,1,0:T(8,128)(2,1)}, bf16[2,128,1024]{2,1,0:T(8,128)(2,1)S(1)}, bf16[2,128,1024]{2,1,0:T(8,128)(2,1)S(1)}) custom-call(bf16[4,512,512]{2,1,0:T(8,128)(2,1)} %get-tuple-element.53.own_ref, ...), custom_call_target="tpu_custom_call" | custom-call | flops 1 | bytes 1 | tf_op jit(solution)/shard_map/pallas_call | solution.py:528
  239.3 10.4 %shard_map.364 = (bf16[4,160,1024]{2,1,0:T(8,128)(2,1)}, bf16[4,160,1024]{2,1,0:T(8,128)(2,1)}, bf16[4,160,1024]{2,1,0:T(8,128)(2,1)}, bf16[2,160,1024]{2,1,0:T(8,128)(2,1)S(1)}, bf16[2,160,1024]{2,1,0:T(8,128)(2,1)S(1)}) custom-call(bf16[512,512]{1,0:T(8,128)(2,1)S(1)} %get-tuple-element.158.key_ref, bf16[512,512]{1,0:T(8,128)(2,1)S(1)} %get-tuple-element.154.other_key_ref, ...), custom_call_target="tpu_custom_call" | custom-call | flops 1 | bytes 1 | tf_op jit(solution)/shard_map/pallas_call | solution.py:528
  262.4 13.7 %shard_map.365 = (bf16[512,1024]{1,0:T(8,128)(2,1)S(1)}, f32[512,1024]{1,0:T(8,128)S(1)}, f32[512,1024]{1,0:T(8,128)}, f32[2,1,1024]{2,1,0:T(1,128)S(1)}, f32[2,...) custom-call(bf16[512,1024]{1,0:T(8,128)(2,1)S(1)} %bitcast.257, ...), custom_call_target="tpu_custom_call" | custom-call | flops 1 | bytes 1 | tf_op jit(solution)/shard_map/pallas_call | solution.py:492
  285.2 6.1 %collective-permute-done.31 = bf16[4,128,1024]{2,1,0:T(8,128)(2,1)} collective-permute-done((bf16[4,128,1024]{2,1,0:T(8,128)(2,1)}, bf16[4,128,1024]{2,1,0:T(8,128)(2,1)}, u32[]{:S(2)}, u32[]{:S(2)}) %collective-permute-start.31) | collective-permute-done | bytes 1048608 | tf_op jit(solution)/shard_map/ppermute | solution.py:29
  291.4 3.7 fusion.115
  305.0 3.1 multiply_reduce_fusion.3
  310.5 3.3 pad_maximum_fusion.5.own_ref
  318.7 3.7 collective-permute-start.58
  327.2 9.6 %shard_map.366 = (bf16[4,128,1024]{2,1,0:T(8,128)(2,1)S(1)}, bf16[4,128,1024]{2,1,0:T(8,128)(2,1)S(1)}, bf16[4,128,1024]{2,1,0:T(8,128)(2,1)}, bf16[2,128,1024]{...) custom-call(bf16[512,2048]{1,0:T(8,128)(2,1)} %pad_maximum_fusion.5.own_ref, ...), custom_call_target="tpu_custom_call" | custom-call | flops 1 | bytes 1 | tf_op jit(solution)/shard_map/pallas_call | solution.py:528
  342.4 3.4 collective-permute-done.52
  347.4 3.8 fusion.113
  357.4 4.3 collective-permute-start.55
  362.5 3.4 collective-permute-done.38
  370.9 4.4 fusion.23
  380.7 4.9 %fusion.22 = f32[2,256,1024]{2,1,0:T(8,128)} fusion(bf16[2,256,1024]{2,1,0:T(8,128)(2,1)S(1)} %copy-done.21, f32[2,256,1024]{2,1,0:T(8,128)} %get-tuple-element.116, f32[2,256]{1,0:T(2,128)S(1)} %broadcast_multiply_fusion.9, f32[2,256]{1,0:T(2,128)} %broadcast_multiply_fusion.10, f32[1024]{0:T(1024)S(1)} %bitcast.304, f32[2,256]{1,0:T(2,128)} %copy-done.86, ...), kind=kLoop, calls=%fused_computation.34 | loop fusion | flops 9437184 | bytes 10510336 | tf_op jit(solution)/shard_map/add | solution.py:1158
  385.7 3.9 collective-permute-done.54
  392.4 10.3 %collective-permute-done.41 = f32[11,1024]{1,0:T(8,128)S(1)} collective-permute-done((f32[11,1024]{1,0:T(8,128)S(1)}, f32[11,1024]{1,0:T(8,128)S(1)}, u32[]{:S(2)}, u32[]{:S(2)}) %collective-permute-start.41) | collective-permute-done | bytes 45088 | tf_op jit(solution)/shard_map/ppermute | solution.py:29
  407.4 3.3 collective-permute-start.50
  411.7 6.2 %collective-permute-done.45 = bf16[128,1024]{1,0:T(8,128)(2,1)S(1)} collective-permute-done((bf16[128,1024]{1,0:T(8,128)(2,1)S(1)}, bf16[128,1024]{1,0:T(8,128)(2,1)S(1)}, u32[]{:S(2)}, u32[]{:S(2)}) %collective-permute-start.45) | collective-permute-done | bytes 262176 | tf_op jit(solution)/shard_map/ppermute | solution.py:29
  419.1 6.4 %collective-permute-start.48 = (f32[11,1024]{1,0:T(8,128)S(1)}, f32[11,1024]{1,0:T(8,128)S(1)}, u32[]{:S(2)}, u32[]{:S(2)}) collective-permute-start(f32[11,1024]{1,0:T(8,128)S(1)} %add_add_fusion.1), channel_id=1, source_target_pairs={{0,6},{1,7},{2,0},{3,1},{4,2},{5,3},{6,4},{7,5},{8,14},{9,15},{10,... | collective-permute-start | bytes 135176 | tf_op jit(solution)/shard_map/ppermute | solution.py:29
  425.4 4.9 %collective-permute-start.47 = (f32[11,1024]{1,0:T(8,128)S(1)}, f32[11,1024]{1,0:T(8,128)S(1)}, u32[]{:S(2)}, u32[]{:S(2)}) collective-permute-start(f32[11,1024]{1,0:T(8,128)S(1)} %add_add_fusion.1), channel_id=1, source_target_pairs={{0,4},{1,5},{2,6},{3,7},{4,0},{5,1},{6,2},{7,3},{8,12},{9,13},{10,... | collective-permute-start | bytes 135176 | tf_op jit(solution)/shard_map/ppermute | solution.py:29
  (519 shorter events, 165.8 us)
Async XLA Ops:
  7.3 166.4 %all-gather.3.cloned.1.call-start = ((), (), s32[]{:S(2)}) async-start(), calls=%async_computation | async-start | bytes 19464192 | tf_op jit(solution)/shard_map/all_gather | solution.py:822
  16.3 37.7 %collective-permute-start.1 = (bf16[144,1024]{1,0:T(8,128)(2,1)S(1)}, bf16[144,1024]{1,0:T(8,128)(2,1)S(1)}, u32[]{:S(2)}, u32[]{:S(2)}) collective-permute-start(bf16[144,1024]{1,0:T(8,128)(2,1)S(1)} %select_dynamic-update-slice_fusion), channel_id=1, source_target_pairs={{0,4},{1,5},{2,6},{3,7},{4,0},{5,1},{6,2},{7,3},{8,12},{9,13},{10,... | collective-permute-start | bytes 884744 | tf_op jit(solution)/shard_map/ppermute | solution.py:29
  16.3 37.7 %collective-permute-start = (bf16[144,1024]{1,0:T(8,128)(2,1)S(1)}, bf16[144,1024]{1,0:T(8,128)(2,1)S(1)}, u32[]{:S(2)}, u32[]{:S(2)}) collective-permute-start(bf16[144,1024]{1,0:T(8,128)(2,1)S(1)} %select_dynamic-update-slice_fusion), channel_id=1, source_target_pairs={{0,2},{1,3},{2,4},{3,5},{4,6},{5,7},{6,0},{7,1},{8,10},{9,11},{10,... | collective-permute-start | bytes 884744 | tf_op jit(solution)/shard_map/ppermute | solution.py:29
  17.9 85.3 %collective-permute-start.12 = (bf16[2,1,1024]{2,1,0:T(2,128)(2,1)}, bf16[2,1,1024]{2,1,0:T(2,128)(2,1)S(1)}, u32[]{:S(2)}, u32[]{:S(2)}) collective-permute-start(bf16[2,1,1024]{2,1,0:T(2,128)(2,1)} %slice.328), channel_id=1, source_target_pairs={{0,1},{1,2},{2,3},{3,4},{4,5},{5,6},{6,7},{8,9},{9,10},{10,11},{11... | collective-permute-start | bytes 12296 | tf_op jit(solution)/shard_map/ppermute | solution.py:650
  54.1 42.8 %collective-permute-start.3 = (bf16[4,144,1024]{2,1,0:T(8,128)(2,1)S(1)}, bf16[4,144,1024]{2,1,0:T(8,128)(2,1)S(1)}, u32[]{:S(2)}, u32[]{:S(2)}) collective-permute-start(bf16[4,144,1024]{2,1,0:T(8,128)(2,1)S(1)} %pad_maximum_fusion.6.refs_0_), channel_id=1, source_target_pairs={{0,8},{1,9},{2,10},{3,11},{4,12},{5,13},{6,14},{7,15},{8,0},{9,1},... | collective-permute-start | bytes 3538952 | tf_op jit(solution)/shard_map/ppermute | solution.py:29
  55.7 44.4 %collective-permute-start.4 = (bf16[4,144,1024]{2,1,0:T(8,128)(2,1)S(1)}, bf16[4,144,1024]{2,1,0:T(8,128)(2,1)S(1)}, u32[]{:S(2)}, u32[]{:S(2)}) collective-permute-start(bf16[4,144,1024]{2,1,0:T(8,128)(2,1)S(1)} %pad_maximum_fusion.6.refs_0_), channel_id=1, source_target_pairs={{0,16},{1,17},{2,18},{3,19},{4,20},{5,21},{6,22},{7,23},{8,24},{9,... | collective-permute-start | bytes 3538952 | tf_op jit(solution)/shard_map/ppermute | solution.py:29
  142.2 19.5 %collective-permute-start.16 = (f32[2,2,1024]{2,1,0:T(2,128)S(1)}, f32[2,2,1024]{2,1,0:T(2,128)S(1)}, u32[]{:S(2)}, u32[]{:S(2)}) collective-permute-start(f32[2,2,1024]{2,1,0:T(2,128)S(1)} %select_add_fusion.1), channel_id=1, source_target_pairs={{0,6},{1,7},{2,0},{3,1},{4,2},{5,3},{6,4},{7,5},{8,14},{9,15},{10,... | collective-permute-start | bytes 49160 | tf_op jit(solution)/shard_map/ppermute | solution.py:29
  142.3 19.5 %collective-permute-start.15 = (f32[2,2,1024]{2,1,0:T(2,128)S(1)}, f32[2,2,1024]{2,1,0:T(2,128)S(1)}, u32[]{:S(2)}, u32[]{:S(2)}) collective-permute-start(f32[2,2,1024]{2,1,0:T(2,128)S(1)} %select_add_fusion.1), channel_id=1, source_target_pairs={{0,4},{1,5},{2,6},{3,7},{4,0},{5,1},{6,2},{7,3},{8,12},{9,13},{10,... | collective-permute-start | bytes 49160 | tf_op jit(solution)/shard_map/ppermute | solution.py:29
  205.4 33.9 %collective-permute-start.23 = (bf16[512,4096]{1,0:T(8,128)(2,1)}, bf16[512,4096]{1,0:T(8,128)(2,1)}, u32[]{:S(2)}, u32[]{:S(2)}) collective-permute-start(bf16[512,4096]{1,0:T(8,128)(2,1)} %get-tuple-element.58.refs_0_), channel_id=1, source_target_pairs={{0,1},{1,0},{2,3},{3,2},{4,5},{5,4},{6,7},{7,6},{8,9},{9,8},{10,11... | collective-permute-start | bytes 12582920 | tf_op jit(solution)/shard_map/ppermute | solution.py:29
  213.5 68.7 %collective-permute-start.30 = (bf16[512,2048]{1,0:T(8,128)(2,1)}, bf16[512,2048]{1,0:T(8,128)(2,1)}, u32[]{:S(2)}, u32[]{:S(2)}) collective-permute-start(bf16[512,2048]{1,0:T(8,128)(2,1)} %pad_maximum_fusion.4), channel_id=1, source_target_pairs={{0,1},{1,0},{2,3},{3,2},{4,5},{5,4},{6,7},{7,6},{8,9},{9,8},{10,11... | collective-permute-start | bytes 6291464 | tf_op jit(solution)/shard_map/ppermute | solution.py:29
  221.2 18.0 %collective-permute-start.24 = (bf16[512,1024]{1,0:T(8,128)(2,1)}, bf16[512,1024]{1,0:T(8,128)(2,1)}, u32[]{:S(2)}, u32[]{:S(2)}) collective-permute-start(bf16[512,1024]{1,0:T(8,128)(2,1)} %get-tuple-element.59.refs_2_), channel_id=1, source_target_pairs={{0,1},{1,0},{2,3},{3,2},{4,5},{5,4},{6,7},{7,6},{8,9},{9,8},{10,11... | collective-permute-start | bytes 3145736 | tf_op jit(solution)/shard_map/ppermute | solution.py:29
  235.9 17.1 %collective-permute-start.21 = (bf16[2,128,1024]{2,1,0:T(8,128)(2,1)S(1)}, bf16[2,128,1024]{2,1,0:T(8,128)(2,1)S(1)}, u32[]{:S(2)}, u32[]{:S(2)}) collective-permute-start(bf16[2,128,1024]{2,1,0:T(8,128)(2,1)S(1)} %get-tuple-element.57), channel_id=1, source_target_pairs={{0,8},{1,9},{2,10},{3,11},{4,12},{5,13},{6,14},{7,15},{8,0},{9,1},... | collective-permute-start | bytes 1572872 | tf_op jit(solution)/shard_map/ppermute | solution.py:29
  238.4 16.8 %collective-permute-start.25 = (bf16[2,128,1024]{2,1,0:T(8,128)(2,1)S(1)}, bf16[2,128,1024]{2,1,0:T(8,128)(2,1)S(1)}, u32[]{:S(2)}, u32[]{:S(2)}) collective-permute-start(bf16[2,128,1024]{2,1,0:T(8,128)(2,1)S(1)} %get-tuple-element.62), channel_id=1, source_target_pairs={{0,16},{1,17},{2,18},{3,19},{4,20},{5,21},{6,22},{7,23},{8,24},{9,... | collective-permute-start | bytes 1572872 | tf_op jit(solution)/shard_map/ppermute | solution.py:29
  250.2 29.7 %collective-permute-start.27 = (bf16[2,160,1024]{2,1,0:T(8,128)(2,1)S(1)}, bf16[2,160,1024]{2,1,0:T(8,128)(2,1)S(1)}, u32[]{:S(2)}, u32[]{:S(2)}) collective-permute-start(bf16[2,160,1024]{2,1,0:T(8,128)(2,1)S(1)} %get-tuple-element.60), channel_id=1, source_target_pairs={{0,16},{1,17},{2,18},{3,19},{4,20},{5,21},{6,22},{7,23},{8,24},{9,... | collective-permute-start | bytes 1966088 | tf_op jit(solution)/shard_map/ppermute | solution.py:29
  252.8 25.4 %collective-permute-start.26 = (bf16[2,160,1024]{2,1,0:T(8,128)(2,1)S(1)}, bf16[2,160,1024]{2,1,0:T(8,128)(2,1)S(1)}, u32[]{:S(2)}, u32[]{:S(2)}) collective-permute-start(bf16[2,160,1024]{2,1,0:T(8,128)(2,1)S(1)} %get-tuple-element.67), channel_id=1, source_target_pairs={{0,8},{1,9},{2,10},{3,11},{4,12},{5,13},{6,14},{7,15},{8,0},{9,1},... | collective-permute-start | bytes 1966088 | tf_op jit(solution)/shard_map/ppermute | solution.py:29
  259.6 31.7 %collective-permute-start.31 = (bf16[4,128,1024]{2,1,0:T(8,128)(2,1)}, bf16[4,128,1024]{2,1,0:T(8,128)(2,1)}, u32[]{:S(2)}, u32[]{:S(2)}) collective-permute-start(bf16[4,128,1024]{2,1,0:T(8,128)(2,1)} %get-tuple-element.121), channel_id=1, source_target_pairs={{0,8},{1,9},{2,10},{3,11},{4,12},{5,13},{6,14},{7,15},{8,0},{9,1},... | collective-permute-start | bytes 3145736 | tf_op jit(solution)/shard_map/ppermute | solution.py:29
  261.6 29.7 %collective-permute-start.29 = (bf16[4,128,1024]{2,1,0:T(8,128)(2,1)}, bf16[4,128,1024]{2,1,0:T(8,128)(2,1)}, u32[]{:S(2)}, u32[]{:S(2)}) collective-permute-start(bf16[4,128,1024]{2,1,0:T(8,128)(2,1)} %get-tuple-element.119), channel_id=1, source_target_pairs={{0,16},{1,17},{2,18},{3,19},{4,20},{5,21},{6,22},{7,23},{8,24},{9,... | collective-permute-start | bytes 3145736 | tf_op jit(solution)/shard_map/ppermute | solution.py:29
  314.9 30.9 %collective-permute-start.52 = (bf16[4,160,1024]{2,1,0:T(8,128)(2,1)}, bf16[4,160,1024]{2,1,0:T(8,128)(2,1)S(1)}, u32[]{:S(2)}, u32[]{:S(2)}) collective-permute-start(bf16[4,160,1024]{2,1,0:T(8,128)(2,1)} %copy-done.48), channel_id=1, source_target_pairs={{0,8},{1,9},{2,10},{3,11},{4,12},{5,13},{6,14},{7,15},{8,0},{9,1},... | collective-permute-start | bytes 3932168 | tf_op jit(solution)/shard_map/ppermute | solution.py:29
  315.3 30.8 %collective-permute-start.51 = (bf16[4,160,1024]{2,1,0:T(8,128)(2,1)}, bf16[4,160,1024]{2,1,0:T(8,128)(2,1)S(1)}, u32[]{:S(2)}, u32[]{:S(2)}) collective-permute-start(bf16[4,160,1024]{2,1,0:T(8,128)(2,1)} %copy-done.50), channel_id=1, source_target_pairs={{0,16},{1,17},{2,18},{3,19},{4,20},{5,21},{6,22},{7,23},{8,24},{9,... | collective-permute-start | bytes 3932168 | tf_op jit(solution)/shard_map/ppermute | solution.py:29
  318.7 32.5 %collective-permute-start.58 = (bf16[128,1024]{1,0:T(8,128)(2,1)}, bf16[128,1024]{1,0:T(8,128)(2,1)}, u32[]{:S(2)}, u32[]{:S(2)}) collective-permute-start(bf16[128,1024]{1,0:T(8,128)(2,1)} %get-tuple-element.141), channel_id=1, source_target_pairs={{0,6},{1,7},{2,0},{3,1},{4,2},{5,3},{6,4},{7,5},{8,14},{9,15},{10,... | collective-permute-start | bytes 786440 | tf_op jit(solution)/shard_map/ppermute | solution.py:29
  326.5 26.1 %collective-permute-start.57 = (bf16[128,1024]{1,0:T(8,128)(2,1)}, bf16[128,1024]{1,0:T(8,128)(2,1)}, u32[]{:S(2)}, u32[]{:S(2)}) collective-permute-start(bf16[128,1024]{1,0:T(8,128)(2,1)} %get-tuple-element.140), channel_id=1, source_target_pairs={{0,4},{1,5},{2,6},{3,7},{4,0},{5,1},{6,2},{7,3},{8,12},{9,13},{10,... | collective-permute-start | bytes 786440 | tf_op jit(solution)/shard_map/ppermute | solution.py:29
  326.6 26.0 %collective-permute-start.56 = (bf16[128,1024]{1,0:T(8,128)(2,1)S(1)}, bf16[128,1024]{1,0:T(8,128)(2,1)}, u32[]{:S(2)}, u32[]{:S(2)}) collective-permute-start(bf16[128,1024]{1,0:T(8,128)(2,1)S(1)} %broadcast_add_fusion), channel_id=1, source_target_pairs={{0,2},{1,3},{2,4},{3,5},{4,6},{5,7},{6,0},{7,1},{8,10},{9,11},{10,... | collective-permute-start | bytes 786440 | tf_op jit(solution)/shard_map/ppermute | solution.py:29
  345.8 23.5 %collective-permute-start.39 = (bf16[2,128,1024]{2,1,0:T(8,128)(2,1)S(1)}, bf16[2,128,1024]{2,1,0:T(8,128)(2,1)S(1)}, u32[]{:S(2)}, u32[]{:S(2)}) collective-permute-start(bf16[2,128,1024]{2,1,0:T(8,128)(2,1)S(1)} %get-tuple-element.72), channel_id=1, source_target_pairs={{0,16},{1,17},{2,18},{3,19},{4,20},{5,21},{6,22},{7,23},{8,24},{9,... | collective-permute-start | bytes 1572872 | tf_op jit(solution)/shard_map/ppermute | solution.py:29
  357.4 28.2 %collective-permute-start.55 = (bf16[160,1024]{1,0:T(8,128)(2,1)}, bf16[160,1024]{1,0:T(8,128)(2,1)S(1)}, u32[]{:S(2)}, u32[]{:S(2)}) collective-permute-start(bf16[160,1024]{1,0:T(8,128)(2,1)} %get-tuple-element.138), channel_id=1, source_target_pairs={{0,6},{1,7},{2,0},{3,1},{4,2},{5,3},{6,4},{7,5},{8,14},{9,15},{10,... | collective-permute-start | bytes 983048 | tf_op jit(solution)/shard_map/ppermute | solution.py:29
  361.7 27.9 %collective-permute-start.54 = (bf16[160,1024]{1,0:T(8,128)(2,1)}, bf16[160,1024]{1,0:T(8,128)(2,1)}, u32[]{:S(2)}, u32[]{:S(2)}) collective-permute-start(bf16[160,1024]{1,0:T(8,128)(2,1)} %get-tuple-element.139), channel_id=1, source_target_pairs={{0,4},{1,5},{2,6},{3,7},{4,0},{5,1},{6,2},{7,3},{8,12},{9,13},{10,... | collective-permute-start | bytes 983048 | tf_op jit(solution)/shard_map/ppermute | solution.py:29
  361.7 27.9 %collective-permute-start.53 = (bf16[160,1024]{1,0:T(8,128)(2,1)}, bf16[160,1024]{1,0:T(8,128)(2,1)}, u32[]{:S(2)}, u32[]{:S(2)}) collective-permute-start(bf16[160,1024]{1,0:T(8,128)(2,1)} %get-tuple-element.137), channel_id=1, source_target_pairs={{0,2},{1,3},{2,4},{3,5},{4,6},{5,7},{6,0},{7,1},{8,10},{9,11},{10,... | collective-permute-start | bytes 983048 | tf_op jit(solution)/shard_map/ppermute | solution.py:29
  375.9 28.5 %collective-permute-start.44 = (bf16[4,128,1024]{2,1,0:T(8,128)(2,1)S(1)}, bf16[4,128,1024]{2,1,0:T(8,128)(2,1)}, u32[]{:S(2)}, u32[]{:S(2)}) collective-permute-start(bf16[4,128,1024]{2,1,0:T(8,128)(2,1)S(1)} %get-tuple-element.114), channel_id=1, source_target_pairs={{0,8},{1,9},{2,10},{3,11},{4,12},{5,13},{6,14},{7,15},{8,0},{9,1},... | collective-permute-start | bytes 3145736 | tf_op jit(solution)/shard_map/ppermute | solution.py:29
  377.4 27.1 %collective-permute-start.43 = (bf16[4,128,1024]{2,1,0:T(8,128)(2,1)}, bf16[4,128,1024]{2,1,0:T(8,128)(2,1)}, u32[]{:S(2)}, u32[]{:S(2)}) collective-permute-start(bf16[4,128,1024]{2,1,0:T(8,128)(2,1)} %get-tuple-element.112), channel_id=1, source_target_pairs={{0,16},{1,17},{2,18},{3,19},{4,20},{5,21},{6,22},{7,23},{8,24},{9,... | collective-permute-start | bytes 3145736 | tf_op jit(solution)/shard_map/ppermute | solution.py:29
  402.7 16.4 %collective-permute-start.42 = (f32[11,1024]{1,0:T(8,128)S(1)}, f32[11,1024]{1,0:T(8,128)S(1)}, u32[]{:S(2)}, u32[]{:S(2)}) collective-permute-start(f32[11,1024]{1,0:T(8,128)S(1)} %add.733), channel_id=1, source_target_pairs={{0,16},{1,17},{2,18},{3,19},{4,20},{5,21},{6,22},{7,23},{8,24},{9,... | collective-permute-start | bytes 135176 | tf_op jit(solution)/shard_map/ppermute | solution.py:29
  407.4 24.9 %collective-permute-start.50 = (bf16[128,1024]{1,0:T(8,128)(2,1)S(1)}, bf16[128,1024]{1,0:T(8,128)(2,1)S(1)}, u32[]{:S(2)}, u32[]{:S(2)}) collective-permute-start(bf16[128,1024]{1,0:T(8,128)(2,1)S(1)} %get-tuple-element.143), channel_id=1, source_target_pairs={{0,6},{1,7},{2,0},{3,1},{4,2},{5,3},{6,4},{7,5},{8,14},{9,15},{10,... | collective-permute-start | bytes 786440 | tf_op jit(solution)/shard_map/ppermute | solution.py:29
  410.7 24.5 %collective-permute-start.49 = (bf16[128,1024]{1,0:T(8,128)(2,1)S(1)}, bf16[128,1024]{1,0:T(8,128)(2,1)S(1)}, u32[]{:S(2)}, u32[]{:S(2)}) collective-permute-start(bf16[128,1024]{1,0:T(8,128)(2,1)S(1)} %get-tuple-element.142), channel_id=1, source_target_pairs={{0,4},{1,5},{2,6},{3,7},{4,0},{5,1},{6,2},{7,3},{8,12},{9,13},{10,... | collective-permute-start | bytes 786440 | tf_op jit(solution)/shard_map/ppermute | solution.py:29
  419.1 17.0 %collective-permute-start.48 = (f32[11,1024]{1,0:T(8,128)S(1)}, f32[11,1024]{1,0:T(8,128)S(1)}, u32[]{:S(2)}, u32[]{:S(2)}) collective-permute-start(f32[11,1024]{1,0:T(8,128)S(1)} %add_add_fusion.1), channel_id=1, source_target_pairs={{0,6},{1,7},{2,0},{3,1},{4,2},{5,3},{6,4},{7,5},{8,14},{9,15},{10,... | collective-permute-start | bytes 135176 | tf_op jit(solution)/shard_map/ppermute | solution.py:29
  (151 other events, 1488.4 us)
Sparse Core Ops, SparseCore 0:
  11.1 161.6 all-gather.2

commit v7 on v6

--- a/solution.py
+++ b/solution.py
@@ -1148,7 +1148,7 @@
     from_next = shifted(before_one_grad[:, :1, :], "seq", -1)
     if tuned:
         key_got = send_column(all_tied(key_outgoing, from_next))
-        from_next = tied(from_next, time_sides[0], time_sides[1][2:])
+        from_next = tied(from_next, time_sides[0])
     normed_one_grad = normed_one_grad + jnp.concatenate(
         [before_one_grad[:, 1:, :], from_next], axis=1
     )

time: 453 us -> 447 us (0.987)
  waiting for transfers between devices: 112 us -> 103 us
    ppermute x55, waiting for transfers between devices: 111 us -> 103 us  [sent(): return lax.ppermute(array, BOTH, pairs)]
    slice x17 -> x16, local copies, waits for them, and re-layouts: 9.41 us -> 8.95 us  [tied(): first = other[(0,) * other.ndim].astype(jnp.float32)]
  transfers between devices with their start and end apart: 60 -> 60, of which waited for: 16 -> 15; matrix products, arithmetic and copies ran while one was open for 26% -> 26% of each run, Pallas kernels for 13% -> 13%
where the time goes in v7:
time: 447 us; the launch traced here: 441 us
  waiting for transfers between devices  103 us (23%)
  Pallas kernels  90.8 us (20%)
  starting transfers between devices  84.7 us (19%)
  other arithmetic  77.5 us (17%)
  local copies, waits for them, and re-layouts  32 us (7%)
  between operations  28.3 us (6%)
  matrix products  23.8 us (5%)
    ppermute x55, waiting for transfers between devices, sent(): return lax.ppermute(array, BOTH, pairs)  103 us
    ppermute x55, starting transfers between devices, sent(): return lax.ppermute(array, BOTH, pairs)  79 us
    pallas_call x1, Pallas kernels, channel_mix(): pl.pallas_call(channel_kernel, out_shape=(half_rows, half_rows, half_rows...  31.7 us
    pallas_call x3, Pallas kernels, quarters_call(): pl.pallas_call(kernel, grid=(steps,), out_shape=tuple((jax.ShapeDtypeStru...  28.4 us
    pallas_call x5, Pallas kernels, assemble(): pl.pallas_call(partial(assemble_kernel, counts, start, columns), out_shap...  15 us
    pallas_call x1, Pallas kernels, time_mix_back(): pl.pallas_call(time_mix_kernel, grid=(1024 // tile,), out_shape=(jax.Shap...  13.7 us
    another operation x5, other arithmetic  11 us
    unnamed x254, local copies, waits for them, and re-layouts  9.04 us
  transfers between devices with their start and end apart: 60, of which 15 were waited for; matrix products, arithmetic and copies ran while one was open for 26% of the time, Pallas kernels for 13%

profile of v7, /device:TPU:0, one launch (start us, length us, event | category | flops | bytes accessed | tf_op | source)
XLA Modules:
  0.0 440.5 jit_solution(739055739258398499)
XLA Ops:
  11.2 5.1 %collective-permute-start.2 = (bf16[144,1024]{1,0:T(8,128)(2,1)S(1)}, bf16[144,1024]{1,0:T(8,128)(2,1)S(1)}, u32[]{:S(2)}, u32[]{:S(2)}) collective-permute-start(bf16[144,1024]{1,0:T(8,128)(2,1)S(1)} %select_dynamic-update-slice_fusion), channel_id=1, source_target_pairs={{0,6},{1,7},{2,0},{3,1},{4,2},{5,3},{6,4},{7,5},{8,14},{9,15},{10,... | collective-permute-start | bytes 884744 | tf_op jit(solution)/shard_map/ppermute | solution.py:29
  24.6 29.4 %collective-permute-done.1 = bf16[144,1024]{1,0:T(8,128)(2,1)S(1)} collective-permute-done((bf16[144,1024]{1,0:T(8,128)(2,1)S(1)}, bf16[144,1024]{1,0:T(8,128)(2,1)S(1)}, u32[]{:S(2)}, u32[]{:S(2)}) %collective-permute-start.1) | collective-permute-done | bytes 294944 | tf_op jit(solution)/shard_map/ppermute | solution.py:29
  62.0 34.9 %collective-permute-done.3.refs_1_ = bf16[4,144,1024]{2,1,0:T(8,128)(2,1)S(1)} collective-permute-done((bf16[4,144,1024]{2,1,0:T(8,128)(2,1)S(1)}, bf16[4,144,1024]{2,1,0:T(8,128)(2,1)S(1)}, u32[]{:S(2)}, u32[]{:S(2)}) %collective-permute-start.3) | collective-permute-done | bytes 1179680 | tf_op jit(solution)/shard_map/ppermute | solution.py:29
  108.3 2.9 collective-permute-done.6.refs_4_
  111.5 2.7 collective-permute-done.11.refs_9_
  116.6 3.1 shard_map.358
  119.7 3.1 shard_map.359
  139.0 3.0 fusion.9
  142.2 10.3 %collective-permute-start.15 = (f32[2,2,1024]{2,1,0:T(2,128)S(1)}, f32[2,2,1024]{2,1,0:T(2,128)S(1)}, u32[]{:S(2)}, u32[]{:S(2)}) collective-permute-start(f32[2,2,1024]{2,1,0:T(2,128)S(1)} %select_add_fusion.1), channel_id=1, source_target_pairs={{0,4},{1,5},{2,6},{3,7},{4,0},{5,1},{6,2},{7,3},{8,12},{9,13},{10,... | collective-permute-start | bytes 49160 | tf_op jit(solution)/shard_map/ppermute | solution.py:29
  155.2 3.3 shard_map.357
  158.5 3.1 shard_map.360
  161.8 3.5 fusion.42
  173.6 31.7 %shard_map.362 = (bf16[512,1024]{1,0:T(8,128)(2,1)}, bf16[512,1024]{1,0:T(8,128)(2,1)}, bf16[512,1024]{1,0:T(8,128)(2,1)}, f32[512,1024]{1,0:T(8,128)}, f32[512,...) custom-call(s32[32]{0:T(128)} %and_add_fusion.slots_ref, ...), custom_call_target="tpu_custom_call" | custom-call | flops 19327352832 | bytes 41943040 | tf_op jit(solution)/shard_map/pallas_call | solution.py:286
  222.7 3.2 multiply_reduce_fusion.2
  227.2 8.6 %shard_map.363 = (bf16[4,128,1024]{2,1,0:T(8,128)(2,1)S(1)}, bf16[4,128,1024]{2,1,0:T(8,128)(2,1)}, bf16[4,128,1024]{2,1,0:T(8,128)(2,1)}, bf16[2,128,1024]{2,1,0:T(8,128)(2,1)S(1)}, bf16[2,128,1024]{2,1,0:T(8,128)(2,1)S(1)}) custom-call(bf16[4,512,512]{2,1,0:T(8,128)(2,1)} %get-tuple-element.53.own_ref, ...), custom_call_target="tpu_custom_call" | custom-call | flops 1 | bytes 1 | tf_op jit(solution)/shard_map/pallas_call | solution.py:528
  239.2 10.3 %shard_map.364 = (bf16[4,160,1024]{2,1,0:T(8,128)(2,1)}, bf16[4,160,1024]{2,1,0:T(8,128)(2,1)}, bf16[4,160,1024]{2,1,0:T(8,128)(2,1)}, bf16[2,160,1024]{2,1,0:T(8,128)(2,1)S(1)}, bf16[2,160,1024]{2,1,0:T(8,128)(2,1)S(1)}) custom-call(bf16[512,512]{1,0:T(8,128)(2,1)S(1)} %get-tuple-element.156.key_ref, bf16[512,512]{1,0:T(8,128)(2,1)S(1)} %get-tuple-element.152.other_key_ref, ...), custom_call_target="tpu_custom_call" | custom-call | flops 1 | bytes 1 | tf_op jit(solution)/shard_map/pallas_call | solution.py:528
  262.3 13.7 %shard_map.365 = (bf16[512,1024]{1,0:T(8,128)(2,1)S(1)}, f32[512,1024]{1,0:T(8,128)S(1)}, f32[512,1024]{1,0:T(8,128)}, f32[2,1,1024]{2,1,0:T(1,128)S(1)}, f32[2,...) custom-call(bf16[512,1024]{1,0:T(8,128)(2,1)S(1)} %bitcast.257, ...), custom_call_target="tpu_custom_call" | custom-call | flops 1 | bytes 1 | tf_op jit(solution)/shard_map/pallas_call | solution.py:492
  285.1 6.0 %collective-permute-done.31 = bf16[4,128,1024]{2,1,0:T(8,128)(2,1)} collective-permute-done((bf16[4,128,1024]{2,1,0:T(8,128)(2,1)}, bf16[4,128,1024]{2,1,0:T(8,128)(2,1)}, u32[]{:S(2)}, u32[]{:S(2)}) %collective-permute-start.31) | collective-permute-done | bytes 1048608 | tf_op jit(solution)/shard_map/ppermute | solution.py:29
  291.3 3.7 fusion.116
  304.9 3.1 multiply_reduce_fusion.3
  310.4 3.3 pad_maximum_fusion.5.own_ref
  318.5 3.6 collective-permute-start.58
  326.9 9.5 %shard_map.366 = (bf16[4,128,1024]{2,1,0:T(8,128)(2,1)S(1)}, bf16[4,128,1024]{2,1,0:T(8,128)(2,1)}, bf16[4,128,1024]{2,1,0:T(8,128)(2,1)S(1)}, bf16[2,128,1024]{...) custom-call(bf16[512,2048]{1,0:T(8,128)(2,1)} %pad_maximum_fusion.5.own_ref, ...), custom_call_target="tpu_custom_call" | custom-call | flops 1 | bytes 1 | tf_op jit(solution)/shard_map/pallas_call | solution.py:528
  351.4 4.1 fusion.114
  358.1 2.9 collective-permute-start.55
  363.8 4.5 %fusion.23 = (f32[1024]{0:T(1024)S(1)}, f32[2,256]{1,0:T(2,128)S(1)}, f32[2,256]{1,0:T(2,128)S(1)}, f32[1024]{0:T(1024)}, f32[1024]{0:T(1024)}, /*index=5*/f32[1024]{0:T(1024)}, f32[1024]{0:T(1024)}, f32[2,256,1024]{2,1,0:T(8,128)}) fusion(bf16[2,256,1024]{2,1,0:T(8,128)(2,1)S(1)} %copy-done.21, f32[2,256]{1,0:T(2,128)S(1)} %copy-done.87, ...), kind=kLoop, calls=%fused_computation.35 | loop fusion | flops 14673920 | bytes 13682688 | tf_op jit(solution)/shard_map/reduce_sum | solution.py:706
  375.9 4.9 %fusion.22 = f32[2,256,1024]{2,1,0:T(8,128)} fusion(bf16[2,256,1024]{2,1,0:T(8,128)(2,1)S(1)} %copy-done.21, f32[2,256,1024]{2,1,0:T(8,128)} %get-tuple-element.114, f32[2,256]{1,0:T(2,128)S(1)} %broadcast_multiply_fusion.9, f32[2,256]{1,0:T(2,128)} %broadcast_multiply_fusion.10, f32[1024]{0:T(1024)S(1)} %bitcast.304, f32[2,256]{1,0:T(2,128)} %copy-done.86, ...), kind=kLoop, calls=%fused_computation.34 | loop fusion | flops 9437184 | bytes 10510336 | tf_op jit(solution)/shard_map/add | solution.py:1158
  380.9 10.3 %collective-permute-done.54 = bf16[160,1024]{1,0:T(8,128)(2,1)} collective-permute-done((bf16[160,1024]{1,0:T(8,128)(2,1)}, bf16[160,1024]{1,0:T(8,128)(2,1)}, u32[]{:S(2)}, u32[]{:S(2)}) %collective-permute-start.54) | collective-permute-done | bytes 327712 | tf_op jit(solution)/shard_map/ppermute | solution.py:29
  393.8 3.4 collective-permute-done.40
  402.1 2.5 collective-permute-start.50
  405.7 6.2 %collective-permute-done.45 = bf16[128,1024]{1,0:T(8,128)(2,1)S(1)} collective-permute-done((bf16[128,1024]{1,0:T(8,128)(2,1)S(1)}, bf16[128,1024]{1,0:T(8,128)(2,1)S(1)}, u32[]{:S(2)}, u32[]{:S(2)}) %collective-permute-start.45) | collective-permute-done | bytes 262176 | tf_op jit(solution)/shard_map/ppermute | solution.py:29
  415.6 11.1 %collective-permute-start.47 = (f32[11,1024]{1,0:T(8,128)S(1)}, f32[11,1024]{1,0:T(8,128)S(1)}, u32[]{:S(2)}, u32[]{:S(2)}) collective-permute-start(f32[11,1024]{1,0:T(8,128)S(1)} %add_add_fusion.1), channel_id=1, source_target_pairs={{0,4},{1,5},{2,6},{3,7},{4,0},{5,1},{6,2},{7,3},{8,12},{9,13},{10,... | collective-permute-start | bytes 135176 | tf_op jit(solution)/shard_map/ppermute | solution.py:29
  (518 shorter events, 161.1 us)
Async XLA Ops:
  7.3 166.3 %all-gather.3.cloned.1.call-start = ((), (), s32[]{:S(2)}) async-start(), calls=%async_computation | async-start | bytes 19464192 | tf_op jit(solution)/shard_map/all_gather | solution.py:822
  16.3 37.7 %collective-permute-start.1 = (bf16[144,1024]{1,0:T(8,128)(2,1)S(1)}, bf16[144,1024]{1,0:T(8,128)(2,1)S(1)}, u32[]{:S(2)}, u32[]{:S(2)}) collective-permute-start(bf16[144,1024]{1,0:T(8,128)(2,1)S(1)} %select_dynamic-update-slice_fusion), channel_id=1, source_target_pairs={{0,4},{1,5},{2,6},{3,7},{4,0},{5,1},{6,2},{7,3},{8,12},{9,13},{10,... | collective-permute-start | bytes 884744 | tf_op jit(solution)/shard_map/ppermute | solution.py:29
  16.3 37.7 %collective-permute-start = (bf16[144,1024]{1,0:T(8,128)(2,1)S(1)}, bf16[144,1024]{1,0:T(8,128)(2,1)S(1)}, u32[]{:S(2)}, u32[]{:S(2)}) collective-permute-start(bf16[144,1024]{1,0:T(8,128)(2,1)S(1)} %select_dynamic-update-slice_fusion), channel_id=1, source_target_pairs={{0,2},{1,3},{2,4},{3,5},{4,6},{5,7},{6,0},{7,1},{8,10},{9,11},{10,... | collective-permute-start | bytes 884744 | tf_op jit(solution)/shard_map/ppermute | solution.py:29
  17.9 85.3 %collective-permute-start.12 = (bf16[2,1,1024]{2,1,0:T(2,128)(2,1)}, bf16[2,1,1024]{2,1,0:T(2,128)(2,1)S(1)}, u32[]{:S(2)}, u32[]{:S(2)}) collective-permute-start(bf16[2,1,1024]{2,1,0:T(2,128)(2,1)} %slice.324), channel_id=1, source_target_pairs={{0,1},{1,2},{2,3},{3,4},{4,5},{5,6},{6,7},{8,9},{9,10},{10,11},{11... | collective-permute-start | bytes 12296 | tf_op jit(solution)/shard_map/ppermute | solution.py:650
  54.1 42.8 %collective-permute-start.3 = (bf16[4,144,1024]{2,1,0:T(8,128)(2,1)S(1)}, bf16[4,144,1024]{2,1,0:T(8,128)(2,1)S(1)}, u32[]{:S(2)}, u32[]{:S(2)}) collective-permute-start(bf16[4,144,1024]{2,1,0:T(8,128)(2,1)S(1)} %pad_maximum_fusion.6.refs_0_), channel_id=1, source_target_pairs={{0,8},{1,9},{2,10},{3,11},{4,12},{5,13},{6,14},{7,15},{8,0},{9,1},... | collective-permute-start | bytes 3538952 | tf_op jit(solution)/shard_map/ppermute | solution.py:29
  55.7 44.4 %collective-permute-start.4 = (bf16[4,144,1024]{2,1,0:T(8,128)(2,1)S(1)}, bf16[4,144,1024]{2,1,0:T(8,128)(2,1)S(1)}, u32[]{:S(2)}, u32[]{:S(2)}) collective-permute-start(bf16[4,144,1024]{2,1,0:T(8,128)(2,1)S(1)} %pad_maximum_fusion.6.refs_0_), channel_id=1, source_target_pairs={{0,16},{1,17},{2,18},{3,19},{4,20},{5,21},{6,22},{7,23},{8,24},{9,... | collective-permute-start | bytes 3538952 | tf_op jit(solution)/shard_map/ppermute | solution.py:29
  142.2 19.5 %collective-permute-start.16 = (f32[2,2,1024]{2,1,0:T(2,128)S(1)}, f32[2,2,1024]{2,1,0:T(2,128)S(1)}, u32[]{:S(2)}, u32[]{:S(2)}) collective-permute-start(f32[2,2,1024]{2,1,0:T(2,128)S(1)} %select_add_fusion.1), channel_id=1, source_target_pairs={{0,6},{1,7},{2,0},{3,1},{4,2},{5,3},{6,4},{7,5},{8,14},{9,15},{10,... | collective-permute-start | bytes 49160 | tf_op jit(solution)/shard_map/ppermute | solution.py:29
  142.2 19.4 %collective-permute-start.15 = (f32[2,2,1024]{2,1,0:T(2,128)S(1)}, f32[2,2,1024]{2,1,0:T(2,128)S(1)}, u32[]{:S(2)}, u32[]{:S(2)}) collective-permute-start(f32[2,2,1024]{2,1,0:T(2,128)S(1)} %select_add_fusion.1), channel_id=1, source_target_pairs={{0,4},{1,5},{2,6},{3,7},{4,0},{5,1},{6,2},{7,3},{8,12},{9,13},{10,... | collective-permute-start | bytes 49160 | tf_op jit(solution)/shard_map/ppermute | solution.py:29
  205.3 33.9 %collective-permute-start.23 = (bf16[512,4096]{1,0:T(8,128)(2,1)}, bf16[512,4096]{1,0:T(8,128)(2,1)}, u32[]{:S(2)}, u32[]{:S(2)}) collective-permute-start(bf16[512,4096]{1,0:T(8,128)(2,1)} %get-tuple-element.58.refs_0_), channel_id=1, source_target_pairs={{0,1},{1,0},{2,3},{3,2},{4,5},{5,4},{6,7},{7,6},{8,9},{9,8},{10,11... | collective-permute-start | bytes 12582920 | tf_op jit(solution)/shard_map/ppermute | solution.py:29
  213.4 68.7 %collective-permute-start.30 = (bf16[512,2048]{1,0:T(8,128)(2,1)}, bf16[512,2048]{1,0:T(8,128)(2,1)}, u32[]{:S(2)}, u32[]{:S(2)}) collective-permute-start(bf16[512,2048]{1,0:T(8,128)(2,1)} %pad_maximum_fusion.4), channel_id=1, source_target_pairs={{0,1},{1,0},{2,3},{3,2},{4,5},{5,4},{6,7},{7,6},{8,9},{9,8},{10,11... | collective-permute-start | bytes 6291464 | tf_op jit(solution)/shard_map/ppermute | solution.py:29
  221.1 18.1 %collective-permute-start.24 = (bf16[512,1024]{1,0:T(8,128)(2,1)}, bf16[512,1024]{1,0:T(8,128)(2,1)}, u32[]{:S(2)}, u32[]{:S(2)}) collective-permute-start(bf16[512,1024]{1,0:T(8,128)(2,1)} %get-tuple-element.59.refs_2_), channel_id=1, source_target_pairs={{0,1},{1,0},{2,3},{3,2},{4,5},{5,4},{6,7},{7,6},{8,9},{9,8},{10,11... | collective-permute-start | bytes 3145736 | tf_op jit(solution)/shard_map/ppermute | solution.py:29
  235.8 17.1 %collective-permute-start.21 = (bf16[2,128,1024]{2,1,0:T(8,128)(2,1)S(1)}, bf16[2,128,1024]{2,1,0:T(8,128)(2,1)S(1)}, u32[]{:S(2)}, u32[]{:S(2)}) collective-permute-start(bf16[2,128,1024]{2,1,0:T(8,128)(2,1)S(1)} %get-tuple-element.57), channel_id=1, source_target_pairs={{0,8},{1,9},{2,10},{3,11},{4,12},{5,13},{6,14},{7,15},{8,0},{9,1},... | collective-permute-start | bytes 1572872 | tf_op jit(solution)/shard_map/ppermute | solution.py:29
  238.3 16.7 %collective-permute-start.25 = (bf16[2,128,1024]{2,1,0:T(8,128)(2,1)S(1)}, bf16[2,128,1024]{2,1,0:T(8,128)(2,1)S(1)}, u32[]{:S(2)}, u32[]{:S(2)}) collective-permute-start(bf16[2,128,1024]{2,1,0:T(8,128)(2,1)S(1)} %get-tuple-element.62), channel_id=1, source_target_pairs={{0,16},{1,17},{2,18},{3,19},{4,20},{5,21},{6,22},{7,23},{8,24},{9,... | collective-permute-start | bytes 1572872 | tf_op jit(solution)/shard_map/ppermute | solution.py:29
  250.0 29.7 %collective-permute-start.27 = (bf16[2,160,1024]{2,1,0:T(8,128)(2,1)S(1)}, bf16[2,160,1024]{2,1,0:T(8,128)(2,1)S(1)}, u32[]{:S(2)}, u32[]{:S(2)}) collective-permute-start(bf16[2,160,1024]{2,1,0:T(8,128)(2,1)S(1)} %get-tuple-element.60), channel_id=1, source_target_pairs={{0,16},{1,17},{2,18},{3,19},{4,20},{5,21},{6,22},{7,23},{8,24},{9,... | collective-permute-start | bytes 1966088 | tf_op jit(solution)/shard_map/ppermute | solution.py:29
  252.7 25.4 %collective-permute-start.26 = (bf16[2,160,1024]{2,1,0:T(8,128)(2,1)S(1)}, bf16[2,160,1024]{2,1,0:T(8,128)(2,1)S(1)}, u32[]{:S(2)}, u32[]{:S(2)}) collective-permute-start(bf16[2,160,1024]{2,1,0:T(8,128)(2,1)S(1)} %get-tuple-element.67), channel_id=1, source_target_pairs={{0,8},{1,9},{2,10},{3,11},{4,12},{5,13},{6,14},{7,15},{8,0},{9,1},... | collective-permute-start | bytes 1966088 | tf_op jit(solution)/shard_map/ppermute | solution.py:29
  259.5 31.7 %collective-permute-start.31 = (bf16[4,128,1024]{2,1,0:T(8,128)(2,1)}, bf16[4,128,1024]{2,1,0:T(8,128)(2,1)}, u32[]{:S(2)}, u32[]{:S(2)}) collective-permute-start(bf16[4,128,1024]{2,1,0:T(8,128)(2,1)} %get-tuple-element.119), channel_id=1, source_target_pairs={{0,8},{1,9},{2,10},{3,11},{4,12},{5,13},{6,14},{7,15},{8,0},{9,1},... | collective-permute-start | bytes 3145736 | tf_op jit(solution)/shard_map/ppermute | solution.py:29
  261.5 29.7 %collective-permute-start.29 = (bf16[4,128,1024]{2,1,0:T(8,128)(2,1)}, bf16[4,128,1024]{2,1,0:T(8,128)(2,1)}, u32[]{:S(2)}, u32[]{:S(2)}) collective-permute-start(bf16[4,128,1024]{2,1,0:T(8,128)(2,1)} %get-tuple-element.117), channel_id=1, source_target_pairs={{0,16},{1,17},{2,18},{3,19},{4,20},{5,21},{6,22},{7,23},{8,24},{9,... | collective-permute-start | bytes 3145736 | tf_op jit(solution)/shard_map/ppermute | solution.py:29
  310.3 16.0 %collective-permute-start.35 = (bf16[512,3072]{1,0:T(8,128)(2,1)}, bf16[512,3072]{1,0:T(8,128)(2,1)}, u32[]{:S(2)}, u32[]{:S(2)}) collective-permute-start(bf16[512,3072]{1,0:T(8,128)(2,1)} %pad_maximum_fusion.grad_ref), channel_id=1, source_target_pairs={{0,1},{1,0},{2,3},{3,2},{4,5},{5,4},{6,7},{7,6},{8,9},{9,8},{10,11... | collective-permute-start | bytes 9437192 | tf_op jit(solution)/shard_map/ppermute | solution.py:29
  314.8 35.6 %collective-permute-start.52 = (bf16[4,160,1024]{2,1,0:T(8,128)(2,1)}, bf16[4,160,1024]{2,1,0:T(8,128)(2,1)S(1)}, u32[]{:S(2)}, u32[]{:S(2)}) collective-permute-start(bf16[4,160,1024]{2,1,0:T(8,128)(2,1)} %copy-done.48), channel_id=1, source_target_pairs={{0,8},{1,9},{2,10},{3,11},{4,12},{5,13},{6,14},{7,15},{8,0},{9,1},... | collective-permute-start | bytes 3932168 | tf_op jit(solution)/shard_map/ppermute | solution.py:29
  315.1 35.2 %collective-permute-start.51 = (bf16[4,160,1024]{2,1,0:T(8,128)(2,1)}, bf16[4,160,1024]{2,1,0:T(8,128)(2,1)}, u32[]{:S(2)}, u32[]{:S(2)}) collective-permute-start(bf16[4,160,1024]{2,1,0:T(8,128)(2,1)} %copy-done.50), channel_id=1, source_target_pairs={{0,16},{1,17},{2,18},{3,19},{4,20},{5,21},{6,22},{7,23},{8,24},{9,... | collective-permute-start | bytes 3932168 | tf_op jit(solution)/shard_map/ppermute | solution.py:29
  318.5 24.0 %collective-permute-start.58 = (bf16[128,1024]{1,0:T(8,128)(2,1)}, bf16[128,1024]{1,0:T(8,128)(2,1)}, u32[]{:S(2)}, u32[]{:S(2)}) collective-permute-start(bf16[128,1024]{1,0:T(8,128)(2,1)} %get-tuple-element.139), channel_id=1, source_target_pairs={{0,6},{1,7},{2,0},{3,1},{4,2},{5,3},{6,4},{7,5},{8,14},{9,15},{10,... | collective-permute-start | bytes 786440 | tf_op jit(solution)/shard_map/ppermute | solution.py:29
  326.3 18.8 %collective-permute-start.57 = (bf16[128,1024]{1,0:T(8,128)(2,1)}, bf16[128,1024]{1,0:T(8,128)(2,1)}, u32[]{:S(2)}, u32[]{:S(2)}) collective-permute-start(bf16[128,1024]{1,0:T(8,128)(2,1)} %get-tuple-element.138), channel_id=1, source_target_pairs={{0,4},{1,5},{2,6},{3,7},{4,0},{5,1},{6,2},{7,3},{8,12},{9,13},{10,... | collective-permute-start | bytes 786440 | tf_op jit(solution)/shard_map/ppermute | solution.py:29
  326.4 20.0 %collective-permute-start.56 = (bf16[128,1024]{1,0:T(8,128)(2,1)S(1)}, bf16[128,1024]{1,0:T(8,128)(2,1)}, u32[]{:S(2)}, u32[]{:S(2)}) collective-permute-start(bf16[128,1024]{1,0:T(8,128)(2,1)S(1)} %broadcast_add_fusion), channel_id=1, source_target_pairs={{0,2},{1,3},{2,4},{3,5},{4,6},{5,7},{6,0},{7,1},{8,10},{9,11},{10,... | collective-permute-start | bytes 786440 | tf_op jit(solution)/shard_map/ppermute | solution.py:29
  342.5 26.4 %collective-permute-start.43 = (bf16[2,128,1024]{2,1,0:T(8,128)(2,1)S(1)}, bf16[2,128,1024]{2,1,0:T(8,128)(2,1)S(1)}, u32[]{:S(2)}, u32[]{:S(2)}) collective-permute-start(bf16[2,128,1024]{2,1,0:T(8,128)(2,1)S(1)} %get-tuple-element.72), channel_id=1, source_target_pairs={{0,16},{1,17},{2,18},{3,19},{4,20},{5,21},{6,22},{7,23},{8,24},{9,... | collective-permute-start | bytes 1572872 | tf_op jit(solution)/shard_map/ppermute | solution.py:29
  358.1 22.7 %collective-permute-start.55 = (bf16[160,1024]{1,0:T(8,128)(2,1)}, bf16[160,1024]{1,0:T(8,128)(2,1)S(1)}, u32[]{:S(2)}, u32[]{:S(2)}) collective-permute-start(bf16[160,1024]{1,0:T(8,128)(2,1)} %get-tuple-element.136), channel_id=1, source_target_pairs={{0,6},{1,7},{2,0},{3,1},{4,2},{5,3},{6,4},{7,5},{8,14},{9,15},{10,... | collective-permute-start | bytes 983048 | tf_op jit(solution)/shard_map/ppermute | solution.py:29
  360.9 30.2 %collective-permute-start.54 = (bf16[160,1024]{1,0:T(8,128)(2,1)}, bf16[160,1024]{1,0:T(8,128)(2,1)}, u32[]{:S(2)}, u32[]{:S(2)}) collective-permute-start(bf16[160,1024]{1,0:T(8,128)(2,1)} %get-tuple-element.137), channel_id=1, source_target_pairs={{0,4},{1,5},{2,6},{3,7},{4,0},{5,1},{6,2},{7,3},{8,12},{9,13},{10,... | collective-permute-start | bytes 983048 | tf_op jit(solution)/shard_map/ppermute | solution.py:29
  362.0 29.2 %collective-permute-start.53 = (bf16[160,1024]{1,0:T(8,128)(2,1)}, bf16[160,1024]{1,0:T(8,128)(2,1)}, u32[]{:S(2)}, u32[]{:S(2)}) collective-permute-start(bf16[160,1024]{1,0:T(8,128)(2,1)} %get-tuple-element.135), channel_id=1, source_target_pairs={{0,2},{1,3},{2,4},{3,5},{4,6},{5,7},{6,0},{7,1},{8,10},{9,11},{10,... | collective-permute-start | bytes 983048 | tf_op jit(solution)/shard_map/ppermute | solution.py:29
  370.9 27.5 %collective-permute-start.44 = (bf16[4,128,1024]{2,1,0:T(8,128)(2,1)}, bf16[4,128,1024]{2,1,0:T(8,128)(2,1)}, u32[]{:S(2)}, u32[]{:S(2)}) collective-permute-start(bf16[4,128,1024]{2,1,0:T(8,128)(2,1)} %fusion.51), channel_id=1, source_target_pairs={{0,8},{1,9},{2,10},{3,11},{4,12},{5,13},{6,14},{7,15},{8,0},{9,1},... | collective-permute-start | bytes 3145736 | tf_op jit(solution)/shard_map/ppermute | solution.py:29
  371.4 27.0 %collective-permute-start.42 = (bf16[4,128,1024]{2,1,0:T(8,128)(2,1)S(1)}, bf16[4,128,1024]{2,1,0:T(8,128)(2,1)}, u32[]{:S(2)}, u32[]{:S(2)}) collective-permute-start(bf16[4,128,1024]{2,1,0:T(8,128)(2,1)S(1)} %get-tuple-element.112), channel_id=1, source_target_pairs={{0,16},{1,17},{2,18},{3,19},{4,20},{5,21},{6,22},{7,23},{8,24},{9,... | collective-permute-start | bytes 3145736 | tf_op jit(solution)/shard_map/ppermute | solution.py:29
  402.1 26.5 %collective-permute-start.50 = (bf16[128,1024]{1,0:T(8,128)(2,1)S(1)}, bf16[128,1024]{1,0:T(8,128)(2,1)S(1)}, u32[]{:S(2)}, u32[]{:S(2)}) collective-permute-start(bf16[128,1024]{1,0:T(8,128)(2,1)S(1)} %get-tuple-element.141), channel_id=1, source_target_pairs={{0,6},{1,7},{2,0},{3,1},{4,2},{5,3},{6,4},{7,5},{8,14},{9,15},{10,... | collective-permute-start | bytes 786440 | tf_op jit(solution)/shard_map/ppermute | solution.py:29
  404.7 24.0 %collective-permute-start.49 = (bf16[128,1024]{1,0:T(8,128)(2,1)S(1)}, bf16[128,1024]{1,0:T(8,128)(2,1)S(1)}, u32[]{:S(2)}, u32[]{:S(2)}) collective-permute-start(bf16[128,1024]{1,0:T(8,128)(2,1)S(1)} %get-tuple-element.140), channel_id=1, source_target_pairs={{0,4},{1,5},{2,6},{3,7},{4,0},{5,1},{6,2},{7,3},{8,12},{9,13},{10,... | collective-permute-start | bytes 786440 | tf_op jit(solution)/shard_map/ppermute | solution.py:29
  413.1 16.5 %collective-permute-start.48 = (f32[11,1024]{1,0:T(8,128)S(1)}, f32[11,1024]{1,0:T(8,128)S(1)}, u32[]{:S(2)}, u32[]{:S(2)}) collective-permute-start(f32[11,1024]{1,0:T(8,128)S(1)} %add_add_fusion.1), channel_id=1, source_target_pairs={{0,6},{1,7},{2,0},{3,1},{4,2},{5,3},{6,4},{7,5},{8,14},{9,15},{10,... | collective-permute-start | bytes 135176 | tf_op jit(solution)/shard_map/ppermute | solution.py:29
  (151 other events, 1521.9 us)
Sparse Core Ops, SparseCore 0:
  11.1 161.6 all-gather.2
